TPU v7x, 32 devices: a whole 2x2x4 slice. The times are simulated.
32 devices in a mesh: group: 2 (over y), ctx: 4 (over z), section: 2 (over x), rep: 2 (over core).
Axes of the slice: x: 2, y: 2, z: 4, core: 2. Of those that a mesh axis runs over, the one named last changes fastest.
Arguments:
- stream: bfloat16 [1024, 4096], P(('group', 'ctx'), ('section', 'rep')), parts along dimension 0, may hold values from -12 to 12
- query_proj: bfloat16 [1024, 4096], P(('group', 'ctx'), ('section', 'rep')), parts along dimension 0, may hold values from -105 to 105
- key_proj: bfloat16 [1024, 256], P(('group', 'ctx')), parts along dimension 0, may hold values from -4 to 4
- value_projected: bfloat16 [1024, 256], P(('group', 'ctx')), parts along dimension 0, may hold values from -6 to 6
- expert_ids: int32 [1024, 2], P(('group', 'ctx')), parts along dimension 0, may hold values from 0 to 3, all different within a row; in each aligned block of 128 rows (0 to 127, 128 to 255, ...) at most 80 rows name the same one
- expert_home: int32 [4], replicated, may hold values from 0 to 3, each once
- router: bfloat16 [4096, 4], P(('section', 'rep')), may hold values from -0.09375 to 0.09375
- norm_gain: bfloat16 [4096], P(('section', 'rep')), may hold values from 0.25 to 1.75
- w_gate: bfloat16 [4, 4096, 768], P('ctx', ('section', 'rep')), may hold values from -0.09375 to 0.09375
- w_up: bfloat16 [4, 4096, 768], P('ctx', ('section', 'rep')), may hold values from -0.09375 to 0.09375
- w_down: bfloat16 [4, 768, 4096], P('ctx', None, ('section', 'rep')), may hold values from -0.21875 to 0.21875
Outputs:
- result: bfloat16 [1024, 4096], P(('group', 'ctx'), ('section', 'rep')), parts along dimension 0
There are 2 independent parts, one for each index of `group`. A program takes and returns all parts, laid end to end along the dimension named above; an argument that names none is the same for every part. Nothing has to cross between parts.
Inputs may be any that keep to these rules, and one draw needn't show every extreme that they name: `expert_ids`: in each token's row the 2 experts differ; within the 128 tokens of one index of ctx no expert is chosen more than 80 times. `expert_home`: each index of ctx holds exactly one expert.
All inputs are finite; a program needn't handle non-finite values.
Results may differ from a plain program's by a relative error of at most 0.0085.
Values may be sent and summed in bfloat16 or wider, within the bound.
No kernel may reach another device: no remote copies, remote signals or barrier semaphores. Data moves between devices by JAX's collectives and lax.ppermute only.
A program may use at most 64 MiB of HBM per device.

v0:
```python
import math

import jax
import jax.numpy as jnp
from jax import lax
from jax.sharding import PartitionSpec as P

D = 4096
HEAD_SIZE = 128
QUERY_HEADS = 32
KEY_VALUE_HEADS = 2


epsilon = 1e-06
very_negative = -1e30


def score_update(running, query_matrix, query_pos, key_block, value_block, key_anchor):
    run_max, run_sum, run_acc = running
    key_len = key_block.shape[0]
    scores = jnp.einsum(
        "tha,pa->htp", query_matrix, key_block, preferred_element_type=jnp.float32
    ) * (1.0 / math.sqrt(HEAD_SIZE))
    key_pos = key_anchor + jnp.arange(key_len, dtype=jnp.int32)
    visible = query_pos[:, None] >= key_pos[None, :]
    scores = jnp.where(visible, scores, very_negative)
    new_max = jnp.maximum(run_max, jnp.max(scores, axis=-1))
    expo = jnp.where(visible, jnp.exp(scores - new_max[..., None]), 0.0)
    factor = jnp.exp(run_max - new_max)
    new_sum = run_sum * factor + jnp.sum(expo, axis=-1)
    weights = expo.astype(jnp.bfloat16)
    new_acc = run_acc * factor[..., None] + jnp.einsum(
        "htp,pa->hta", weights, value_block, preferred_element_type=jnp.float32
    )
    return (new_max, new_sum, new_acc)


def absorb_rows(running, query_matrix, query_pos, key_rows, value_rows, anchor):
    piece_len = key_rows.shape[0]
    if piece_len > 512 and piece_len % 512 == 0:
        blocks = piece_len // 512
        key_tiles = key_rows.reshape(blocks, 512, key_rows.shape[1])
        value_tiles = value_rows.reshape(blocks, 512, value_rows.shape[1])
        anchors = anchor + 512 * jnp.arange(blocks, dtype=jnp.int32)

        def advance(state_now, tile):
            return (
                score_update(state_now, query_matrix, query_pos, tile[0], tile[1], tile[2]),
                None,
            )

        running, ignored = lax.scan(advance, running, (key_tiles, value_tiles, anchors))
        return running
    return score_update(running, query_matrix, query_pos, key_rows, value_rows, anchor)


def local(
    stream,
    query_proj,
    key_proj,
    value_projected,
    expert_ids,
    expert_home,
    router,
    norm_gain,
    w_gate,
    w_up,
    w_down,
):
    tok_rows = stream.shape[0]
    local_width = stream.shape[1]
    top_count = expert_ids.shape[1]
    columns = lax.axis_size("ctx")
    capacity = min(tok_rows, max(2, 5 * tok_rows * top_count // (4 * columns)))
    place = lax.axis_index("ctx")
    feature_index = lax.axis_index(("section", "rep"))
    heads_dev = local_width // HEAD_SIZE
    group_width = QUERY_HEADS // KEY_VALUE_HEADS
    kv_head = feature_index * heads_dev // group_width
    query_matrix = query_proj.reshape(tok_rows, heads_dev, HEAD_SIZE)
    query_pos = place * tok_rows + jnp.arange(tok_rows, dtype=jnp.int32)
    initial = (
        jnp.full((heads_dev, tok_rows), very_negative, jnp.float32),
        jnp.zeros((heads_dev, tok_rows), jnp.float32),
        jnp.zeros((heads_dev, tok_rows, HEAD_SIZE), jnp.float32),
    )
    key_single = lax.dynamic_slice_in_dim(key_proj, kv_head * HEAD_SIZE, HEAD_SIZE, 1)
    value_single = lax.dynamic_slice_in_dim(value_projected, kv_head * HEAD_SIZE, HEAD_SIZE, 1)
    run_max, run_sum, run_acc = absorb_rows(
        initial,
        query_matrix,
        query_pos,
        lax.all_gather(key_single, "ctx", axis=0, tiled=True),
        lax.all_gather(value_single, "ctx", axis=0, tiled=True),
        jnp.int32(0),
    )
    attended = jnp.transpose(run_acc / run_sum[..., None], (1, 0, 2)).reshape(tok_rows, local_width)
    hidden = stream.astype(jnp.float32) + attended
    local_sq = jnp.sum(hidden * hidden, axis=-1)
    total_sq = lax.psum(local_sq, ("section", "rep"))
    scale_rows = lax.rsqrt(total_sq / D + epsilon)
    normed = (hidden * scale_rows[:, None] * norm_gain.astype(jnp.float32)[None, :]).astype(
        jnp.bfloat16
    )
    logits = lax.psum(
        jnp.dot(normed, router, preferred_element_type=jnp.float32), ("section", "rep")
    )
    experts_all = logits.shape[1]
    one_hot = expert_ids[:, :, None] == jnp.arange(experts_all, dtype=jnp.int32)[None, None, :]
    picked = jnp.sum(jnp.where(one_hot, logits[:, None, :], 0.0), axis=-1)
    squashed = jax.nn.sigmoid(picked)
    gates = squashed / jnp.sum(squashed, axis=-1, keepdims=True)
    target = jnp.sum(jnp.where(one_hot, expert_home[None, None, :], 0), axis=-1).reshape(-1)
    target_hot = (target[:, None] == jnp.arange(columns, dtype=jnp.int32)[None, :]).astype(
        jnp.int32
    )
    running_count = jnp.cumsum(target_hot, axis=0)
    rank = jnp.sum(target_hot * (running_count - 1), axis=-1)
    slot_index = target * capacity + rank
    placing = slot_index[None, :] == jnp.arange(columns * capacity, dtype=jnp.int32)[:, None]
    placing = jnp.any(placing.reshape(columns * capacity, tok_rows, top_count), axis=-1).astype(
        jnp.bfloat16
    )
    outgoing = jnp.dot(placing, normed, preferred_element_type=jnp.float32).astype(jnp.bfloat16)
    outgoing = outgoing.reshape(columns, capacity, local_width)
    received = lax.all_to_all(outgoing, "ctx", split_axis=0, concat_axis=0, tiled=True)
    flat_rows = received.reshape(-1, local_width)
    gate_part = jnp.dot(flat_rows, w_gate[0], preferred_element_type=jnp.float32)
    up_part = jnp.dot(flat_rows, w_up[0], preferred_element_type=jnp.float32)
    gate_full = lax.psum(gate_part.astype(jnp.bfloat16), ("section", "rep")).astype(jnp.float32)
    up_full = lax.psum(up_part.astype(jnp.bfloat16), ("section", "rep")).astype(jnp.float32)
    inner = (jax.nn.silu(gate_full) * up_full).astype(jnp.bfloat16)
    answer = jnp.dot(inner, w_down[0], preferred_element_type=jnp.float32).astype(jnp.bfloat16)
    returned = lax.all_to_all(
        answer.reshape(received.shape), "ctx", split_axis=0, concat_axis=0, tiled=True
    )
    flat_back = returned.reshape(columns * capacity, local_width)
    picked_rows = flat_back[slot_index].reshape(tok_rows, top_count, local_width)
    mixed = jnp.sum(gates[:, :, None] * picked_rows.astype(jnp.float32), axis=1)
    return (hidden + mixed).astype(jnp.bfloat16)


def solution(mesh):
    placed = (
        P(("group", "ctx"), ("section", "rep")),
        P(("group", "ctx"), ("section", "rep")),
        P(("group", "ctx"), None),
        P(("group", "ctx"), None),
        P(("group", "ctx"), None),
        P(),
        P(("section", "rep"), None),
        P(("section", "rep")),
        P("ctx", ("section", "rep"), None),
        P("ctx", ("section", "rep"), None),
        P("ctx", None, ("section", "rep")),
    )
    return jax.shard_map(
        local,
        mesh=mesh,
        in_specs=placed,
        out_specs=P(("group", "ctx"), ("section", "rep")),
        check_vma=False,
    )
```

profile of v0, /device:TPU:0, one launch (start us, length us, event | category | flops | bytes accessed | tf_op | source)
XLA Modules:
  0.0 145.9 jit_solution(16333293465355152459)
XLA Ops:
  6.5 0.9 select_reduce_fusion
  7.9 0.8 constant_dynamic-slice_fusion.1
  8.6 15.0 %all_gather.6 = bf16[512,128]{1,0:T(8,128)(2,1)S(1)} all-gather(bf16[128,128]{1,0:T(8,128)(2,1)S(1)} %constant_dynamic-slice_fusion.1), channel_id=1, replica_groups=mesh['group'=2,'ctx'=4,'section'=2,'rep'=2] {'ctx'}, dimensions={0}, use_global_device_ids=true | all-gather | bytes 163840 | tf_op jit(solution)/shard_map/all_gather | solution.py:93
  23.7 1.4 fusion
  25.2 1.3 copy-done.1
  26.5 0.5 fusion.7
  27.2 12.3 %all_gather.7 = bf16[512,128]{0,1:T(8,128)(2,1)S(1)} all-gather(bf16[128,128]{0,1:T(8,128)(2,1)S(1)} %copy.40), channel_id=1, replica_groups=mesh['group'=2,'ctx'=4,'section'=2,'rep'=2] {'ctx'}, dimensions={0}, use_global_device_ids=true | all-gather | bytes 163840 | tf_op jit(solution)/shard_map/all_gather | solution.py:94
  39.5 2.3 %fusion.19 = f32[128,8,128]{0,2,1:T(8,128)S(1)} fusion(f32[512,128,8]{1,0,2:T(8,128)} %copy-done.1, f32[8,128]{1,0:T(8,128)S(1)} %get-tuple-element.8, pred[128,512]{0,1:T(8,128)(4,1)S(1)} %iota_compare_fusion.1, f32[128,8]{0,1:T(8,128)S(1)} %bitcast_add_fusion, f32[128,8]{0,1:T(8,128)S(1)} %get-tuple-element.7, bf16[512,128]{0,1:T(8,128)(2,1)S(1)} %all_gather.7), kind=kOutput, calls=%fused_computation.18 | convolution fusion | flops 137101312 | bytes 2830336 | tf_op jit(solution)/shard_map/htp,pa->hta/dot_general | solution.py:32
  41.8 0.2 copy.31
  42.1 5.7 %psum.28 = f32[128]{0:T(128)S(1)} all-reduce(f32[128]{0:T(128)S(1)} %multiply_reduce_fusion.1), channel_id=1, replica_groups=mesh['group'=2,'ctx'=4,'section'=2,'rep'=2] {'section','rep'}, use_global_device_ids=true, to_apply=%region_3.4 | all-reduce | flops 128 | bytes 1024 | tf_op jit(solution)/shard_map/psum | solution.py:100
  47.8 1.2 reduce-window.6
  49.9 0.3 convolution_convert_fusion
  50.2 21.1 %all_to_all.10 = bf16[4,80,1024]{2,1,0:T(8,128)(2,1)S(1)} all-to-all(bf16[4,80,1024]{2,1,0:T(8,128)(2,1)S(1)} %bitcast.84), channel_id=1, replica_groups=mesh['group'=2,'ctx'=4,'section'=2,'rep'=2] {'ctx'}, dimensions={0} | all-to-all | bytes 1310720 | tf_op jit(solution)/shard_map/all_to_all | solution.py:126
  71.3 1.5 fusion.12
  72.8 1.5 %fusion.15 = bf16[320,768]{1,0:T(8,128)(2,1)} fusion(bf16[320,1024]{1,0:T(8,128)(2,1)S(1)} %bitcast.87, bf16[1,1024,768]{2,1,0:T(8,128)(2,1)S(1)} %copy-done.8), kind=kOutput, calls=%fused_computation.15 | convolution fusion | flops 503562240 | bytes 2719744 | tf_op jit(solution)/shard_map/dot_general | solution.py:129
  74.3 35.0 %all-reduce.3.cloned.1.call-done = (bf16[320,768]{1,0:T(8,128)(2,1)}, bf16[320,768]{1,0:T(8,128)(2,1)}) async-done(((bf16[320,768]{1,0:T(8,128)(2,1)}, bf16[320,768]{1,0:T(8,128)(2,1)}), (bf16[320,768]{1,0:T(8,128)(2,1)}, bf16[320,768]{1,0:T(8,128)(2,1)})) %all-reduce.3.cloned.1.call-update) | async-done | bytes 983056 | tf_op jit(solution)/shard_map/psum | solution.py:131
  109.3 2.8 %fusion.9 = bf16[320,1024]{1,0:T(8,128)(2,1)} fusion(bf16[1,768,1024]{2,1,0:T(8,128)(2,1)S(1)} %copy-done, bf16[320,768]{1,0:T(8,128)(2,1)} %get-tuple-element.5, bf16[320,768]{1,0:T(8,128)(2,1)} %get-tuple-element.6), kind=kOutput, calls=%fused_computation.13 | convolution fusion | flops 505610240 | bytes 3211264 | tf_op jit(solution)/shard_map/dot_general | solution.py:133
  112.1 4.6 %all-to-all-start.1 = ((bf16[4,80,1024]{2,1,0:T(8,128)(2,1)}), bf16[4,80,1024]{2,1,0:T(8,128)(2,1)S(1)}, u32[]{:S(2)}, u32[]{:S(2)}) async-start(bf16[4,80,1024]{2,1,0:T(8,128)(2,1)} %bitcast.85), calls=%async_computation.1 | async-start | bytes 1310720 | tf_op jit(solution)/shard_map/all_to_all | solution.py:134
  116.9 5.9 %psum.29 = f32[128,4]{0,1:T(4,128)S(1)} all-reduce(f32[128,4]{0,1:T(4,128)S(1)} %fusion.45), channel_id=1, replica_groups=mesh['group'=2,'ctx'=4,'section'=2,'rep'=2] {'section','rep'}, use_global_device_ids=true, to_apply=%region_4.5 | all-reduce | flops 512 | bytes 4096 | tf_op jit(solution)/shard_map/psum | solution.py:105
  123.3 9.9 %all-to-all-done.1 = bf16[4,80,1024]{2,1,0:T(8,128)(2,1)S(1)} async-done(((bf16[4,80,1024]{2,1,0:T(8,128)(2,1)}), bf16[4,80,1024]{2,1,0:T(8,128)(2,1)S(1)}, u32[]{:S(2)}, u32[]{:S(2)}) %all-to-all-start.1) | async-done | bytes 655392 | tf_op jit(solution)/shard_map/all_to_all | solution.py:134
  133.2 2.0 %gather_fusion = bf16[256,1024]{1,0:T(8,128)(2,1)} fusion(bf16[320,1024]{1,0:T(8,128)(2,1)S(1)} %bitcast.83, s32[1024]{0:T(1024)S(1)} %pad_clamp_fusion), kind=kCustom, calls=%fused_computation | custom fusion | bytes 1049600 | tf_op jit(solution)/shard_map/gather | solution.py:138
  135.2 1.7 %reshape.137 = f32[128,2,1024]{2,1,0:T(2,128)S(1)} reshape(bf16[256,1024]{1,0:T(8,128)(2,1)} %gather_fusion) | data formatting | bytes 1572864 | tf_op jit(solution)/shard_map/convert_element_type | solution.py:139
  136.9 1.3 multiply_reduce_fusion
  138.2 0.8 add_convert_fusion
  (53 shorter events, 2.2 us)
Async XLA Ops:
  6.5 102.7 %copy-start = (bf16[1,768,1024]{2,1,0:T(8,128)(2,1)S(1)}, bf16[1,768,1024]{2,1,0:T(8,128)(2,1)}, u32[]{:S(2)}) copy-start(bf16[1,768,1024]{2,1,0:T(8,128)(2,1)} %param.21) | copy-start | bytes 4718596
  6.5 102.7 %all-reduce.3.cloned.1.call-start = ((), (), s32[]{:S(2)}) async-start(), calls=%async_computation.2 | async-start | bytes 1966080 | tf_op jit(solution)/shard_map/psum | solution.py:131
  23.7 3.3 %copy-start.3 = (bf16[128,256]{1,0:T(8,128)(2,1)S(1)}, bf16[128,256]{1,0:T(8,128)(2,1)}, u32[]{:S(2)}) copy-start(bf16[128,256]{1,0:T(8,128)(2,1)} %param.14) | copy-start | bytes 196612
  25.2 1.4 copy-start.1
  39.5 2.5 %copy-start.2 = (bf16[128,1024]{1,0:T(8,128)(2,1)S(1)}, bf16[128,1024]{1,0:T(8,128)(2,1)}, u32[]{:S(2)}) copy-start(bf16[128,1024]{1,0:T(8,128)(2,1)} %param.11) | copy-start | bytes 786436
  39.5 8.3 %copy-start.6 = (bf16[1024]{0:T(1024)(128)(2,1)S(1)}, bf16[1024]{0:T(1024)(128)(2,1)}, u32[]{:S(2)}) copy-start(bf16[1024]{0:T(1024)(128)(2,1)} %param.18) | copy-start | bytes 6148
  49.7 21.7 %copy-start.7 = (bf16[1,1024,768]{2,1,0:T(8,128)(2,1)S(1)}, bf16[1,1024,768]{2,1,0:T(8,128)(2,1)}, u32[]{:S(2)}) copy-start(bf16[1,1024,768]{2,1,0:T(8,128)(2,1)} %param.19) | copy-start | bytes 4718596
  71.3 1.5 %copy-start.8 = (bf16[1,1024,768]{2,1,0:T(8,128)(2,1)S(1)}, bf16[1,1024,768]{2,1,0:T(8,128)(2,1)}, u32[]{:S(2)}) copy-start(bf16[1,1024,768]{2,1,0:T(8,128)(2,1)} %param.20) | copy-start | bytes 4718596
  109.3 7.4 %copy-start.4 = (bf16[1024,4]{0,1:T(4,128)(2,1)S(1)}, bf16[1024,4]{0,1:T(4,128)(2,1)}, u32[]{:S(2)}) copy-start(bf16[1024,4]{0,1:T(4,128)(2,1)} %param.17) | copy-start | bytes 24580
  109.3 13.5 %copy-start.5 = (s32[128,2]{0,1:T(2,128)S(1)}, s32[128,2]{0,1:T(2,128)}, u32[]{:S(2)}) copy-start(s32[128,2]{0,1:T(2,128)} %param.15) | copy-start | bytes 3076
  112.1 21.1 %all-to-all-start.1 = ((bf16[4,80,1024]{2,1,0:T(8,128)(2,1)}), bf16[4,80,1024]{2,1,0:T(8,128)(2,1)S(1)}, u32[]{:S(2)}, u32[]{:S(2)}) async-start(bf16[4,80,1024]{2,1,0:T(8,128)(2,1)} %bitcast.85), calls=%async_computation.1 | async-start | bytes 1310720 | tf_op jit(solution)/shard_map/all_to_all | solution.py:134
Sparse Core Ops, SparseCore 0:
  74.4 34.8 all-reduce.2
where the time goes:
time: 146 us
  blocking collectives  60 us (41%)
  waiting for transfers between devices  45 us (31%)
  between operations  13.6 us (9%)
  matrix products  9.95 us (7%)
  local copies, waits for them, and re-layouts  7.34 us (5%)
  other arithmetic  5.41 us (4%)
  starting transfers between devices  4.59 us (3%)
    psum x1, waiting for transfers between devices, local(): lax.psum(up_part.astype(jnp.bfloat16), ('section', 'rep'))  35 us
    all_to_all x1, blocking collectives, local(): lax.all_to_all(outgoing, 'ctx', split_axis=0, concat_axis=0, tiled=True)  21.1 us
    all_gather x1, blocking collectives, local(): lax.all_gather(key_single, 'ctx', axis=0, tiled=True)  15 us
    all_gather x1, blocking collectives, local(): lax.all_gather(value_single, 'ctx', axis=0, tiled=True)  12.3 us
    all_to_all x1, waiting for transfers between devices, local(): lax.all_to_all(answer.reshape(received.shape), 'ctx', split_axis=0, conca...  9.94 us
    psum x1, blocking collectives, local(): lax.psum(jnp.dot(normed, router, preferred_element_type=jnp.float32), ('s...  5.95 us
    psum x1, blocking collectives, local(): total_sq = lax.psum(local_sq, ('section', 'rep'))  5.66 us
    all_to_all x1, starting transfers between devices, local(): lax.all_to_all(answer.reshape(received.shape), 'ctx', split_axis=0, conca...  4.59 us
  transfers between devices with their start and end apart: 2, of which 2 were waited for; matrix products, arithmetic and copies ran while one was open for 0% of the time, Pallas kernels for 0%

commit v1 on v0

v1 whole, which is shorter than its diff:
```python
import functools
import math

import jax
import jax.numpy as jnp
from jax import lax
from jax.experimental import pallas as pl
from jax.experimental.pallas import tpu as pltpu
from jax.sharding import PartitionSpec as P

HEAD_SIZE = 128
LANES = 128
EPSILON = 1e-06
HIDDEN_MASK = -1e30
VMEM_LIMIT = 48 * 1024 * 1024

F32 = jnp.float32
BF16 = jnp.bfloat16
NT = (((1,), (1,)), ((), ()))


def dot(a, b):
    return jnp.dot(a, b, preferred_element_type=F32)


def dot_nt(a, b):
    return lax.dot_general(a, b, NT, preferred_element_type=F32)


def vmem_call(body, out_shape, n_scalar, n_in, scratch=(), flops=0, bytes_accessed=0):
    multi = isinstance(out_shape, (tuple, list))
    n_out = len(out_shape) if multi else 1
    whole = pl.BlockSpec(memory_space=pltpu.VMEM)
    return pl.pallas_call(
        body,
        out_shape=out_shape,
        in_specs=[pl.BlockSpec(memory_space=pltpu.SMEM)] * n_scalar + [whole] * n_in,
        out_specs=[whole] * n_out if multi else whole,
        scratch_shapes=list(scratch),
        compiler_params=pltpu.CompilerParams(vmem_limit_bytes=VMEM_LIMIT),
        cost_estimate=pl.CostEstimate(
            flops=flops, bytes_accessed=bytes_accessed, transcendentals=0
        ),
    )


def attend_kernel(n, cap, place_ref, q_ref, stream_ref, gain_ref, router_ref, target_ref, *rest):
    kv_refs, (hidden_ref, stats_ref), row_refs, (k_all, v_all, gained) = (
        rest[:n],
        rest[n : n + 2],
        rest[n + 2 : 2 * n + 2],
        rest[2 * n + 2 :],
    )
    place = place_ref[0]
    tokens = q_ref.shape[0]
    heads = q_ref.shape[1] // HEAD_SIZE
    for back in range(n):
        rows = slice(back * tokens, (back + 1) * tokens)
        k_all[rows, :] = kv_refs[back][:, :HEAD_SIZE]
        v_all[rows, :] = kv_refs[back][:, HEAD_SIZE:]
    row = lax.broadcasted_iota(jnp.int32, (tokens, n * tokens), 0)
    col = lax.broadcasted_iota(jnp.int32, (tokens, n * tokens), 1)
    visible = jnp.logical_and(col <= jnp.where(col < tokens, row, n * tokens), col < (place + 1) * tokens)
    squares = jnp.zeros((tokens, 1), F32)
    for head in range(heads):
        cols = slice(head * HEAD_SIZE, (head + 1) * HEAD_SIZE)
        scores = dot_nt(q_ref[:, cols], k_all[...]) * (1.0 / math.sqrt(HEAD_SIZE))
        scores = jnp.where(visible, scores, HIDDEN_MASK)
        expo = jnp.exp(scores - jnp.max(scores, axis=-1, keepdims=True))
        total = jnp.sum(expo, axis=-1, keepdims=True)
        attended = dot(expo.astype(BF16), v_all[...]) / total
        hidden = stream_ref[:, cols].astype(F32) + attended
        hidden_ref[:, cols] = hidden
        squares = squares + jnp.sum(hidden * hidden, axis=-1, keepdims=True)
        gained[:, cols] = (hidden * gain_ref[:, cols].astype(F32)).astype(BF16)
    values = gained[...]
    stats = dot_nt(router_ref[...], values)
    stat_row = lax.broadcasted_iota(jnp.int32, stats.shape, 0)
    squares_row = jnp.transpose(jnp.broadcast_to(squares, (tokens, LANES)))[0:1, :]
    stats_ref[...] = jnp.where(stat_row == stats.shape[0] - 1, squares_row, stats)
    earlier = (
        lax.broadcasted_iota(jnp.int32, (tokens, tokens), 0)
        < lax.broadcasted_iota(jnp.int32, (tokens, tokens), 1)
    ).astype(BF16)
    slot = lax.broadcasted_iota(jnp.int32, (cap, tokens), 0)
    for j in range(n):
        member = jnp.sum(
            (target_ref[...] == jnp.bitwise_xor(place, j)).astype(F32), axis=0, keepdims=True
        )
        rank = dot(jnp.broadcast_to(member, (8, tokens)).astype(BF16), earlier)[0:1, :]
        rank = jnp.where(member > 0.5, rank, -1.0).astype(jnp.int32)
        placing = (slot == rank).astype(F32).astype(BF16)
        row_refs[j][...] = dot(placing, values).astype(BF16)


def up_kernel(n_blocks, rep_ref, gate_ref, up_ref, gain_ref, *rest):
    blocks, (keep_ref, send_ref) = rest[:n_blocks], rest[n_blocks:]
    half = gate_ref.shape[1] // 2
    cap = blocks[0].shape[0]
    mine = pl.multiple_of(rep_ref[0] * half, LANES)
    other = pl.multiple_of((1 - rep_ref[0]) * half, LANES)
    rows = (
        blocks[0][...] if n_blocks == 1 else jnp.concatenate([b[...] for b in blocks], axis=0)
    )
    plain = rows.astype(F32) / gain_ref[...].astype(F32)
    squares = jnp.sum(plain * plain, axis=-1, keepdims=True)
    high = squares.astype(BF16)
    low = (squares - high.astype(F32)).astype(BF16)
    lane = lax.broadcasted_iota(jnp.int32, (rows.shape[0], LANES), 1)
    send_ref[:, :half] = dot(rows, gate_ref[:, pl.ds(other, half)]).astype(BF16)
    send_ref[:, half : 2 * half] = dot(rows, up_ref[:, pl.ds(other, half)]).astype(BF16)
    send_ref[:, 2 * half :] = jnp.where(lane < LANES // 2, high.astype(F32), low.astype(F32)).astype(BF16)
    keep_ref[:, :half] = dot(rows, gate_ref[:, pl.ds(mine, half)])
    keep_ref[:, half : 2 * half] = dot(rows, up_ref[:, pl.ds(mine, half)])
    keep_ref[:, 2 * half :] = jnp.broadcast_to(squares, lane.shape)


def received_squares(ref, start):
    return jnp.sum(ref[:, start:].astype(F32), axis=-1, keepdims=True) * (2.0 / LANES)


def add_kernel(keep_ref, got_ref, sum_ref, send_ref):
    wide = keep_ref.shape[1] - LANES
    both = keep_ref[:, :wide] + got_ref[:, :wide].astype(F32)
    sum_ref[:, :wide] = both
    send_ref[:, :wide] = both.astype(BF16)
    squares = keep_ref[:, wide:] + received_squares(got_ref, wide)
    sum_ref[:, wide:] = squares
    high = squares.astype(BF16).astype(F32)
    lane = lax.broadcasted_iota(jnp.int32, squares.shape, 1)
    send_ref[:, wide:] = jnp.where(lane < LANES // 2, high, squares - high).astype(BF16)


def inner_kernel(features, sum_ref, got_ref, inner_ref):
    wide = sum_ref.shape[1] - LANES
    half = wide // 2
    squares = sum_ref[:, wide : wide + 1] + received_squares(got_ref, wide)
    scale = lax.rsqrt(squares * (1.0 / features) + EPSILON)
    gate = (sum_ref[:, :half] + got_ref[:, :half].astype(F32)) * scale
    up = (sum_ref[:, half:wide] + got_ref[:, half:wide].astype(F32)) * scale
    inner_ref[...] = (gate * jax.nn.sigmoid(gate) * up).astype(BF16)


def down_kernel(rep_ref, down_ref, mine_ref, other_ref, *out_refs):
    half = mine_ref.shape[1]
    mine = pl.multiple_of(rep_ref[0] * half, LANES)
    other = pl.multiple_of((1 - rep_ref[0]) * half, LANES)
    answer = dot(mine_ref[...], down_ref[pl.ds(mine, half), :]) + dot(
        other_ref[...], down_ref[pl.ds(other, half), :]
    )
    cap = out_refs[0].shape[0]
    for i, out_ref in enumerate(out_refs):
        out_ref[...] = answer[i * cap : (i + 1) * cap].astype(BF16)


def mix_kernel(n, features, experts, place_ref, hidden_ref, stats_ref, ids_ref, target_ref, *rest):
    answers, (out_ref, stacked) = rest[:n], rest[n:]
    place = place_ref[0]
    tokens = hidden_ref.shape[0]
    top = ids_ref.shape[1]
    cap = answers[0].shape[0]
    for j in range(n):
        stacked[j * cap : (j + 1) * cap, :] = answers[j][...]
    stats = jnp.transpose(stats_ref[...])
    last = stats.shape[1] - 1
    scale = lax.rsqrt(stats[:, last : last + 1] * (1.0 / features) + EPSILON)
    logits = stats * scale
    kinds = lax.broadcasted_iota(jnp.int32, stats.shape, 1)
    squashed = [
        jax.nn.sigmoid(
            jnp.sum(jnp.where(kinds == ids_ref[:, k : k + 1], logits, 0.0), axis=-1, keepdims=True)
        )
        for k in range(top)
    ]
    whole = functools.reduce(lambda a, b: a + b, squashed)
    blocks = jnp.bitwise_xor(lax.broadcasted_iota(jnp.int32, (tokens, LANES), 1), place)
    named = [target_ref[:, k : k + 1] == blocks for k in range(top)]
    member = functools.reduce(lambda a, b: a + b, [x.astype(F32) for x in named])
    later = (
        lax.broadcasted_iota(jnp.int32, (tokens, tokens), 0)
        > lax.broadcasted_iota(jnp.int32, (tokens, tokens), 1)
    ).astype(F32).astype(BF16)
    rank = dot(later, member.astype(BF16))
    rank = rank + lax.broadcasted_iota(jnp.int32, rank.shape, 1).astype(F32) * float(cap)
    slot = lax.broadcasted_iota(jnp.int32, (tokens, n * cap), 1)
    weights = jnp.zeros((tokens, n * cap), F32)
    for k in range(top):
        at = jnp.sum(jnp.where(named[k], rank, 0.0), axis=-1, keepdims=True).astype(jnp.int32)
        weights = weights + jnp.where(slot == at, squashed[k] / whole, 0.0)
    high = weights.astype(BF16)
    low = (weights - high.astype(F32)).astype(BF16)
    mixed = dot(high, stacked[...]) + dot(low, stacked[...])
    out_ref[...] = (hidden_ref[...] + mixed).astype(out_ref.dtype)


def swap(x, axis):
    return lax.ppermute(x, axis, [(0, 1), (1, 0)])


def direct(
    stream,
    query_proj,
    key_proj,
    value_projected,
    expert_ids,
    expert_home,
    router,
    norm_gain,
    w_gate,
    w_up,
    w_down,
):
    tokens, width = stream.shape
    top = expert_ids.shape[1]
    n = lax.axis_size("ctx")
    features = width * lax.axis_size(("section", "rep"))
    experts = router.shape[1]
    hid = w_gate.shape[2]
    cap = capacity_of(tokens, top, n)
    place = lax.axis_index("ctx").astype(jnp.int32)
    rep = lax.axis_index("rep").astype(jnp.int32)
    where = place.reshape(1)
    side = rep.reshape(1)
    heads = width // HEAD_SIZE
    group_width = features // key_proj.shape[1]
    kv_head = lax.axis_index(("section", "rep")) * heads // group_width

    def exchange(x, j):
        return lax.ppermute(x, "ctx", [(i, i ^ j) for i in range(n)])

    own_kv = jnp.concatenate(
        [
            lax.dynamic_slice_in_dim(a, kv_head * HEAD_SIZE, HEAD_SIZE, 1)
            for a in (key_proj, value_projected)
        ],
        axis=1,
    )
    kvs = [own_kv] + [
        lax.ppermute(own_kv, "ctx", [(i, i + back) for i in range(n - back)])
        for back in range(1, n)
    ]
    one_hot = expert_ids[:, :, None] == jnp.arange(experts, dtype=jnp.int32)[None, None, :]
    target = jnp.sum(jnp.where(one_hot, expert_home[None, None, :], 0), axis=-1)
    gain = norm_gain.reshape(1, width)
    stat_rows = -(-(experts + 1) // 8) * 8
    router_rows = jnp.pad(router.T, ((0, stat_rows - experts), (0, 0)))

    hidden, stats, *rows = vmem_call(
        functools.partial(attend_kernel, n, cap),
        [
            jax.ShapeDtypeStruct((tokens, width), F32),
            jax.ShapeDtypeStruct((stat_rows, tokens), F32),
        ]
        + [jax.ShapeDtypeStruct((cap, width), BF16)] * n,
        1,
        5 + n,
        scratch=[
            pltpu.VMEM((n * tokens, HEAD_SIZE), BF16),
            pltpu.VMEM((n * tokens, HEAD_SIZE), BF16),
            pltpu.VMEM((tokens, width), BF16),
        ],
        flops=4 * tokens * n * tokens * width,
        bytes_accessed=10 * tokens * width,
    )(where, query_proj, stream, gain, router_rows, target.T, *kvs)

    order = sorted(range(1, n), key=lambda j: (j < n // 2, j))
    arrived = {j: exchange(rows[j], j) for j in order}
    arrived[0] = rows[0]

    stats = stats + swap(stats, "rep")
    stats = stats + swap(stats, "section")

    far = [(j,) for j in order if j >= n // 2]
    near = tuple(j for j in range(n // 2))
    answers = {}
    for chain in far + [near]:
        count = len(chain) * cap
        wide = hid + LANES
        keep, send = vmem_call(
            functools.partial(up_kernel, len(chain)),
            [jax.ShapeDtypeStruct((count, wide), F32), jax.ShapeDtypeStruct((count, wide), BF16)],
            1,
            3 + len(chain),
            flops=4 * count * width * hid,
            bytes_accessed=4 * width * hid,
        )(side, w_gate[0], w_up[0], gain, *[arrived[j] for j in chain])
        both, send = vmem_call(
            add_kernel,
            [jax.ShapeDtypeStruct((count, wide), F32), jax.ShapeDtypeStruct((count, wide), BF16)],
            0,
            2,
            flops=count * wide,
            bytes_accessed=10 * count * wide,
        )(keep, swap(send, "rep"))
        inner = vmem_call(
            functools.partial(inner_kernel, features),
            jax.ShapeDtypeStruct((count, hid // 2), BF16),
            0,
            2,
            flops=4 * count * wide,
            bytes_accessed=6 * count * wide,
        )(both, swap(send, "section"))
        outs = vmem_call(
            down_kernel,
            [jax.ShapeDtypeStruct((cap, width), BF16)] * len(chain),
            1,
            3,
            flops=2 * count * hid * width,
            bytes_accessed=2 * hid * width,
        )(side, w_down[0], inner, swap(inner, "rep"))
        for j, out in zip(chain, outs):
            answers[j] = exchange(out, j) if j else out

    return vmem_call(
        functools.partial(mix_kernel, n, features, experts),
        jax.ShapeDtypeStruct((tokens, width), BF16),
        1,
        4 + n,
        scratch=[pltpu.VMEM((n * cap, width), BF16)],
        flops=4 * tokens * n * cap * width,
        bytes_accessed=6 * tokens * width + 2 * n * cap * width,
    )(where, hidden, stats, expert_ids, target, *[answers[j] for j in range(n)])


def capacity_of(tokens, top, n):
    return min(tokens, max(2, 5 * tokens * top // (4 * n)))


def score_update(running, query_matrix, query_pos, key_block, value_block, key_anchor):
    run_max, run_sum, run_acc = running
    key_len = key_block.shape[0]
    scores = jnp.einsum(
        "tha,pa->htp", query_matrix, key_block, preferred_element_type=jnp.float32
    ) * (1.0 / math.sqrt(HEAD_SIZE))
    key_pos = key_anchor + jnp.arange(key_len, dtype=jnp.int32)
    visible = query_pos[:, None] >= key_pos[None, :]
    scores = jnp.where(visible, scores, HIDDEN_MASK)
    new_max = jnp.maximum(run_max, jnp.max(scores, axis=-1))
    expo = jnp.where(visible, jnp.exp(scores - new_max[..., None]), 0.0)
    factor = jnp.exp(run_max - new_max)
    new_sum = run_sum * factor + jnp.sum(expo, axis=-1)
    weights = expo.astype(jnp.bfloat16)
    new_acc = run_acc * factor[..., None] + jnp.einsum(
        "htp,pa->hta", weights, value_block, preferred_element_type=jnp.float32
    )
    return (new_max, new_sum, new_acc)


def absorb_rows(running, query_matrix, query_pos, key_rows, value_rows, anchor):
    piece_len = key_rows.shape[0]
    if piece_len > 512 and piece_len % 512 == 0:
        blocks = piece_len // 512
        key_tiles = key_rows.reshape(blocks, 512, key_rows.shape[1])
        value_tiles = value_rows.reshape(blocks, 512, value_rows.shape[1])
        anchors = anchor + 512 * jnp.arange(blocks, dtype=jnp.int32)

        def advance(state_now, tile):
            return (
                score_update(state_now, query_matrix, query_pos, tile[0], tile[1], tile[2]),
                None,
            )

        running, ignored = lax.scan(advance, running, (key_tiles, value_tiles, anchors))
        return running
    return score_update(running, query_matrix, query_pos, key_rows, value_rows, anchor)


def general(
    stream,
    query_proj,
    key_proj,
    value_projected,
    expert_ids,
    expert_home,
    router,
    norm_gain,
    w_gate,
    w_up,
    w_down,
):
    tok_rows, local_width = stream.shape
    top_count = expert_ids.shape[1]
    columns = lax.axis_size("ctx")
    features = local_width * lax.axis_size(("section", "rep"))
    capacity = capacity_of(tok_rows, top_count, columns)
    place = lax.axis_index("ctx")
    feature_index = lax.axis_index(("section", "rep"))
    heads_dev = local_width // HEAD_SIZE
    group_width = features // key_proj.shape[1]
    kv_head = feature_index * heads_dev // group_width
    query_matrix = query_proj.reshape(tok_rows, heads_dev, HEAD_SIZE)
    query_pos = place * tok_rows + jnp.arange(tok_rows, dtype=jnp.int32)
    initial = (
        jnp.full((heads_dev, tok_rows), HIDDEN_MASK, jnp.float32),
        jnp.zeros((heads_dev, tok_rows), jnp.float32),
        jnp.zeros((heads_dev, tok_rows, HEAD_SIZE), jnp.float32),
    )
    key_single = lax.dynamic_slice_in_dim(key_proj, kv_head * HEAD_SIZE, HEAD_SIZE, 1)
    value_single = lax.dynamic_slice_in_dim(value_projected, kv_head * HEAD_SIZE, HEAD_SIZE, 1)
    run_max, run_sum, run_acc = absorb_rows(
        initial,
        query_matrix,
        query_pos,
        lax.all_gather(key_single, "ctx", axis=0, tiled=True),
        lax.all_gather(value_single, "ctx", axis=0, tiled=True),
        jnp.int32(0),
    )
    attended = jnp.transpose(run_acc / run_sum[..., None], (1, 0, 2)).reshape(tok_rows, local_width)
    hidden = stream.astype(jnp.float32) + attended
    total_sq = lax.psum(jnp.sum(hidden * hidden, axis=-1), ("section", "rep"))
    scale_rows = lax.rsqrt(total_sq / features + EPSILON)
    normed = (hidden * scale_rows[:, None] * norm_gain.astype(jnp.float32)[None, :]).astype(
        jnp.bfloat16
    )
    logits = lax.psum(dot(normed, router), ("section", "rep"))
    experts_all = logits.shape[1]
    one_hot = expert_ids[:, :, None] == jnp.arange(experts_all, dtype=jnp.int32)[None, None, :]
    picked = jnp.sum(jnp.where(one_hot, logits[:, None, :], 0.0), axis=-1)
    squashed = jax.nn.sigmoid(picked)
    gates = squashed / jnp.sum(squashed, axis=-1, keepdims=True)
    target = jnp.sum(jnp.where(one_hot, expert_home[None, None, :], 0), axis=-1)
    named = target[:, :, None] == jnp.arange(columns, dtype=jnp.int32)[None, None, :]
    member = jnp.any(named, axis=1).astype(jnp.bfloat16)
    before = jnp.tril(jnp.ones((tok_rows, tok_rows), jnp.bfloat16), -1)
    rank = dot(before, member).astype(jnp.int32)
    rank = jnp.sum(jnp.where(named, rank[:, None, :], 0), axis=-1)
    slot_index = (target * capacity + rank).reshape(-1)
    placing = slot_index[None, :] == jnp.arange(columns * capacity, dtype=jnp.int32)[:, None]
    placing = jnp.any(placing.reshape(columns * capacity, tok_rows, top_count), axis=-1).astype(
        jnp.bfloat16
    )
    outgoing = dot(placing, normed).astype(jnp.bfloat16)
    outgoing = outgoing.reshape(columns, capacity, local_width)
    received = lax.all_to_all(outgoing, "ctx", split_axis=0, concat_axis=0, tiled=True)
    flat_rows = received.reshape(-1, local_width)
    gate_part = dot(flat_rows, w_gate[0])
    up_part = dot(flat_rows, w_up[0])
    gate_full = lax.psum(gate_part.astype(jnp.bfloat16), ("section", "rep")).astype(jnp.float32)
    up_full = lax.psum(up_part.astype(jnp.bfloat16), ("section", "rep")).astype(jnp.float32)
    inner = (jax.nn.silu(gate_full) * up_full).astype(jnp.bfloat16)
    answer = dot(inner, w_down[0]).astype(jnp.bfloat16)
    returned = lax.all_to_all(
        answer.reshape(received.shape), "ctx", split_axis=0, concat_axis=0, tiled=True
    )
    flat_back = returned.reshape(columns * capacity, local_width)
    picked_rows = flat_back[slot_index].reshape(tok_rows, top_count, local_width)
    mixed = jnp.sum(gates[:, :, None] * picked_rows.astype(jnp.float32), axis=1)
    return (hidden + mixed).astype(jnp.bfloat16)


def solution(mesh):
    size = dict(mesh.shape)
    pairs = size["section"] == 2 and size["rep"] == 2
    short = size["ctx"] in (2, 4)
    placed = (
        P(("group", "ctx"), ("section", "rep")),
        P(("group", "ctx"), ("section", "rep")),
        P(("group", "ctx"), None),
        P(("group", "ctx"), None),
        P(("group", "ctx"), None),
        P(),
        P(("section", "rep"), None),
        P(("section", "rep")),
        P("ctx", ("section", "rep"), None),
        P("ctx", ("section", "rep"), None),
        P("ctx", None, ("section", "rep")),
    )
    return jax.shard_map(
        direct if pairs and short else general,
        mesh=mesh,
        in_specs=placed,
        out_specs=P(("group", "ctx"), ("section", "rep")),
        check_vma=False,
    )
```

time: 146 us -> 75 us (0.51)
  blocking collectives: 60 us -> 0 us
  starting transfers between devices: 4.59 us -> 25.4 us
  between operations: 13.6 us -> 0.26 us
  waiting for transfers between devices: 45 us -> 31.9 us
  matrix products: 9.95 us -> 0 us
  Pallas kernels: 0 us -> 9.08 us
  other arithmetic: 5.41 us -> 0.79 us
    psum x1 -> x0, waiting for transfers between devices: 35 us -> none  [local(): lax.psum(up_part.astype(jnp.bfloat16), ('section', 'rep'))]
    ppermute x0 -> x20, waiting for transfers between devices: none -> 31.9 us  [the longest x6 23 us: exchange(): return lax.ppermute(x, 'ctx', [(i, i ^ j) for i in range(n)])]
    all_gather x2 -> x0, blocking collectives: 27.3 us -> none  [the longest x1 15 us: local(): lax.all_gather(key_single, 'ctx', axis=0, tiled=True)]
    ppermute x0 -> x20, starting transfers between devices: none -> 25.4 us  [the longest x3 10.7 us: direct(): lax.ppermute(own_kv, 'ctx', [(i, i + back) for i in range(n - back)])]
    all_to_all x1 -> x0, blocking collectives: 21.1 us -> none  [local(): lax.all_to_all(outgoing, 'ctx', split_axis=0, concat_axis=0, tiled=True)]
    psum x2 -> x0, blocking collectives: 11.6 us -> none  [the longest x1 5.95 us: local(): lax.psum(jnp.dot(normed, router, preferred_element_type=jnp.float32), ('s...]
    dot_general x7 -> x0, matrix products: 9.95 us -> none  [the longest x1 2.83 us: local(): jnp.dot(inner, w_down[0], preferred_element_type=jnp.float32)]
    all_to_all x1 -> x0, waiting for transfers between devices: 9.94 us -> none  [local(): lax.all_to_all(answer.reshape(received.shape), 'ctx', split_axis=0, conca...]
  transfers between devices with their start and end apart: 2 -> 20, of which waited for: 2 -> 8; matrix products, arithmetic and copies ran while one was open for 0% -> 3% of each run, Pallas kernels for 0% -> 5%
where the time goes in v1:
time: 75 us; the launch traced here: 74.6 us
  waiting for transfers between devices  31.9 us (43%)
  starting transfers between devices  25.4 us (34%)
  Pallas kernels  9.08 us (12%)
  local copies, waits for them, and re-layouts  7.13 us (10%)
  other arithmetic  0.79 us (1%)
    ppermute x6, waiting for transfers between devices, exchange(): return lax.ppermute(x, 'ctx', [(i, i ^ j) for i in range(n)])  23 us
    ppermute x3, starting transfers between devices, direct(): lax.ppermute(own_kv, 'ctx', [(i, i + back) for i in range(n - back)])  10.7 us
    ppermute x11, waiting for transfers between devices, swap(): return lax.ppermute(x, axis, [(0, 1), (1, 0)])  8.86 us
    ppermute x6, starting transfers between devices, exchange(): return lax.ppermute(x, 'ctx', [(i, i ^ j) for i in range(n)])  8.49 us
    ppermute x11, starting transfers between devices, swap(): return lax.ppermute(x, axis, [(0, 1), (1, 0)])  6.23 us
    unnamed x17, local copies, waits for them, and re-layouts  4.84 us
    pallas_call x1, Pallas kernels, direct(): vmem_call(functools.partial(attend_kernel, n, cap), [jax.ShapeDtypeStruct...  3.03 us
    pallas_call x3, Pallas kernels, direct(): vmem_call(functools.partial(up_kernel, len(chain)), [jax.ShapeDtypeStruct...  2.09 us
  transfers between devices with their start and end apart: 20, of which 8 were waited for; matrix products, arithmetic and copies ran while one was open for 3% of the time, Pallas kernels for 5%

profile of v1, /device:TPU:0, one launch (start us, length us, event | category | flops | bytes accessed | tf_op | source)
XLA Modules:
  0.0 74.6 jit_solution(4702124693544031313)
XLA Ops:
  0.8 4.9 %collective-permute-start = (bf16[128,256]{1,0:T(8,128)(2,1)S(1)}, bf16[128,256]{1,0:T(8,128)(2,1)S(1)}, u32[]{:S(2)}, u32[]{:S(2)}) collective-permute-start(bf16[128,256]{1,0:T(8,128)(2,1)S(1)} %pad_maximum_fusion.rest_0_), channel_id=1, source_target_pairs={{0,4},{4,8},{8,12},{1,5},{5,9},{9,13},{2,6},{6,10},{10,14},{3,7},{... | collective-permute-start | bytes 196616 | tf_op jit(solution)/shard_map/ppermute | solution.py:239
  5.7 4.5 %collective-permute-start.1 = (bf16[128,256]{1,0:T(8,128)(2,1)S(1)}, bf16[128,256]{1,0:T(8,128)(2,1)S(1)}, u32[]{:S(2)}, u32[]{:S(2)}) collective-permute-start(bf16[128,256]{1,0:T(8,128)(2,1)S(1)} %pad_maximum_fusion.rest_0_), channel_id=1, source_target_pairs={{0,8},{4,12},{1,9},{5,13},{2,10},{6,14},{3,11},{7,15},{16,24},{20,... | collective-permute-start | bytes 196616 | tf_op jit(solution)/shard_map/ppermute | solution.py:239
  10.2 1.3 %collective-permute-start.2 = (bf16[128,256]{1,0:T(8,128)(2,1)S(1)}, bf16[128,256]{1,0:T(8,128)(2,1)S(1)}, u32[]{:S(2)}, u32[]{:S(2)}) collective-permute-start(bf16[128,256]{1,0:T(8,128)(2,1)S(1)} %pad_maximum_fusion.rest_0_), channel_id=1, source_target_pairs={{0,12},{1,13},{2,14},{3,15},{16,28},{17,29},{18,30},{19,31}} | collective-permute-start | bytes 196616 | tf_op jit(solution)/shard_map/ppermute | solution.py:239
  13.7 0.9 %copy-done.5 = bf16[128,1024]{1,0:T(8,128)(2,1)S(1)} copy-done((bf16[128,1024]{1,0:T(8,128)(2,1)S(1)}, bf16[128,1024]{1,0:T(8,128)(2,1)}, u32[]{:S(2)}) %copy-start.5) | copy-done | bytes 262168
  14.7 0.9 %copy-done.6 = bf16[128,1024]{1,0:T(8,128)(2,1)S(1)} copy-done((bf16[128,1024]{1,0:T(8,128)(2,1)S(1)}, bf16[128,1024]{1,0:T(8,128)(2,1)}, u32[]{:S(2)}) %copy-start.6) | copy-done | bytes 262168
  15.6 3.0 %shard_map.109 = (f32[128,1024]{1,0:T(8,128)S(1)}, f32[8,128]{1,0:T(8,128)S(1)}, bf16[80,1024]{1,0:T(8,128)(2,1)S(1)}, bf16[80,1024]{1,0:T(8,128)(2,1)S(1)}, bf1...) custom-call(s32[1]{0:T(128)} %bitcast.place_ref, bf16[128,1024]{1,0:T(8,128)(2,1)S(1)} %copy-done.5, ...), custom_call_target="tpu_custom_call" | custom-call | flops 268435456 | bytes 1310720 | tf_op jit(solution)/shard_map/pallas_call | solution.py:248
  18.7 5.4 %collective-permute-done.5.rest_1_ = bf16[80,1024]{1,0:T(8,128)(2,1)S(1)} collective-permute-done((bf16[80,1024]{1,0:T(8,128)(2,1)S(1)}, bf16[80,1024]{1,0:T(8,128)(2,1)S(1)}, u32[]{:S(2)}, u32[]{:S(2)}) %collective-permute-start.5) | collective-permute-done | bytes 163872 | tf_op jit(solution)/shard_map/ppermute | solution.py:229
  24.1 1.4 %copy-done.1 = bf16[1,1024,768]{2,1,0:T(8,128)(2,1)S(1)} copy-done((bf16[1,1024,768]{2,1,0:T(8,128)(2,1)S(1)}, bf16[1,1024,768]{2,1,0:T(8,128)(2,1)}, u32[]{:S(2)}) %copy-start.1) | copy-done | bytes 1572888
  25.5 1.4 %copy-done.3 = bf16[1,1024,768]{2,1,0:T(8,128)(2,1)S(1)} copy-done((bf16[1,1024,768]{2,1,0:T(8,128)(2,1)S(1)}, bf16[1,1024,768]{2,1,0:T(8,128)(2,1)}, u32[]{:S(2)}) %copy-start.3) | copy-done | bytes 1572888
  27.9 3.9 %collective-permute-start.15 = (bf16[80,1024]{1,0:T(8,128)(2,1)S(1)}, bf16[80,1024]{1,0:T(8,128)(2,1)S(1)}, u32[]{:S(2)}, u32[]{:S(2)}) collective-permute-start(bf16[80,1024]{1,0:T(8,128)(2,1)S(1)} %get-tuple-element.40), channel_id=1, source_target_pairs={{0,12},{4,8},{8,4},{12,0},{1,13},{5,9},{9,5},{13,1},{2,14},{6,10},... | collective-permute-start | bytes 491528 | tf_op jit(solution)/shard_map/ppermute | solution.py:229
  31.9 1.6 %collective-permute-start.7 = (bf16[160,896]{1,0:T(8,128)(2,1)S(1)}, bf16[160,896]{1,0:T(8,128)(2,1)S(1)}, u32[]{:S(2)}, u32[]{:S(2)}) collective-permute-start(bf16[160,896]{1,0:T(8,128)(2,1)S(1)} %get-tuple-element.32), channel_id=1, source_target_pairs={{0,2},{2,0},{1,3},{3,1},{4,6},{6,4},{5,7},{7,5},{8,10},{10,8},{9,1... | collective-permute-start | bytes 860168 | tf_op jit(solution)/shard_map/ppermute | solution.py:197
  33.5 3.4 %collective-permute-done.15.rest_0_ = bf16[80,1024]{1,0:T(8,128)(2,1)S(1)} collective-permute-done((bf16[80,1024]{1,0:T(8,128)(2,1)S(1)}, bf16[80,1024]{1,0:T(8,128)(2,1)S(1)}, u32[]{:S(2)}, u32[]{:S(2)}) %collective-permute-start.15) | collective-permute-done | bytes 163872 | tf_op jit(solution)/shard_map/ppermute | solution.py:229
  37.6 8.0 %collective-permute-done.10.rest_0_ = bf16[80,1024]{1,0:T(8,128)(2,1)S(1)} collective-permute-done((bf16[80,1024]{1,0:T(8,128)(2,1)S(1)}, bf16[80,1024]{1,0:T(8,128)(2,1)S(1)}, u32[]{:S(2)}, u32[]{:S(2)}) %collective-permute-start.10) | collective-permute-done | bytes 163872 | tf_op jit(solution)/shard_map/ppermute | solution.py:229
  46.5 1.5 %collective-permute-start.17 = (bf16[80,896]{1,0:T(8,128)(2,1)S(1)}, bf16[80,896]{1,0:T(8,128)(2,1)S(1)}, u32[]{:S(2)}, u32[]{:S(2)}) collective-permute-start(bf16[80,896]{1,0:T(8,128)(2,1)S(1)} %get-tuple-element.44), channel_id=1, source_target_pairs={{0,2},{2,0},{1,3},{3,1},{4,6},{6,4},{5,7},{7,5},{8,10},{10,8},{9,1... | collective-permute-start | bytes 430088 | tf_op jit(solution)/shard_map/ppermute | solution.py:197
  48.2 1.2 %collective-permute-start.12 = (bf16[80,896]{1,0:T(8,128)(2,1)S(1)}, bf16[80,896]{1,0:T(8,128)(2,1)S(1)}, u32[]{:S(2)}, u32[]{:S(2)}) collective-permute-start(bf16[80,896]{1,0:T(8,128)(2,1)S(1)} %get-tuple-element.39), channel_id=1, source_target_pairs={{0,2},{2,0},{1,3},{3,1},{4,6},{6,4},{5,7},{7,5},{8,10},{10,8},{9,1... | collective-permute-start | bytes 430088 | tf_op jit(solution)/shard_map/ppermute | solution.py:197
  49.7 3.4 %collective-permute-done.17.got_ref = bf16[80,896]{1,0:T(8,128)(2,1)S(1)} collective-permute-done((bf16[80,896]{1,0:T(8,128)(2,1)S(1)}, bf16[80,896]{1,0:T(8,128)(2,1)S(1)}, u32[]{:S(2)}, u32[]{:S(2)}) %collective-permute-start.17) | collective-permute-done | bytes 143392 | tf_op jit(solution)/shard_map/ppermute | solution.py:197
  53.4 2.4 %collective-permute-done.12.got_ref = bf16[80,896]{1,0:T(8,128)(2,1)S(1)} collective-permute-done((bf16[80,896]{1,0:T(8,128)(2,1)S(1)}, bf16[80,896]{1,0:T(8,128)(2,1)S(1)}, u32[]{:S(2)}, u32[]{:S(2)}) %collective-permute-start.12) | collective-permute-done | bytes 143392 | tf_op jit(solution)/shard_map/ppermute | solution.py:197
  56.5 2.7 %collective-permute-start.19 = (bf16[80,1024]{1,0:T(8,128)(2,1)S(1)}, bf16[80,1024]{1,0:T(8,128)(2,1)S(1)}, u32[]{:S(2)}, u32[]{:S(2)}) collective-permute-start(bf16[80,1024]{1,0:T(8,128)(2,1)S(1)} %shard_map.121), channel_id=1, source_target_pairs={{0,12},{4,8},{8,4},{12,0},{1,13},{5,9},{9,5},{13,1},{2,14},{6,10},... | collective-permute-start | bytes 491528 | tf_op jit(solution)/shard_map/ppermute | solution.py:229
  60.3 1.8 %collective-permute-start.9 = (bf16[80,1024]{1,0:T(8,128)(2,1)S(1)}, bf16[80,1024]{1,0:T(8,128)(2,1)S(1)}, u32[]{:S(2)}, u32[]{:S(2)}) collective-permute-start(bf16[80,1024]{1,0:T(8,128)(2,1)S(1)} %get-tuple-element.34), channel_id=1, source_target_pairs={{0,4},{4,0},{8,12},{12,8},{1,5},{5,1},{9,13},{13,9},{2,6},{6,2},{1... | collective-permute-start | bytes 491528 | tf_op jit(solution)/shard_map/ppermute | solution.py:229
  62.1 1.2 %collective-permute-done.3 = f32[8,128]{1,0:T(8,128)S(1)} collective-permute-done((f32[8,128]{1,0:T(8,128)S(1)}, f32[8,128]{1,0:T(8,128)S(1)}, u32[]{:S(2)}, u32[]{:S(2)}) %collective-permute-start.3) | collective-permute-done | bytes 4128 | tf_op jit(solution)/shard_map/ppermute | solution.py:197
  63.2 1.5 %collective-permute-start.4 = (f32[8,128]{1,0:T(8,128)S(1)}, f32[8,128]{1,0:T(8,128)S(1)}, u32[]{:S(2)}, u32[]{:S(2)}) collective-permute-start(f32[8,128]{1,0:T(8,128)S(1)} %add.18), channel_id=1, source_target_pairs={{0,2},{2,0},{1,3},{3,1},{4,6},{6,4},{5,7},{7,5},{8,10},{10,8},{9,1... | collective-permute-start | bytes 12296 | tf_op jit(solution)/shard_map/ppermute | solution.py:197
  65.0 1.9 %collective-permute-done.4 = f32[8,128]{1,0:T(8,128)S(1)} collective-permute-done((f32[8,128]{1,0:T(8,128)S(1)}, f32[8,128]{1,0:T(8,128)S(1)}, u32[]{:S(2)}, u32[]{:S(2)}) %collective-permute-start.4) | collective-permute-done | bytes 4128 | tf_op jit(solution)/shard_map/ppermute | solution.py:197
  66.9 6.1 %collective-permute-done.14.rest_2_ = bf16[80,1024]{1,0:T(8,128)(2,1)S(1)} collective-permute-done((bf16[80,1024]{1,0:T(8,128)(2,1)S(1)}, bf16[80,1024]{1,0:T(8,128)(2,1)S(1)}, u32[]{:S(2)}, u32[]{:S(2)}) %collective-permute-start.14) | collective-permute-done | bytes 163872 | tf_op jit(solution)/shard_map/ppermute | solution.py:229
  73.0 1.6 %shard_map.122 = bf16[128,1024]{1,0:T(8,128)(2,1)} custom-call(s32[1]{0:T(128)} %bitcast.place_ref, f32[128,1024]{1,0:T(8,128)S(1)} %get-tuple-element.25.hidden_ref, f32[8,128]{1,0:T(8,128)S(1)} %add.19.stats_ref, s32[128,2]{1,0:T(8,128)S(1)} %copy.15.ids_ref, s32[128,2]{1,0:T(8,128)S(1)} %copy.16.target_ref, ...), custom_call_target="tpu_custom_call" | custom-call | flops 167772160 | bytes 1441792 | tf_op jit(solution)/shard_map/pallas_call | solution.py:314
  (55 shorter events, 8.3 us)
Async XLA Ops:
  0.8 12.9 %collective-permute-start = (bf16[128,256]{1,0:T(8,128)(2,1)S(1)}, bf16[128,256]{1,0:T(8,128)(2,1)S(1)}, u32[]{:S(2)}, u32[]{:S(2)}) collective-permute-start(bf16[128,256]{1,0:T(8,128)(2,1)S(1)} %pad_maximum_fusion.rest_0_), channel_id=1, source_target_pairs={{0,4},{4,8},{8,12},{1,5},{5,9},{9,13},{2,6},{6,10},{10,14},{3,7},{... | collective-permute-start | bytes 196616 | tf_op jit(solution)/shard_map/ppermute | solution.py:239
  5.7 8.0 %collective-permute-start.1 = (bf16[128,256]{1,0:T(8,128)(2,1)S(1)}, bf16[128,256]{1,0:T(8,128)(2,1)S(1)}, u32[]{:S(2)}, u32[]{:S(2)}) collective-permute-start(bf16[128,256]{1,0:T(8,128)(2,1)S(1)} %pad_maximum_fusion.rest_0_), channel_id=1, source_target_pairs={{0,8},{4,12},{1,9},{5,13},{2,10},{6,14},{3,11},{7,15},{16,24},{20,... | collective-permute-start | bytes 196616 | tf_op jit(solution)/shard_map/ppermute | solution.py:239
  10.2 3.5 %collective-permute-start.2 = (bf16[128,256]{1,0:T(8,128)(2,1)S(1)}, bf16[128,256]{1,0:T(8,128)(2,1)S(1)}, u32[]{:S(2)}, u32[]{:S(2)}) collective-permute-start(bf16[128,256]{1,0:T(8,128)(2,1)S(1)} %pad_maximum_fusion.rest_0_), channel_id=1, source_target_pairs={{0,12},{1,13},{2,14},{3,15},{16,28},{17,29},{18,30},{19,31}} | collective-permute-start | bytes 196616 | tf_op jit(solution)/shard_map/ppermute | solution.py:239
  18.7 5.4 %collective-permute-start.5 = (bf16[80,1024]{1,0:T(8,128)(2,1)S(1)}, bf16[80,1024]{1,0:T(8,128)(2,1)S(1)}, u32[]{:S(2)}, u32[]{:S(2)}) collective-permute-start(bf16[80,1024]{1,0:T(8,128)(2,1)S(1)} %get-tuple-element.28), channel_id=1, source_target_pairs={{0,4},{4,0},{8,12},{12,8},{1,5},{5,1},{9,13},{13,9},{2,6},{6,2},{1... | collective-permute-start | bytes 491528 | tf_op jit(solution)/shard_map/ppermute | solution.py:229
  26.9 10.0 %copy-start.2 = (bf16[1,1024,768]{2,1,0:T(8,128)(2,1)S(1)}, bf16[1,1024,768]{2,1,0:T(8,128)(2,1)}, u32[]{:S(2)}) copy-start(bf16[1,1024,768]{2,1,0:T(8,128)(2,1)} %param.19) | copy-start | bytes 4718596
  26.9 10.0 %copy-start.4 = (bf16[1,1024,768]{2,1,0:T(8,128)(2,1)S(1)}, bf16[1,1024,768]{2,1,0:T(8,128)(2,1)}, u32[]{:S(2)}) copy-start(bf16[1,1024,768]{2,1,0:T(8,128)(2,1)} %param.20) | copy-start | bytes 4718596
  27.8 3.9 %collective-permute-start.6 = (bf16[160,896]{1,0:T(8,128)(2,1)S(1)}, bf16[160,896]{1,0:T(8,128)(2,1)S(1)}, u32[]{:S(2)}, u32[]{:S(2)}) collective-permute-start(bf16[160,896]{1,0:T(8,128)(2,1)S(1)} %get-tuple-element.30), channel_id=1, source_target_pairs={{0,1},{1,0},{2,3},{3,2},{4,5},{5,4},{6,7},{7,6},{8,9},{9,8},{10,11... | collective-permute-start | bytes 860168 | tf_op jit(solution)/shard_map/ppermute | solution.py:197
  27.9 9.0 %collective-permute-start.15 = (bf16[80,1024]{1,0:T(8,128)(2,1)S(1)}, bf16[80,1024]{1,0:T(8,128)(2,1)S(1)}, u32[]{:S(2)}, u32[]{:S(2)}) collective-permute-start(bf16[80,1024]{1,0:T(8,128)(2,1)S(1)} %get-tuple-element.40), channel_id=1, source_target_pairs={{0,12},{4,8},{8,4},{12,0},{1,13},{5,9},{9,5},{13,1},{2,14},{6,10},... | collective-permute-start | bytes 491528 | tf_op jit(solution)/shard_map/ppermute | solution.py:229
  31.7 13.9 %collective-permute-start.10 = (bf16[80,1024]{1,0:T(8,128)(2,1)S(1)}, bf16[80,1024]{1,0:T(8,128)(2,1)S(1)}, u32[]{:S(2)}, u32[]{:S(2)}) collective-permute-start(bf16[80,1024]{1,0:T(8,128)(2,1)S(1)} %get-tuple-element.35), channel_id=1, source_target_pairs={{0,8},{4,12},{8,0},{12,4},{1,9},{5,13},{9,1},{13,5},{2,10},{6,14},... | collective-permute-start | bytes 491528 | tf_op jit(solution)/shard_map/ppermute | solution.py:229
  31.9 17.5 %collective-permute-start.7 = (bf16[160,896]{1,0:T(8,128)(2,1)S(1)}, bf16[160,896]{1,0:T(8,128)(2,1)S(1)}, u32[]{:S(2)}, u32[]{:S(2)}) collective-permute-start(bf16[160,896]{1,0:T(8,128)(2,1)S(1)} %get-tuple-element.32), channel_id=1, source_target_pairs={{0,2},{2,0},{1,3},{3,1},{4,6},{6,4},{5,7},{7,5},{8,10},{10,8},{9,1... | collective-permute-start | bytes 860168 | tf_op jit(solution)/shard_map/ppermute | solution.py:197
  37.5 8.8 %collective-permute-start.16 = (bf16[80,896]{1,0:T(8,128)(2,1)S(1)}, bf16[80,896]{1,0:T(8,128)(2,1)S(1)}, u32[]{:S(2)}, u32[]{:S(2)}) collective-permute-start(bf16[80,896]{1,0:T(8,128)(2,1)S(1)} %get-tuple-element.42), channel_id=1, source_target_pairs={{0,1},{1,0},{2,3},{3,2},{4,5},{5,4},{6,7},{7,6},{8,9},{9,8},{10,11... | collective-permute-start | bytes 430088 | tf_op jit(solution)/shard_map/ppermute | solution.py:197
  46.3 9.8 %copy-start = (bf16[1,768,1024]{2,1,0:T(8,128)(2,1)S(1)}, bf16[1,768,1024]{2,1,0:T(8,128)(2,1)}, u32[]{:S(2)}) copy-start(bf16[1,768,1024]{2,1,0:T(8,128)(2,1)} %param.21) | copy-start | bytes 4718596
  46.3 1.8 %collective-permute-start.11 = (bf16[80,896]{1,0:T(8,128)(2,1)S(1)}, bf16[80,896]{1,0:T(8,128)(2,1)S(1)}, u32[]{:S(2)}, u32[]{:S(2)}) collective-permute-start(bf16[80,896]{1,0:T(8,128)(2,1)S(1)} %get-tuple-element.37), channel_id=1, source_target_pairs={{0,1},{1,0},{2,3},{3,2},{4,5},{5,4},{6,7},{7,6},{8,9},{9,8},{10,11... | collective-permute-start | bytes 430088 | tf_op jit(solution)/shard_map/ppermute | solution.py:197
  46.5 6.6 %collective-permute-start.17 = (bf16[80,896]{1,0:T(8,128)(2,1)S(1)}, bf16[80,896]{1,0:T(8,128)(2,1)S(1)}, u32[]{:S(2)}, u32[]{:S(2)}) collective-permute-start(bf16[80,896]{1,0:T(8,128)(2,1)S(1)} %get-tuple-element.44), channel_id=1, source_target_pairs={{0,2},{2,0},{1,3},{3,1},{4,6},{6,4},{5,7},{7,5},{8,10},{10,8},{9,1... | collective-permute-start | bytes 430088 | tf_op jit(solution)/shard_map/ppermute | solution.py:197
  48.2 7.6 %collective-permute-start.12 = (bf16[80,896]{1,0:T(8,128)(2,1)S(1)}, bf16[80,896]{1,0:T(8,128)(2,1)S(1)}, u32[]{:S(2)}, u32[]{:S(2)}) collective-permute-start(bf16[80,896]{1,0:T(8,128)(2,1)S(1)} %get-tuple-element.39), channel_id=1, source_target_pairs={{0,2},{2,0},{1,3},{3,1},{4,6},{6,4},{5,7},{7,5},{8,10},{10,8},{9,1... | collective-permute-start | bytes 430088 | tf_op jit(solution)/shard_map/ppermute | solution.py:197
  49.6 10.1 %collective-permute-start.8 = (bf16[160,384]{1,0:T(8,128)(2,1)S(1)}, bf16[160,384]{1,0:T(8,128)(2,1)S(1)}, u32[]{:S(2)}, u32[]{:S(2)}) collective-permute-start(bf16[160,384]{1,0:T(8,128)(2,1)S(1)} %shard_map.112.mine_ref), channel_id=1, source_target_pairs={{0,1},{1,0},{2,3},{3,2},{4,5},{5,4},{6,7},{7,6},{8,9},{9,8},{10,11... | collective-permute-start | bytes 368648 | tf_op jit(solution)/shard_map/ppermute | solution.py:197
  53.3 2.8 %collective-permute-start.18 = (bf16[80,384]{1,0:T(8,128)(2,1)S(1)}, bf16[80,384]{1,0:T(8,128)(2,1)S(1)}, u32[]{:S(2)}, u32[]{:S(2)}) collective-permute-start(bf16[80,384]{1,0:T(8,128)(2,1)S(1)} %shard_map.120.mine_ref), channel_id=1, source_target_pairs={{0,1},{1,0},{2,3},{3,2},{4,5},{5,4},{6,7},{7,6},{8,9},{9,8},{10,11... | collective-permute-start | bytes 184328 | tf_op jit(solution)/shard_map/ppermute | solution.py:197
  56.0 3.3 %collective-permute-start.13 = (bf16[80,384]{1,0:T(8,128)(2,1)S(1)}, bf16[80,384]{1,0:T(8,128)(2,1)S(1)}, u32[]{:S(2)}, u32[]{:S(2)}) collective-permute-start(bf16[80,384]{1,0:T(8,128)(2,1)S(1)} %shard_map.116.mine_ref), channel_id=1, source_target_pairs={{0,1},{1,0},{2,3},{3,2},{4,5},{5,4},{6,7},{7,6},{8,9},{9,8},{10,11... | collective-permute-start | bytes 184328 | tf_op jit(solution)/shard_map/ppermute | solution.py:197
  56.5 8.3 %copy-start.7 = (s32[128,2]{0,1:T(2,128)S(1)}, s32[128,2]{0,1:T(2,128)}, u32[]{:S(2)}) copy-start(s32[128,2]{0,1:T(2,128)} %param.15) | copy-start | bytes 3076
  56.5 10.3 %collective-permute-start.19 = (bf16[80,1024]{1,0:T(8,128)(2,1)S(1)}, bf16[80,1024]{1,0:T(8,128)(2,1)S(1)}, u32[]{:S(2)}, u32[]{:S(2)}) collective-permute-start(bf16[80,1024]{1,0:T(8,128)(2,1)S(1)} %shard_map.121), channel_id=1, source_target_pairs={{0,12},{4,8},{8,4},{12,0},{1,13},{5,9},{9,5},{13,1},{2,14},{6,10},... | collective-permute-start | bytes 491528 | tf_op jit(solution)/shard_map/ppermute | solution.py:229
  59.7 13.3 %collective-permute-start.14 = (bf16[80,1024]{1,0:T(8,128)(2,1)S(1)}, bf16[80,1024]{1,0:T(8,128)(2,1)S(1)}, u32[]{:S(2)}, u32[]{:S(2)}) collective-permute-start(bf16[80,1024]{1,0:T(8,128)(2,1)S(1)} %shard_map.117), channel_id=1, source_target_pairs={{0,8},{4,12},{8,0},{12,4},{1,9},{5,13},{9,1},{13,5},{2,10},{6,14},... | collective-permute-start | bytes 491528 | tf_op jit(solution)/shard_map/ppermute | solution.py:229
  60.3 12.7 %collective-permute-start.9 = (bf16[80,1024]{1,0:T(8,128)(2,1)S(1)}, bf16[80,1024]{1,0:T(8,128)(2,1)S(1)}, u32[]{:S(2)}, u32[]{:S(2)}) collective-permute-start(bf16[80,1024]{1,0:T(8,128)(2,1)S(1)} %get-tuple-element.34), channel_id=1, source_target_pairs={{0,4},{4,0},{8,12},{12,8},{1,5},{5,1},{9,13},{13,9},{2,6},{6,2},{1... | collective-permute-start | bytes 491528 | tf_op jit(solution)/shard_map/ppermute | solution.py:229
  62.1 1.2 %collective-permute-start.3 = (f32[8,128]{1,0:T(8,128)S(1)}, f32[8,128]{1,0:T(8,128)S(1)}, u32[]{:S(2)}, u32[]{:S(2)}) collective-permute-start(f32[8,128]{1,0:T(8,128)S(1)} %get-tuple-element.26), channel_id=1, source_target_pairs={{0,1},{1,0},{2,3},{3,2},{4,5},{5,4},{6,7},{7,6},{8,9},{9,8},{10,11... | collective-permute-start | bytes 12296 | tf_op jit(solution)/shard_map/ppermute | solution.py:197
  63.2 3.6 %collective-permute-start.4 = (f32[8,128]{1,0:T(8,128)S(1)}, f32[8,128]{1,0:T(8,128)S(1)}, u32[]{:S(2)}, u32[]{:S(2)}) collective-permute-start(f32[8,128]{1,0:T(8,128)S(1)} %add.18), channel_id=1, source_target_pairs={{0,2},{2,0},{1,3},{3,1},{4,6},{6,4},{5,7},{7,5},{8,10},{10,8},{9,1... | collective-permute-start | bytes 12296 | tf_op jit(solution)/shard_map/ppermute | solution.py:197
  (4 other events, 4.7 us)

commit v2 on v0

v2 whole, which is shorter than its diff:
```python
import functools
import math

import jax
import jax.numpy as jnp
from jax import lax
from jax.experimental import pallas as pl
from jax.experimental.pallas import tpu as pltpu
from jax.sharding import PartitionSpec as P

HEAD_SIZE = 128
LANES = 128
EPSILON = 1e-06
HIDDEN_MASK = -1e30
VMEM_LIMIT = 16 * 1024 * 1024

F32 = jnp.float32
BF16 = jnp.bfloat16
NT = (((1,), (1,)), ((), ()))


def dot(a, b):
    return jnp.dot(a, b, preferred_element_type=F32)


def dot_nt(a, b):
    return lax.dot_general(a, b, NT, preferred_element_type=F32)


def vmem_call(body, out_shape, scalars, arrays, after=(), scratch=(), remote=(), held=True):
    multi = isinstance(out_shape, (tuple, list))
    n_out = len(out_shape) if multi else 1
    n_given = len(scalars) + len(remote) + len(arrays)
    whole = pl.BlockSpec(memory_space=pltpu.VMEM)
    anywhere = pl.BlockSpec(memory_space=pl.ANY)

    def placed(x):
        return pltpu.VMEM(x.shape, x.dtype) if held else x

    def kernel(*refs):
        body(*refs[:n_given], *refs[n_given + len(after) :])

    kernel.__name__ = getattr(body, "func", body).__name__
    return pl.pallas_call(
        kernel,
        out_shape=[placed(x) for x in out_shape] if multi else placed(out_shape),
        in_specs=[pl.BlockSpec(memory_space=pltpu.SMEM)] * len(scalars)
        + [pl.BlockSpec(memory_space=pltpu.HBM)] * len(remote)
        + [whole] * len(arrays)
        + [anywhere] * len(after),
        out_specs=[whole] * n_out if multi else whole,
        scratch_shapes=list(scratch),
        compiler_params=pltpu.CompilerParams(vmem_limit_bytes=VMEM_LIMIT),
        cost_estimate=pl.CostEstimate(flops=1, bytes_accessed=1, transcendentals=0),
    )(
        *scalars,
        *[pltpu.with_memory_space_constraint(x, pltpu.HBM) for x in remote],
        *[pltpu.with_memory_space_constraint(x, pltpu.VMEM) for x in arrays],
        *after,
    )


def carry(copies):
    for copy in copies:
        copy.start()
    for copy in copies:
        copy.wait()


def prepare_kernel(experts, head_ref, rep_ref, key_in, value_in, q_in, stream_in, gain_in, router_in, ids_in, home_in, *rest):
    part_ref, key_ref, value_ref, q_ref, stream_ref, gain_ref, router_ref, ids_ref, target_ref = rest[:9]
    home_ref, sems = rest[9:]
    columns = pl.ds(pl.multiple_of(head_ref[0] * HEAD_SIZE, HEAD_SIZE), HEAD_SIZE)
    pairs = [
        (key_in.at[:, columns], key_ref),
        (value_in.at[:, columns], value_ref),
        (ids_in, ids_ref),
        (home_in, home_ref),
        (gain_in, gain_ref),
        (router_in, router_ref),
        (q_in, q_ref),
        (stream_in, stream_ref),
    ]
    carry([pltpu.make_async_copy(a, b, sems.at[i]) for i, (a, b) in enumerate(pairs)])
    ids = ids_ref[...]
    target = jnp.zeros(ids.shape, jnp.int32)
    for expert in range(experts):
        target = jnp.where(ids == expert, home_ref[0:1, expert : expert + 1], target)
    target_ref[...] = target

    @pl.when(rep_ref[0] == 0)
    def _():
        part_ref[...] = key_ref[...]

    @pl.when(rep_ref[0] == 1)
    def _():
        part_ref[...] = value_ref[...]


def attend_kernel(n, cap, place_ref, rep_ref, gate_in, up_in, down_in, q_ref, stream_ref, gain_ref, router_ref, target_ref, key_ref, value_ref, *rest):
    mine, theirs, rest = rest[: n - 1], rest[n - 1 : 2 * n - 2], rest[2 * n - 2 :]
    (hidden_ref, stats_ref), row_refs, weight_refs, (k_all, v_all, gained, sems) = (
        rest[:2],
        rest[2 : n + 2],
        rest[n + 2 : n + 5],
        rest[n + 5 :],
    )
    pairs = zip((gate_in, up_in, down_in), weight_refs)
    copies = [pltpu.make_async_copy(a, b, sems.at[i]) for i, (a, b) in enumerate(pairs)]
    for copy in copies:
        copy.start()
    place = place_ref[0]
    tokens = q_ref.shape[0]
    heads = q_ref.shape[1] // HEAD_SIZE
    row = lax.broadcasted_iota(jnp.int32, (tokens, tokens), 0)
    col = lax.broadcasted_iota(jnp.int32, (tokens, tokens), 1)
    pieces = [jnp.where(row >= col, 0.0, HIDDEN_MASK)]
    k_all[:tokens, :] = key_ref[...]
    v_all[:tokens, :] = value_ref[...]
    for i in range(n - 1):
        rows = slice((i + 1) * tokens, (i + 2) * tokens)
        seen = jnp.where(jnp.bitwise_xor(place, i + 1) < place, 0.0, HIDDEN_MASK)
        pieces.append(jnp.full((tokens, tokens), seen, F32))

        @pl.when(rep_ref[0] == 0)
        def _():
            k_all[rows, :] = mine[i][...]
            v_all[rows, :] = theirs[i][...]

        @pl.when(rep_ref[0] == 1)
        def _():
            k_all[rows, :] = theirs[i][...]
            v_all[rows, :] = mine[i][...]

    bias = jnp.concatenate(pieces, axis=1)
    squares = jnp.zeros((tokens, 1), F32)
    for head in range(heads):
        cols = slice(head * HEAD_SIZE, (head + 1) * HEAD_SIZE)
        scores = dot_nt(q_ref[:, cols], k_all[...]) * (1.0 / math.sqrt(HEAD_SIZE)) + bias
        expo = jnp.exp(scores - jnp.max(scores, axis=-1, keepdims=True))
        total = jnp.sum(expo, axis=-1, keepdims=True)
        attended = dot(expo.astype(BF16), v_all[...]) / total
        hidden = stream_ref[:, cols].astype(F32) + attended
        hidden_ref[:, cols] = hidden
        squares = squares + jnp.sum(hidden * hidden, axis=-1, keepdims=True)
        gained[:, cols] = (hidden * gain_ref[head : head + 1, :].astype(F32)).astype(BF16)
    values = gained[...]
    earlier = (row < col).astype(F32).astype(BF16)
    slot = lax.broadcasted_iota(jnp.int32, (cap, tokens), 0)
    for j in range(n):
        member = jnp.sum((target_ref[...] == jnp.bitwise_xor(place, j)).astype(F32), axis=0, keepdims=True)
        rank = dot(jnp.broadcast_to(member, (8, tokens)).astype(BF16), earlier)[0:1, :]
        rank = jnp.where(member > 0.5, rank, -1.0).astype(jnp.int32)
        placing = (slot == rank).astype(F32).astype(BF16)
        row_refs[j][...] = dot(placing, values).astype(BF16)
    squares_row = jnp.transpose(jnp.broadcast_to(squares, (tokens, LANES)))
    height = stats_ref.shape[0]
    stats_ref[...] = jnp.concatenate(
        [dot_nt(router_ref[...], values), squares_row[: height - router_ref.shape[0], :]], axis=0
    )
    for copy in copies:
        copy.wait()


def split_pair(x):
    high = x.astype(BF16).astype(F32)
    lane = lax.broadcasted_iota(jnp.int32, x.shape, 1)
    return jnp.where(lane < LANES // 2, high, x - high).astype(BF16)


def join_pair(ref, rows, start):
    return jnp.sum(ref[rows, start:].astype(F32), axis=-1, keepdims=True) * (2.0 / LANES)


def put_stats(ref, base, stats):
    height, tokens = stats.shape
    ref[base:, :] = jnp.zeros((ref.shape[0] - base, ref.shape[1]), BF16)
    terms = []
    for i in range(3):
        term = stats.astype(BF16)
        stats = stats - term.astype(F32)
        terms.append(term.astype(F32))
    pad = jnp.zeros((ref.shape[0] - base - height, 3 * tokens), F32)
    ref[base:, : 3 * tokens] = jnp.concatenate(
        [jnp.concatenate(terms, axis=1), pad], axis=0
    ).astype(BF16)


def get_stats(ref, base, like):
    height, tokens = like.shape
    parts = ref[base:, : 3 * tokens].astype(F32)[:height]
    return parts[:, :tokens] + parts[:, tokens : 2 * tokens] + parts[:, 2 * tokens :]


def up_kernel(with_stats, rep_ref, gate_ref, up_ref, gain_ref, *rest):
    rows_ref, keep_ref, first_ref, second_ref = rest[-4:]
    count = rows_ref.shape[0]
    half = gate_ref.shape[1] // 2
    mine = pl.multiple_of(rep_ref[0] * half, LANES)
    other = pl.multiple_of((1 - rep_ref[0]) * half, LANES)
    rows = rows_ref[...]
    squares = jnp.zeros((count, LANES), F32)
    for i in range(gain_ref.shape[0]):
        plain = rows[:, i * LANES : (i + 1) * LANES].astype(F32) / gain_ref[i : i + 1, :].astype(F32)
        squares = squares + plain * plain
    squares = jnp.broadcast_to(jnp.sum(squares, axis=-1, keepdims=True), (count, LANES))
    first_ref[...] = dot(rows, gate_ref[:, pl.ds(other, half)]).astype(BF16)
    second_ref[:count, :half] = dot(rows, up_ref[:, pl.ds(other, half)]).astype(BF16)
    second_ref[:count, half:] = split_pair(squares)
    keep_ref[:, :half] = dot(rows, gate_ref[:, pl.ds(mine, half)])
    keep_ref[:, half : 2 * half] = dot(rows, up_ref[:, pl.ds(mine, half)])
    keep_ref[:, 2 * half :] = squares
    if with_stats:
        put_stats(second_ref, count, rest[0][...])


def add_kernel(with_stats, *refs):
    keep_ref, first_ref, second_ref, sum_ref, send_ref = refs[with_stats : with_stats + 5]
    count = keep_ref.shape[0]
    wide = keep_ref.shape[1] - LANES
    half = first_ref.shape[1]
    for start, ref in ((0, first_ref), (half, second_ref)):
        both = keep_ref[:, start : start + half] + ref[:count, :half].astype(F32)
        sum_ref[:, start : start + half] = both
        send_ref[:count, start : start + half] = both.astype(BF16)
    squares = keep_ref[:, wide:] + join_pair(second_ref, slice(0, count), half)
    sum_ref[:, wide:] = squares
    send_ref[:count, wide:] = split_pair(squares)
    if with_stats:
        stats_ref, total_ref = refs[0], refs[-1]
        stats = stats_ref[...] + get_stats(second_ref, count, stats_ref)
        total_ref[...] = stats
        put_stats(send_ref, count, stats)


def inner_kernel(features, with_stats, *refs):
    sum_ref, got_ref, inner_ref = refs[with_stats : with_stats + 3]
    count = sum_ref.shape[0]
    wide = sum_ref.shape[1] - LANES
    half = wide // 2
    squares = sum_ref[:, wide : wide + 1] + join_pair(got_ref, slice(0, count), wide)
    scale = lax.rsqrt(squares * (1.0 / features) + EPSILON)
    gate = (sum_ref[:, :half] + got_ref[:count, :half].astype(F32)) * scale
    up = (sum_ref[:, half:wide] + got_ref[:count, half:wide].astype(F32)) * scale
    inner_ref[...] = (gate * jax.nn.sigmoid(gate) * up).astype(BF16)
    if with_stats:
        stats_ref, total_ref = refs[0], refs[-1]
        total_ref[...] = stats_ref[...] + get_stats(got_ref, count, stats_ref)


def down_kernel(rep_ref, down_ref, mine_ref, other_ref, out_ref):
    half = mine_ref.shape[1]
    mine = pl.multiple_of(rep_ref[0] * half, LANES)
    other = pl.multiple_of((1 - rep_ref[0]) * half, LANES)
    out_ref[...] = (
        dot(mine_ref[...], down_ref[pl.ds(mine, half), :])
        + dot(other_ref[...], down_ref[pl.ds(other, half), :])
    ).astype(BF16)


def gates_kernel(cap, features, place_ref, stats_ref, ids_ref, target_ref, *weight_refs):
    place = place_ref[0]
    top, tokens = ids_ref.shape
    stats = jnp.transpose(stats_ref[...])
    height = stats.shape[1]
    scale = lax.rsqrt(stats[:, height - 1 :] * (1.0 / features) + EPSILON)
    logits = stats * scale
    both = jnp.concatenate(
        [ids_ref[...], target_ref[...], jnp.zeros((8 - 2 * top, tokens), jnp.int32)], axis=0
    )
    both = jnp.transpose(both.astype(F32)).astype(jnp.int32)
    kinds = lax.broadcasted_iota(jnp.int32, stats.shape, 1)
    squashed = [
        jax.nn.sigmoid(
            jnp.sum(jnp.where(kinds == both[:, k : k + 1], logits, 0.0), axis=-1, keepdims=True)
        )
        for k in range(top)
    ]
    whole = functools.reduce(lambda a, b: a + b, squashed)
    blocks = jnp.bitwise_xor(lax.broadcasted_iota(jnp.int32, (tokens, LANES), 1), place)
    named = [both[:, top + k : top + k + 1] == blocks for k in range(top)]
    member = functools.reduce(lambda a, b: a + b, [x.astype(F32) for x in named])
    later = (
        lax.broadcasted_iota(jnp.int32, (tokens, tokens), 0)
        > lax.broadcasted_iota(jnp.int32, (tokens, tokens), 1)
    ).astype(F32).astype(BF16)
    rank = dot(later, member.astype(BF16))
    slot = lax.broadcasted_iota(jnp.int32, (tokens, cap), 1)
    for j, weights_ref in enumerate(weight_refs):
        weights = jnp.zeros((tokens, cap), F32)
        for k in range(top):
            at = jnp.where(named[k][:, j : j + 1], rank[:, j : j + 1], -1.0).astype(jnp.int32)
            weights = weights + jnp.where(slot == at, squashed[k] / whole, 0.0)
        high = weights.astype(BF16)
        weights_ref[:tokens, :] = high
        weights_ref[tokens:, :] = (weights - high.astype(F32)).astype(BF16)


def mix_kernel(count, partial_ref, *rest):
    weights, answers, out_ref = rest[:count], rest[count : 2 * count], rest[-1]
    tokens = partial_ref.shape[0]
    total = partial_ref[...]
    for weights_ref, answer_ref in zip(weights, answers):
        mixed = dot(weights_ref[...], answer_ref[...])
        total = total + (mixed[:tokens] + mixed[tokens:])
    out_ref[...] = total.astype(out_ref.dtype)


def swap(x, axis):
    return lax.ppermute(x, axis, [(0, 1), (1, 0)])


def direct(
    stream,
    query_proj,
    key_proj,
    value_projected,
    expert_ids,
    expert_home,
    router,
    norm_gain,
    w_gate,
    w_up,
    w_down,
):
    tokens, width = stream.shape
    top = expert_ids.shape[1]
    n = lax.axis_size("ctx")
    features = width * lax.axis_size(("section", "rep"))
    experts = router.shape[1]
    hid = w_gate.shape[2]
    wide = hid + LANES
    cap = capacity_of(tokens, top, n)
    where = lax.axis_index("ctx").astype(jnp.int32).reshape(1)
    side = lax.axis_index("rep").astype(jnp.int32).reshape(1)
    heads = width // HEAD_SIZE
    group_width = features // key_proj.shape[1]
    kv_head = (lax.axis_index(("section", "rep")) * heads // group_width).astype(jnp.int32).reshape(1)

    def exchange(x, j):
        return lax.ppermute(x, "ctx", [(i, i ^ j) for i in range(n)])

    def like(x):
        return jax.ShapeDtypeStruct(x.shape, x.dtype)

    gain = norm_gain.reshape(width // LANES, LANES)
    part, own_key, own_value, queries, stream, gain, router_rows, ids_rows, target = vmem_call(
        functools.partial(prepare_kernel, experts),
        [jax.ShapeDtypeStruct((tokens, HEAD_SIZE), BF16)] * 3
        + [like(x) for x in (query_proj, stream, gain, router.T)]
        + [jax.ShapeDtypeStruct((top, tokens), jnp.int32)] * 2,
        [kv_head, side],
        [],
        remote=[key_proj, value_projected, query_proj, stream, gain, router.T, expert_ids.T]
        + [expert_home.reshape(1, experts)],
        scratch=[pltpu.VMEM((1, experts), jnp.int32), pltpu.SemaphoreType.DMA((8,))],
    )
    distance = sorted(range(1, n), key=lambda j: (j < n // 2, j))
    mine = {j: exchange(part, j) for j in distance}
    theirs = {j: swap(mine[j], "rep") for j in distance}
    stat_rows = -(-(experts + 1) // 8) * 8

    weights = [w_gate[0], w_up[0], w_down[0]]
    hidden, stats, *rows = vmem_call(
        functools.partial(attend_kernel, n, cap),
        [
            jax.ShapeDtypeStruct((tokens, width), F32),
            jax.ShapeDtypeStruct((stat_rows, tokens), F32),
        ]
        + [jax.ShapeDtypeStruct((cap, width), BF16)] * n
        + [like(x) for x in weights],
        [where, side],
        [queries, stream, gain, router_rows, target, own_key, own_value]
        + [kept[j] for kept in (mine, theirs) for j in range(1, n)],
        remote=weights,
        scratch=[
            pltpu.VMEM((n * tokens, HEAD_SIZE), BF16),
            pltpu.VMEM((n * tokens, HEAD_SIZE), BF16),
            pltpu.VMEM((tokens, width), BF16),
            pltpu.SemaphoreType.DMA((3,)),
        ],
    )
    rows, (gate, up, down) = rows[:n], rows[n:]
    arrived = {j: exchange(rows[j], j) for j in distance}
    arrived[0] = rows[0]

    extra = -(-stat_rows // 16) * 16
    state = {}
    made = {"last": hidden, "stats": stats, "partial": hidden}

    def run(body, out_shape, scalars, arrays, held=True):
        outs = vmem_call(body, out_shape, scalars, arrays, after=[made["last"]], held=held)
        made["last"] = outs[0] if isinstance(outs, (tuple, list)) else outs
        return outs

    def stat_part(j):
        return (1, [made["stats"]], [like(stats)], extra) if j == 1 else (0, [], [], 0)

    def up_step(j):
        flag, given, made_too, more = stat_part(j)
        keep, first, second = run(
            functools.partial(up_kernel, flag),
            [
                jax.ShapeDtypeStruct((cap, wide), F32),
                jax.ShapeDtypeStruct((cap, hid // 2), BF16),
                jax.ShapeDtypeStruct((cap + more, hid // 2 + LANES), BF16),
            ],
            [side],
            [gate, up, gain] + given + [arrived[j]],
        )
        state[j] = (keep, swap(first, "rep"), swap(second, "rep"))

    def add_step(j):
        flag, given, made_too, more = stat_part(j)
        both, send, *rest = run(
            functools.partial(add_kernel, flag),
            [jax.ShapeDtypeStruct((cap, wide), F32), jax.ShapeDtypeStruct((cap + more, wide), BF16)]
            + made_too,
            [],
            given + list(state[j]),
        )
        if rest:
            made["stats"] = rest[0]
        state[j] = (both, swap(send, "section"))

    def inner_step(j):
        flag, given, made_too, more = stat_part(j)
        inner, *rest = run(
            functools.partial(inner_kernel, features, flag),
            [jax.ShapeDtypeStruct((cap, hid // 2), BF16)] + made_too,
            [],
            given + list(state[j]),
        )
        if rest:
            made["stats"] = rest[0]
        state[j] = (inner, swap(inner, "rep"))

    def down_step(j):
        answer = run(down_kernel, jax.ShapeDtypeStruct((cap, width), BF16), [side], [down, *state[j]])
        state[j] = exchange(answer, j) if j else answer

    def gates_step():
        made["weights"] = run(
            functools.partial(gates_kernel, cap, features),
            [jax.ShapeDtypeStruct((2 * tokens, cap), BF16)] * n,
            [where],
            [made["stats"], ids_rows, target],
        )

    def mix_step(blocks, dtype=F32, held=True):
        made["partial"] = run(
            functools.partial(mix_kernel, len(blocks)),
            jax.ShapeDtypeStruct((tokens, width), dtype),
            [],
            [made["partial"]] + [made["weights"][j] for j in blocks] + [state[j] for j in blocks],
            held=held,
        )

    steps = dict(u=up_step, a=add_step, i=inner_step, d=down_step, m=lambda j: mix_step([j]))
    chain = [0] + [distance[0], *distance[:0:-1]]
    plan = (
        *("u0", "a0", "u1", "u2", "i0", "a1", "a2", "u3", "i1", "d0", "d1"),
        *("a3", "i2", "g", "d2", "m0", "i3", "m1", "d3"),
    )
    for name in plan:
        if name == "g":
            gates_step()
        elif int(name[1]) < n - (name[0] == "m"):
            steps[name[0]](chain[int(name[1])])
    mix_step(chain[2:] if n > 2 else chain[1:], BF16, held=False)
    return made["partial"]


def capacity_of(tokens, top, n):
    return min(tokens, max(2, 5 * tokens * top // (4 * n)))


def score_update(running, query_matrix, query_pos, key_block, value_block, key_anchor):
    run_max, run_sum, run_acc = running
    key_len = key_block.shape[0]
    scores = jnp.einsum(
        "tha,pa->htp", query_matrix, key_block, preferred_element_type=jnp.float32
    ) * (1.0 / math.sqrt(HEAD_SIZE))
    key_pos = key_anchor + jnp.arange(key_len, dtype=jnp.int32)
    visible = query_pos[:, None] >= key_pos[None, :]
    scores = jnp.where(visible, scores, HIDDEN_MASK)
    new_max = jnp.maximum(run_max, jnp.max(scores, axis=-1))
    expo = jnp.where(visible, jnp.exp(scores - new_max[..., None]), 0.0)
    factor = jnp.exp(run_max - new_max)
    new_sum = run_sum * factor + jnp.sum(expo, axis=-1)
    weights = expo.astype(jnp.bfloat16)
    new_acc = run_acc * factor[..., None] + jnp.einsum(
        "htp,pa->hta", weights, value_block, preferred_element_type=jnp.float32
    )
    return (new_max, new_sum, new_acc)


def absorb_rows(running, query_matrix, query_pos, key_rows, value_rows, anchor):
    piece_len = key_rows.shape[0]
    if piece_len > 512 and piece_len % 512 == 0:
        blocks = piece_len // 512
        key_tiles = key_rows.reshape(blocks, 512, key_rows.shape[1])
        value_tiles = value_rows.reshape(blocks, 512, value_rows.shape[1])
        anchors = anchor + 512 * jnp.arange(blocks, dtype=jnp.int32)

        def advance(state_now, tile):
            return (
                score_update(state_now, query_matrix, query_pos, tile[0], tile[1], tile[2]),
                None,
            )

        running, ignored = lax.scan(advance, running, (key_tiles, value_tiles, anchors))
        return running
    return score_update(running, query_matrix, query_pos, key_rows, value_rows, anchor)


def general(
    stream,
    query_proj,
    key_proj,
    value_projected,
    expert_ids,
    expert_home,
    router,
    norm_gain,
    w_gate,
    w_up,
    w_down,
):
    tok_rows, local_width = stream.shape
    top_count = expert_ids.shape[1]
    columns = lax.axis_size("ctx")
    features = local_width * lax.axis_size(("section", "rep"))
    capacity = capacity_of(tok_rows, top_count, columns)
    place = lax.axis_index("ctx")
    feature_index = lax.axis_index(("section", "rep"))
    heads_dev = local_width // HEAD_SIZE
    group_width = features // key_proj.shape[1]
    kv_head = feature_index * heads_dev // group_width
    query_matrix = query_proj.reshape(tok_rows, heads_dev, HEAD_SIZE)
    query_pos = place * tok_rows + jnp.arange(tok_rows, dtype=jnp.int32)
    initial = (
        jnp.full((heads_dev, tok_rows), HIDDEN_MASK, jnp.float32),
        jnp.zeros((heads_dev, tok_rows), jnp.float32),
        jnp.zeros((heads_dev, tok_rows, HEAD_SIZE), jnp.float32),
    )
    key_single = lax.dynamic_slice_in_dim(key_proj, kv_head * HEAD_SIZE, HEAD_SIZE, 1)
    value_single = lax.dynamic_slice_in_dim(value_projected, kv_head * HEAD_SIZE, HEAD_SIZE, 1)
    run_max, run_sum, run_acc = absorb_rows(
        initial,
        query_matrix,
        query_pos,
        lax.all_gather(key_single, "ctx", axis=0, tiled=True),
        lax.all_gather(value_single, "ctx", axis=0, tiled=True),
        jnp.int32(0),
    )
    attended = jnp.transpose(run_acc / run_sum[..., None], (1, 0, 2)).reshape(tok_rows, local_width)
    hidden = stream.astype(jnp.float32) + attended
    total_sq = lax.psum(jnp.sum(hidden * hidden, axis=-1), ("section", "rep"))
    scale_rows = lax.rsqrt(total_sq / features + EPSILON)
    normed = (hidden * scale_rows[:, None] * norm_gain.astype(jnp.float32)[None, :]).astype(
        jnp.bfloat16
    )
    logits = lax.psum(dot(normed, router), ("section", "rep"))
    experts_all = logits.shape[1]
    one_hot = expert_ids[:, :, None] == jnp.arange(experts_all, dtype=jnp.int32)[None, None, :]
    picked = jnp.sum(jnp.where(one_hot, logits[:, None, :], 0.0), axis=-1)
    squashed = jax.nn.sigmoid(picked)
    gates = squashed / jnp.sum(squashed, axis=-1, keepdims=True)
    target = jnp.sum(jnp.where(one_hot, expert_home[None, None, :], 0), axis=-1)
    named = target[:, :, None] == jnp.arange(columns, dtype=jnp.int32)[None, None, :]
    member = jnp.any(named, axis=1).astype(jnp.bfloat16)
    before = jnp.tril(jnp.ones((tok_rows, tok_rows), jnp.bfloat16), -1)
    rank = dot(before, member).astype(jnp.int32)
    rank = jnp.sum(jnp.where(named, rank[:, None, :], 0), axis=-1)
    slot_index = (target * capacity + rank).reshape(-1)
    placing = slot_index[None, :] == jnp.arange(columns * capacity, dtype=jnp.int32)[:, None]
    placing = jnp.any(placing.reshape(columns * capacity, tok_rows, top_count), axis=-1).astype(
        jnp.bfloat16
    )
    outgoing = dot(placing, normed).astype(jnp.bfloat16)
    outgoing = outgoing.reshape(columns, capacity, local_width)
    received = lax.all_to_all(outgoing, "ctx", split_axis=0, concat_axis=0, tiled=True)
    flat_rows = received.reshape(-1, local_width)
    gate_part = dot(flat_rows, w_gate[0])
    up_part = dot(flat_rows, w_up[0])
    gate_full = lax.psum(gate_part.astype(jnp.bfloat16), ("section", "rep")).astype(jnp.float32)
    up_full = lax.psum(up_part.astype(jnp.bfloat16), ("section", "rep")).astype(jnp.float32)
    inner = (jax.nn.silu(gate_full) * up_full).astype(jnp.bfloat16)
    answer = dot(inner, w_down[0]).astype(jnp.bfloat16)
    returned = lax.all_to_all(
        answer.reshape(received.shape), "ctx", split_axis=0, concat_axis=0, tiled=True
    )
    flat_back = returned.reshape(columns * capacity, local_width)
    picked_rows = flat_back[slot_index].reshape(tok_rows, top_count, local_width)
    mixed = jnp.sum(gates[:, :, None] * picked_rows.astype(jnp.float32), axis=1)
    return (hidden + mixed).astype(jnp.bfloat16)


def solution(mesh):
    size = dict(mesh.shape)
    pairs = size["section"] == 2 and size["rep"] == 2
    short = size["ctx"] in (2, 4)
    placed = (
        P(("group", "ctx"), ("section", "rep")),
        P(("group", "ctx"), ("section", "rep")),
        P(("group", "ctx"), None),
        P(("group", "ctx"), None),
        P(("group", "ctx"), None),
        P(),
        P(("section", "rep"), None),
        P(("section", "rep")),
        P("ctx", ("section", "rep"), None),
        P("ctx", ("section", "rep"), None),
        P("ctx", None, ("section", "rep")),
    )
    return jax.shard_map(
        direct if pairs and short else general,
        mesh=mesh,
        in_specs=placed,
        out_specs=P(("group", "ctx"), ("section", "rep")),
        check_vma=False,
    )
```

time: 146 us -> 60.2 us (0.41)
  blocking collectives: 60 us -> 0 us
  waiting for transfers between devices: 45 us -> 24.7 us
  starting transfers between devices: 4.59 us -> 22.9 us
  between operations: 13.6 us -> 0.25 us
  Pallas kernels: 0 us -> 12.2 us
  matrix products: 9.95 us -> 0 us
  local copies, waits for them, and re-layouts: 7.34 us -> 0 us
  other arithmetic: 5.41 us -> 0 us
    psum x1 -> x0, waiting for transfers between devices: 35 us -> none  [local(): lax.psum(up_part.astype(jnp.bfloat16), ('section', 'rep'))]
    all_gather x2 -> x0, blocking collectives: 27.3 us -> none  [the longest x1 15 us: local(): lax.all_gather(key_single, 'ctx', axis=0, tiled=True)]
    ppermute x0 -> x28, waiting for transfers between devices: none -> 24.7 us  [the longest x9 20.6 us: exchange(): return lax.ppermute(x, 'ctx', [(i, i ^ j) for i in range(n)])]
    ppermute x0 -> x28, starting transfers between devices: none -> 22.9 us  [the longest x9 14.2 us: exchange(): return lax.ppermute(x, 'ctx', [(i, i ^ j) for i in range(n)])]
    all_to_all x1 -> x0, blocking collectives: 21.1 us -> none  [local(): lax.all_to_all(outgoing, 'ctx', split_axis=0, concat_axis=0, tiled=True)]
    pallas_call x0 -> x22, Pallas kernels: none -> 12.2 us  [vmem_call(): pl.pallas_call(kernel, out_shape=[placed(x) for x in out_shape] if multi...]
    psum x2 -> x0, blocking collectives: 11.6 us -> none  [the longest x1 5.95 us: local(): lax.psum(jnp.dot(normed, router, preferred_element_type=jnp.float32), ('s...]
    dot_general x7 -> x0, matrix products: 9.95 us -> none  [the longest x1 2.83 us: local(): jnp.dot(inner, w_down[0], preferred_element_type=jnp.float32)]
  transfers between devices with their start and end apart: 2 -> 28, of which waited for: 2 -> 15; matrix products, arithmetic and copies ran while one was open for 0% -> 0% of each run, Pallas kernels for 0% -> 11%
where the time goes in v2:
time: 60.2 us; the launch traced here: 60 us
  waiting for transfers between devices  24.7 us (41%)
  starting transfers between devices  22.9 us (38%)
  Pallas kernels  12.2 us (20%)
    ppermute x9, waiting for transfers between devices, exchange(): return lax.ppermute(x, 'ctx', [(i, i ^ j) for i in range(n)])  20.6 us
    ppermute x9, starting transfers between devices, exchange(): return lax.ppermute(x, 'ctx', [(i, i ^ j) for i in range(n)])  14.2 us
    pallas_call x22, Pallas kernels, vmem_call(): pl.pallas_call(kernel, out_shape=[placed(x) for x in out_shape] if multi...  12.2 us
    ppermute x19, starting transfers between devices, swap(): return lax.ppermute(x, axis, [(0, 1), (1, 0)])  8.73 us
    ppermute x19, waiting for transfers between devices, swap(): return lax.ppermute(x, axis, [(0, 1), (1, 0)])  4.08 us
  transfers between devices with their start and end apart: 28, of which 15 were waited for; matrix products, arithmetic and copies ran while one was open for 0% of the time, Pallas kernels for 11%

profile of v2, /device:TPU:0, one launch (start us, length us, event | category | flops | bytes accessed | tf_op | source)
XLA Modules:
  0.0 60.0 jit_solution(16158197342344786944)
XLA Ops:
  0.0 1.3 %shard_map.109 = (bf16[128,128]{1,0:T(8,128)(2,1)S(1)}, bf16[128,128]{1,0:T(8,128)(2,1)S(1)}, bf16[128,128]{1,0:T(8,128)(2,1)S(1)}, bf16[128,1024]{1,0:T(8,128)(...) custom-call(s32[1]{0:T(128)} %bitcast.5.refs_0_, ...), custom_call_target="tpu_custom_call" | custom-call | flops 1 | bytes 1 | tf_op jit(solution)/shard_map/pallas_call | solution.py:44
  1.3 5.1 %collective-permute-start.2 = (bf16[128,128]{1,0:T(8,128)(2,1)S(1)}, bf16[128,128]{1,0:T(8,128)(2,1)S(1)}, u32[]{:S(2)}, u32[]{:S(2)}) collective-permute-start(bf16[128,128]{1,0:T(8,128)(2,1)S(1)} %get-tuple-element.57), channel_id=1, source_target_pairs={{0,12},{4,8},{8,4},{12,0},{1,13},{5,9},{9,5},{13,1},{2,14},{6,10},... | collective-permute-start | bytes 98312 | tf_op jit(solution)/shard_map/ppermute | solution.py:341
  6.4 0.6 %collective-permute-start = (bf16[128,128]{1,0:T(8,128)(2,1)S(1)}, bf16[128,128]{1,0:T(8,128)(2,1)S(1)}, u32[]{:S(2)}, u32[]{:S(2)}) collective-permute-start(bf16[128,128]{1,0:T(8,128)(2,1)S(1)} %get-tuple-element.57), channel_id=1, source_target_pairs={{0,4},{4,0},{8,12},{12,8},{1,5},{5,1},{9,13},{13,9},{2,6},{6,2},{1... | collective-permute-start | bytes 98312 | tf_op jit(solution)/shard_map/ppermute | solution.py:341
  7.0 1.3 %collective-permute-done.2.refs_14_ = bf16[128,128]{1,0:T(8,128)(2,1)S(1)} collective-permute-done((bf16[128,128]{1,0:T(8,128)(2,1)S(1)}, bf16[128,128]{1,0:T(8,128)(2,1)S(1)}, u32[]{:S(2)}, u32[]{:S(2)}) %collective-permute-start.2) | collective-permute-done | bytes 32800 | tf_op jit(solution)/shard_map/ppermute | solution.py:341
  8.3 2.9 %collective-permute-done.1.refs_13_ = bf16[128,128]{1,0:T(8,128)(2,1)S(1)} collective-permute-done((bf16[128,128]{1,0:T(8,128)(2,1)S(1)}, bf16[128,128]{1,0:T(8,128)(2,1)S(1)}, u32[]{:S(2)}, u32[]{:S(2)}) %collective-permute-start.1) | collective-permute-done | bytes 32800 | tf_op jit(solution)/shard_map/ppermute | solution.py:341
  11.7 0.7 %collective-permute-done.4.refs_16_ = bf16[128,128]{1,0:T(8,128)(2,1)S(1)} collective-permute-done((bf16[128,128]{1,0:T(8,128)(2,1)S(1)}, bf16[128,128]{1,0:T(8,128)(2,1)S(1)}, u32[]{:S(2)}, u32[]{:S(2)}) %collective-permute-start.4) | collective-permute-done | bytes 32800 | tf_op jit(solution)/shard_map/ppermute | solution.py:310
  12.6 3.2 %shard_map.110 = (f32[128,1024]{1,0:T(8,128)S(1)}, f32[8,128]{1,0:T(8,128)S(1)}, bf16[80,1024]{1,0:T(8,128)(2,1)S(1)}, bf16[80,1024]{1,0:T(8,128)(2,1)S(1)}, bf1...) custom-call(s32[1]{0:T(128)} %bitcast.refs_0_, ...), custom_call_target="tpu_custom_call" | custom-call | flops 1 | bytes 1 | tf_op jit(solution)/shard_map/pallas_call | solution.py:44
  15.8 1.9 %collective-permute-start.7 = (bf16[80,1024]{1,0:T(8,128)(2,1)S(1)}, bf16[80,1024]{1,0:T(8,128)(2,1)S(1)}, u32[]{:S(2)}, u32[]{:S(2)}) collective-permute-start(bf16[80,1024]{1,0:T(8,128)(2,1)S(1)} %get-tuple-element.63), channel_id=1, source_target_pairs={{0,8},{4,12},{8,0},{12,4},{1,9},{5,13},{9,1},{13,5},{2,10},{6,14},... | collective-permute-start | bytes 491528 | tf_op jit(solution)/shard_map/ppermute | solution.py:341
  18.9 0.9 %collective-permute-done.8.refs_1_ = bf16[80,384]{1,0:T(8,128)(2,1)S(1)} collective-permute-done((bf16[80,384]{1,0:T(8,128)(2,1)S(1)}, bf16[80,384]{1,0:T(8,128)(2,1)S(1)}, u32[]{:S(2)}, u32[]{:S(2)}) %collective-permute-start.8) | collective-permute-done | bytes 61472 | tf_op jit(solution)/shard_map/ppermute | solution.py:310
  19.9 1.6 %collective-permute-start.14 = (bf16[80,896]{1,0:T(8,128)(2,1)S(1)}, bf16[80,896]{1,0:T(8,128)(2,1)S(1)}, u32[]{:S(2)}, u32[]{:S(2)}) collective-permute-start(bf16[80,896]{1,0:T(8,128)(2,1)S(1)} %get-tuple-element.75), channel_id=1, source_target_pairs={{0,2},{2,0},{1,3},{3,1},{4,6},{6,4},{5,7},{7,5},{8,10},{10,8},{9,1... | collective-permute-start | bytes 430088 | tf_op jit(solution)/shard_map/ppermute | solution.py:310
  21.5 4.3 %collective-permute-done.7.refs_4_ = bf16[80,1024]{1,0:T(8,128)(2,1)S(1)} collective-permute-done((bf16[80,1024]{1,0:T(8,128)(2,1)S(1)}, bf16[80,1024]{1,0:T(8,128)(2,1)S(1)}, u32[]{:S(2)}, u32[]{:S(2)}) %collective-permute-start.7) | collective-permute-done | bytes 163872 | tf_op jit(solution)/shard_map/ppermute | solution.py:341
  27.0 2.0 %collective-permute-start.16 = (bf16[80,1024]{1,0:T(8,128)(2,1)S(1)}, bf16[80,1024]{1,0:T(8,128)(2,1)S(1)}, u32[]{:S(2)}, u32[]{:S(2)}) collective-permute-start(bf16[80,1024]{1,0:T(8,128)(2,1)S(1)} %get-tuple-element.80), channel_id=1, source_target_pairs={{0,12},{4,8},{8,4},{12,0},{1,13},{5,9},{9,5},{13,1},{2,14},{6,10},... | collective-permute-start | bytes 491528 | tf_op jit(solution)/shard_map/ppermute | solution.py:341
  30.0 1.5 %collective-permute-start.19 = (bf16[80,896]{1,0:T(8,128)(2,1)S(1)}, bf16[80,896]{1,0:T(8,128)(2,1)S(1)}, u32[]{:S(2)}, u32[]{:S(2)}) collective-permute-start(bf16[80,896]{1,0:T(8,128)(2,1)S(1)} %get-tuple-element.85), channel_id=1, source_target_pairs={{0,2},{2,0},{1,3},{3,1},{4,6},{6,4},{5,7},{7,5},{8,10},{10,8},{9,1... | collective-permute-start | bytes 430088 | tf_op jit(solution)/shard_map/ppermute | solution.py:310
  32.1 0.9 %collective-permute-done.10.refs_2_ = bf16[80,384]{1,0:T(8,128)(2,1)S(1)} collective-permute-done((bf16[80,384]{1,0:T(8,128)(2,1)S(1)}, bf16[80,384]{1,0:T(8,128)(2,1)S(1)}, u32[]{:S(2)}, u32[]{:S(2)}) %collective-permute-start.10) | collective-permute-done | bytes 61472 | tf_op jit(solution)/shard_map/ppermute | solution.py:310
  33.7 1.4 %collective-permute-done.16.refs_4_ = bf16[80,1024]{1,0:T(8,128)(2,1)S(1)} collective-permute-done((bf16[80,1024]{1,0:T(8,128)(2,1)S(1)}, bf16[80,1024]{1,0:T(8,128)(2,1)S(1)}, u32[]{:S(2)}, u32[]{:S(2)}) %collective-permute-start.16) | collective-permute-done | bytes 163872 | tf_op jit(solution)/shard_map/ppermute | solution.py:341
  38.4 1.6 %collective-permute-start.24 = (bf16[80,896]{1,0:T(8,128)(2,1)S(1)}, bf16[80,896]{1,0:T(8,128)(2,1)S(1)}, u32[]{:S(2)}, u32[]{:S(2)}) collective-permute-start(bf16[80,896]{1,0:T(8,128)(2,1)S(1)} %get-tuple-element.92), channel_id=1, source_target_pairs={{0,2},{2,0},{1,3},{3,1},{4,6},{6,4},{5,7},{7,5},{8,10},{10,8},{9,1... | collective-permute-start | bytes 430088 | tf_op jit(solution)/shard_map/ppermute | solution.py:310
  39.9 1.5 %collective-permute-start.23 = (bf16[80,1024]{1,0:T(8,128)(2,1)S(1)}, bf16[80,1024]{1,0:T(8,128)(2,1)S(1)}, u32[]{:S(2)}, u32[]{:S(2)}) collective-permute-start(bf16[80,1024]{1,0:T(8,128)(2,1)S(1)} %shard_map.121.refs_3_), channel_id=1, source_target_pairs={{0,8},{4,12},{8,0},{12,4},{1,9},{5,13},{9,1},{13,5},{2,10},{6,14},... | collective-permute-start | bytes 491528 | tf_op jit(solution)/shard_map/ppermute | solution.py:341
  41.7 0.7 %shard_map.124 = (bf16[256,80]{1,0:T(8,128)(2,1)S(1)}, bf16[256,80]{1,0:T(8,128)(2,1)S(1)}, bf16[256,80]{1,0:T(8,128)(2,1)S(1)}, bf16[256,80]{1,0:T(8,128)(2,1)S(1)}) custom-call(s32[1]{0:T(128)} %bitcast.refs_0_, f32[8,128]{1,0:T(8,128)S(1)} %get-tuple-element.87.refs_1_, s32[2,128]{1,0:T(2,128)S(1)} %get-tuple-element.88.refs_2_, ...), custom_call_target="tpu_custom_call" | custom-call | flops 1 | bytes 1 | tf_op jit(solution)/shard_map/pallas_call | solution.py:44
  44.6 0.9 %collective-permute-start.25 = (bf16[80,1024]{1,0:T(8,128)(2,1)S(1)}, bf16[80,1024]{1,0:T(8,128)(2,1)S(1)}, u32[]{:S(2)}, u32[]{:S(2)}) collective-permute-start(bf16[80,1024]{1,0:T(8,128)(2,1)S(1)} %shard_map.125.refs_3_), channel_id=1, source_target_pairs={{0,4},{4,0},{8,12},{12,8},{1,5},{5,1},{9,13},{13,9},{2,6},{6,2},{1... | collective-permute-start | bytes 491528 | tf_op jit(solution)/shard_map/ppermute | solution.py:341
  45.4 5.0 %collective-permute-done.23.refs_2_ = bf16[80,1024]{1,0:T(8,128)(2,1)S(1)} collective-permute-done((bf16[80,1024]{1,0:T(8,128)(2,1)S(1)}, bf16[80,1024]{1,0:T(8,128)(2,1)S(1)}, u32[]{:S(2)}, u32[]{:S(2)}) %collective-permute-start.23) | collective-permute-done | bytes 163872 | tf_op jit(solution)/shard_map/ppermute | solution.py:341
  51.1 2.1 %collective-permute-start.27 = (bf16[80,1024]{1,0:T(8,128)(2,1)S(1)}, bf16[80,1024]{1,0:T(8,128)(2,1)S(1)}, u32[]{:S(2)}, u32[]{:S(2)}) collective-permute-start(bf16[80,1024]{1,0:T(8,128)(2,1)S(1)} %shard_map.129.refs_5_), channel_id=1, source_target_pairs={{0,12},{4,8},{8,4},{12,0},{1,13},{5,9},{9,5},{13,1},{2,14},{6,10},... | collective-permute-start | bytes 491528 | tf_op jit(solution)/shard_map/ppermute | solution.py:341
  53.2 0.6 %collective-permute-done.25.refs_3_ = bf16[80,1024]{1,0:T(8,128)(2,1)S(1)} collective-permute-done((bf16[80,1024]{1,0:T(8,128)(2,1)S(1)}, bf16[80,1024]{1,0:T(8,128)(2,1)S(1)}, u32[]{:S(2)}, u32[]{:S(2)}) %collective-permute-start.25) | collective-permute-done | bytes 163872 | tf_op jit(solution)/shard_map/ppermute | solution.py:341
  53.9 5.1 %collective-permute-done.27.refs_4_ = bf16[80,1024]{1,0:T(8,128)(2,1)S(1)} collective-permute-done((bf16[80,1024]{1,0:T(8,128)(2,1)S(1)}, bf16[80,1024]{1,0:T(8,128)(2,1)S(1)}, u32[]{:S(2)}, u32[]{:S(2)}) %collective-permute-start.27) | collective-permute-done | bytes 163872 | tf_op jit(solution)/shard_map/ppermute | solution.py:341
  58.9 1.1 %shard_map.130 = bf16[128,1024]{1,0:T(8,128)(2,1)} custom-call(f32[128,1024]{1,0:T(8,128)S(1)} %shard_map.128.refs_4_.refs_0_, bf16[256,80]{1,0:T(8,128)(2,1)S(1)} %get-tuple-element.93.refs_1_, bf16[256,80]{1,0:T(8,128)(2,1)S(1)} %get-tuple-element.94.refs_2_, bf16[80,1024]{1,0:T(8,128)(2,1)S(1)} %collective-permute-done.25.refs_3_, ...), custom_call_target="tpu_custom_call" | custom-call | flops 1 | bytes 1 | tf_op jit(solution)/shard_map/pallas_call | solution.py:44
  (54 shorter events, 11.6 us)
Async XLA Ops:
  1.3 7.0 %collective-permute-start.2 = (bf16[128,128]{1,0:T(8,128)(2,1)S(1)}, bf16[128,128]{1,0:T(8,128)(2,1)S(1)}, u32[]{:S(2)}, u32[]{:S(2)}) collective-permute-start(bf16[128,128]{1,0:T(8,128)(2,1)S(1)} %get-tuple-element.57), channel_id=1, source_target_pairs={{0,12},{4,8},{8,4},{12,0},{1,13},{5,9},{9,5},{13,1},{2,14},{6,10},... | collective-permute-start | bytes 98312 | tf_op jit(solution)/shard_map/ppermute | solution.py:341
  6.4 4.8 %collective-permute-start.1 = (bf16[128,128]{1,0:T(8,128)(2,1)S(1)}, bf16[128,128]{1,0:T(8,128)(2,1)S(1)}, u32[]{:S(2)}, u32[]{:S(2)}) collective-permute-start(bf16[128,128]{1,0:T(8,128)(2,1)S(1)} %get-tuple-element.57), channel_id=1, source_target_pairs={{0,8},{4,12},{8,0},{12,4},{1,9},{5,13},{9,1},{13,5},{2,10},{6,14},... | collective-permute-start | bytes 98312 | tf_op jit(solution)/shard_map/ppermute | solution.py:341
  6.4 4.8 %collective-permute-start = (bf16[128,128]{1,0:T(8,128)(2,1)S(1)}, bf16[128,128]{1,0:T(8,128)(2,1)S(1)}, u32[]{:S(2)}, u32[]{:S(2)}) collective-permute-start(bf16[128,128]{1,0:T(8,128)(2,1)S(1)} %get-tuple-element.57), channel_id=1, source_target_pairs={{0,4},{4,0},{8,12},{12,8},{1,5},{5,1},{9,13},{13,9},{2,6},{6,2},{1... | collective-permute-start | bytes 98312 | tf_op jit(solution)/shard_map/ppermute | solution.py:341
  8.3 3.4 %collective-permute-start.5 = (bf16[128,128]{1,0:T(8,128)(2,1)S(1)}, bf16[128,128]{1,0:T(8,128)(2,1)S(1)}, u32[]{:S(2)}, u32[]{:S(2)}) collective-permute-start(bf16[128,128]{1,0:T(8,128)(2,1)S(1)} %collective-permute-done.2.refs_14_), channel_id=1, source_target_pairs={{0,1},{1,0},{2,3},{3,2},{4,5},{5,4},{6,7},{7,6},{8,9},{9,8},{10,11... | collective-permute-start | bytes 98312 | tf_op jit(solution)/shard_map/ppermute | solution.py:310
  15.8 10.0 %collective-permute-start.7 = (bf16[80,1024]{1,0:T(8,128)(2,1)S(1)}, bf16[80,1024]{1,0:T(8,128)(2,1)S(1)}, u32[]{:S(2)}, u32[]{:S(2)}) collective-permute-start(bf16[80,1024]{1,0:T(8,128)(2,1)S(1)} %get-tuple-element.63), channel_id=1, source_target_pairs={{0,8},{4,12},{8,0},{12,4},{1,9},{5,13},{9,1},{13,5},{2,10},{6,14},... | collective-permute-start | bytes 491528 | tf_op jit(solution)/shard_map/ppermute | solution.py:341
  18.3 1.5 %collective-permute-start.9 = (bf16[80,512]{1,0:T(8,128)(2,1)S(1)}, bf16[80,512]{1,0:T(8,128)(2,1)S(1)}, u32[]{:S(2)}, u32[]{:S(2)}) collective-permute-start(bf16[80,512]{1,0:T(8,128)(2,1)S(1)} %get-tuple-element.67), channel_id=1, source_target_pairs={{0,1},{1,0},{2,3},{3,2},{4,5},{5,4},{6,7},{7,6},{8,9},{9,8},{10,11... | collective-permute-start | bytes 245768 | tf_op jit(solution)/shard_map/ppermute | solution.py:310
  18.4 1.4 %collective-permute-start.8 = (bf16[80,384]{1,0:T(8,128)(2,1)S(1)}, bf16[80,384]{1,0:T(8,128)(2,1)S(1)}, u32[]{:S(2)}, u32[]{:S(2)}) collective-permute-start(bf16[80,384]{1,0:T(8,128)(2,1)S(1)} %get-tuple-element.66), channel_id=1, source_target_pairs={{0,1},{1,0},{2,3},{3,2},{4,5},{5,4},{6,7},{7,6},{8,9},{9,8},{10,11... | collective-permute-start | bytes 184328 | tf_op jit(solution)/shard_map/ppermute | solution.py:310
  18.9 10.1 %collective-permute-start.6 = (bf16[80,1024]{1,0:T(8,128)(2,1)S(1)}, bf16[80,1024]{1,0:T(8,128)(2,1)S(1)}, u32[]{:S(2)}, u32[]{:S(2)}) collective-permute-start(bf16[80,1024]{1,0:T(8,128)(2,1)S(1)} %get-tuple-element.62), channel_id=1, source_target_pairs={{0,4},{4,0},{8,12},{12,8},{1,5},{5,1},{9,13},{13,9},{2,6},{6,2},{1... | collective-permute-start | bytes 491528 | tf_op jit(solution)/shard_map/ppermute | solution.py:341
  19.9 9.7 %collective-permute-start.14 = (bf16[80,896]{1,0:T(8,128)(2,1)S(1)}, bf16[80,896]{1,0:T(8,128)(2,1)S(1)}, u32[]{:S(2)}, u32[]{:S(2)}) collective-permute-start(bf16[80,896]{1,0:T(8,128)(2,1)S(1)} %get-tuple-element.75), channel_id=1, source_target_pairs={{0,2},{2,0},{1,3},{3,1},{4,6},{6,4},{5,7},{7,5},{8,10},{10,8},{9,1... | collective-permute-start | bytes 430088 | tf_op jit(solution)/shard_map/ppermute | solution.py:310
  26.4 3.5 %collective-permute-start.13 = (bf16[80,512]{1,0:T(8,128)(2,1)S(1)}, bf16[80,512]{1,0:T(8,128)(2,1)S(1)}, u32[]{:S(2)}, u32[]{:S(2)}) collective-permute-start(bf16[80,512]{1,0:T(8,128)(2,1)S(1)} %get-tuple-element.74), channel_id=1, source_target_pairs={{0,1},{1,0},{2,3},{3,2},{4,5},{5,4},{6,7},{7,6},{8,9},{9,8},{10,11... | collective-permute-start | bytes 245768 | tf_op jit(solution)/shard_map/ppermute | solution.py:310
  26.5 3.4 %collective-permute-start.12 = (bf16[80,384]{1,0:T(8,128)(2,1)S(1)}, bf16[80,384]{1,0:T(8,128)(2,1)S(1)}, u32[]{:S(2)}, u32[]{:S(2)}) collective-permute-start(bf16[80,384]{1,0:T(8,128)(2,1)S(1)} %get-tuple-element.73), channel_id=1, source_target_pairs={{0,1},{1,0},{2,3},{3,2},{4,5},{5,4},{6,7},{7,6},{8,9},{9,8},{10,11... | collective-permute-start | bytes 184328 | tf_op jit(solution)/shard_map/ppermute | solution.py:310
  27.0 8.1 %collective-permute-start.16 = (bf16[80,1024]{1,0:T(8,128)(2,1)S(1)}, bf16[80,1024]{1,0:T(8,128)(2,1)S(1)}, u32[]{:S(2)}, u32[]{:S(2)}) collective-permute-start(bf16[80,1024]{1,0:T(8,128)(2,1)S(1)} %get-tuple-element.80), channel_id=1, source_target_pairs={{0,12},{4,8},{8,4},{12,0},{1,13},{5,9},{9,5},{13,1},{2,14},{6,10},... | collective-permute-start | bytes 491528 | tf_op jit(solution)/shard_map/ppermute | solution.py:341
  30.0 6.3 %collective-permute-start.19 = (bf16[80,896]{1,0:T(8,128)(2,1)S(1)}, bf16[80,896]{1,0:T(8,128)(2,1)S(1)}, u32[]{:S(2)}, u32[]{:S(2)}) collective-permute-start(bf16[80,896]{1,0:T(8,128)(2,1)S(1)} %get-tuple-element.85), channel_id=1, source_target_pairs={{0,2},{2,0},{1,3},{3,1},{4,6},{6,4},{5,7},{7,5},{8,10},{10,8},{9,1... | collective-permute-start | bytes 430088 | tf_op jit(solution)/shard_map/ppermute | solution.py:310
  31.6 1.4 %collective-permute-start.11 = (bf16[96,512]{1,0:T(8,128)(2,1)S(1)}, bf16[96,512]{1,0:T(8,128)(2,1)S(1)}, u32[]{:S(2)}, u32[]{:S(2)}) collective-permute-start(bf16[96,512]{1,0:T(8,128)(2,1)S(1)} %get-tuple-element.72), channel_id=1, source_target_pairs={{0,1},{1,0},{2,3},{3,2},{4,5},{5,4},{6,7},{7,6},{8,9},{9,8},{10,11... | collective-permute-start | bytes 294920 | tf_op jit(solution)/shard_map/ppermute | solution.py:310
  31.6 1.4 %collective-permute-start.10 = (bf16[80,384]{1,0:T(8,128)(2,1)S(1)}, bf16[80,384]{1,0:T(8,128)(2,1)S(1)}, u32[]{:S(2)}, u32[]{:S(2)}) collective-permute-start(bf16[80,384]{1,0:T(8,128)(2,1)S(1)} %get-tuple-element.71), channel_id=1, source_target_pairs={{0,1},{1,0},{2,3},{3,2},{4,5},{5,4},{6,7},{7,6},{8,9},{9,8},{10,11... | collective-permute-start | bytes 184328 | tf_op jit(solution)/shard_map/ppermute | solution.py:310
  33.1 8.3 %collective-permute-start.15 = (bf16[96,896]{1,0:T(8,128)(2,1)S(1)}, bf16[96,896]{1,0:T(8,128)(2,1)S(1)}, u32[]{:S(2)}, u32[]{:S(2)}) collective-permute-start(bf16[96,896]{1,0:T(8,128)(2,1)S(1)} %get-tuple-element.79), channel_id=1, source_target_pairs={{0,2},{2,0},{1,3},{3,1},{4,6},{6,4},{5,7},{7,5},{8,10},{10,8},{9,1... | collective-permute-start | bytes 516104 | tf_op jit(solution)/shard_map/ppermute | solution.py:310
  35.7 2.5 %collective-permute-start.18 = (bf16[80,512]{1,0:T(8,128)(2,1)S(1)}, bf16[80,512]{1,0:T(8,128)(2,1)S(1)}, u32[]{:S(2)}, u32[]{:S(2)}) collective-permute-start(bf16[80,512]{1,0:T(8,128)(2,1)S(1)} %get-tuple-element.83), channel_id=1, source_target_pairs={{0,1},{1,0},{2,3},{3,2},{4,5},{5,4},{6,7},{7,6},{8,9},{9,8},{10,11... | collective-permute-start | bytes 245768 | tf_op jit(solution)/shard_map/ppermute | solution.py:310
  35.8 1.4 %collective-permute-start.21 = (bf16[80,384]{1,0:T(8,128)(2,1)S(1)}, bf16[80,384]{1,0:T(8,128)(2,1)S(1)}, u32[]{:S(2)}, u32[]{:S(2)}) collective-permute-start(bf16[80,384]{1,0:T(8,128)(2,1)S(1)} %shard_map.115.refs_3_.refs_2_), channel_id=1, source_target_pairs={{0,1},{1,0},{2,3},{3,2},{4,5},{5,4},{6,7},{7,6},{8,9},{9,8},{10,11... | collective-permute-start | bytes 184328 | tf_op jit(solution)/shard_map/ppermute | solution.py:310
  36.6 1.6 %collective-permute-start.17 = (bf16[80,384]{1,0:T(8,128)(2,1)S(1)}, bf16[80,384]{1,0:T(8,128)(2,1)S(1)}, u32[]{:S(2)}, u32[]{:S(2)}) collective-permute-start(bf16[80,384]{1,0:T(8,128)(2,1)S(1)} %get-tuple-element.82), channel_id=1, source_target_pairs={{0,1},{1,0},{2,3},{3,2},{4,5},{5,4},{6,7},{7,6},{8,9},{9,8},{10,11... | collective-permute-start | bytes 184328 | tf_op jit(solution)/shard_map/ppermute | solution.py:310
  38.4 5.9 %collective-permute-start.24 = (bf16[80,896]{1,0:T(8,128)(2,1)S(1)}, bf16[80,896]{1,0:T(8,128)(2,1)S(1)}, u32[]{:S(2)}, u32[]{:S(2)}) collective-permute-start(bf16[80,896]{1,0:T(8,128)(2,1)S(1)} %get-tuple-element.92), channel_id=1, source_target_pairs={{0,2},{2,0},{1,3},{3,1},{4,6},{6,4},{5,7},{7,5},{8,10},{10,8},{9,1... | collective-permute-start | bytes 430088 | tf_op jit(solution)/shard_map/ppermute | solution.py:310
  39.9 10.5 %collective-permute-start.23 = (bf16[80,1024]{1,0:T(8,128)(2,1)S(1)}, bf16[80,1024]{1,0:T(8,128)(2,1)S(1)}, u32[]{:S(2)}, u32[]{:S(2)}) collective-permute-start(bf16[80,1024]{1,0:T(8,128)(2,1)S(1)} %shard_map.121.refs_3_), channel_id=1, source_target_pairs={{0,8},{4,12},{8,0},{12,4},{1,9},{5,13},{9,1},{13,5},{2,10},{6,14},... | collective-permute-start | bytes 491528 | tf_op jit(solution)/shard_map/ppermute | solution.py:341
  44.5 6.2 %collective-permute-start.26 = (bf16[80,384]{1,0:T(8,128)(2,1)S(1)}, bf16[80,384]{1,0:T(8,128)(2,1)S(1)}, u32[]{:S(2)}, u32[]{:S(2)}) collective-permute-start(bf16[80,384]{1,0:T(8,128)(2,1)S(1)} %shard_map.127.refs_3_.refs_2_), channel_id=1, source_target_pairs={{0,1},{1,0},{2,3},{3,2},{4,5},{5,4},{6,7},{7,6},{8,9},{9,8},{10,11... | collective-permute-start | bytes 184328 | tf_op jit(solution)/shard_map/ppermute | solution.py:310
  44.6 9.3 %collective-permute-start.25 = (bf16[80,1024]{1,0:T(8,128)(2,1)S(1)}, bf16[80,1024]{1,0:T(8,128)(2,1)S(1)}, u32[]{:S(2)}, u32[]{:S(2)}) collective-permute-start(bf16[80,1024]{1,0:T(8,128)(2,1)S(1)} %shard_map.125.refs_3_), channel_id=1, source_target_pairs={{0,4},{4,0},{8,12},{12,8},{1,5},{5,1},{9,13},{13,9},{2,6},{6,2},{1... | collective-permute-start | bytes 491528 | tf_op jit(solution)/shard_map/ppermute | solution.py:341
  51.1 7.8 %collective-permute-start.27 = (bf16[80,1024]{1,0:T(8,128)(2,1)S(1)}, bf16[80,1024]{1,0:T(8,128)(2,1)S(1)}, u32[]{:S(2)}, u32[]{:S(2)}) collective-permute-start(bf16[80,1024]{1,0:T(8,128)(2,1)S(1)} %shard_map.129.refs_5_), channel_id=1, source_target_pairs={{0,12},{4,8},{8,4},{12,0},{1,13},{5,9},{9,5},{13,1},{2,14},{6,10},... | collective-permute-start | bytes 491528 | tf_op jit(solution)/shard_map/ppermute | solution.py:341
  (4 other events, 5.2 us)

commit v3 on v2

--- a/solution.py
+++ b/solution.py
@@ -67,38 +67,42 @@
         copy.wait()
 
 
-def prepare_kernel(experts, head_ref, rep_ref, key_in, value_in, q_in, stream_in, gain_in, router_in, ids_in, home_in, *rest):
-    part_ref, key_ref, value_ref, q_ref, stream_ref, gain_ref, router_ref, ids_ref, target_ref = rest[:9]
-    home_ref, sems = rest[9:]
+def prepare_kernel(head_ref, rep_ref, key_in, value_in, kv_ref, part_ref, sems):
     columns = pl.ds(pl.multiple_of(head_ref[0] * HEAD_SIZE, HEAD_SIZE), HEAD_SIZE)
-    pairs = [
-        (key_in.at[:, columns], key_ref),
-        (value_in.at[:, columns], value_ref),
-        (ids_in, ids_ref),
-        (home_in, home_ref),
-        (gain_in, gain_ref),
-        (router_in, router_ref),
-        (q_in, q_ref),
-        (stream_in, stream_ref),
-    ]
+    carry(
+        [
+            pltpu.make_async_copy(
+                ref.at[:, columns], kv_ref.at[:, pl.ds(i * HEAD_SIZE, HEAD_SIZE)], sems.at[i]
+            )
+            for i, ref in enumerate((key_in, value_in))
+        ]
+    )
+    for i in range(2):
+
+        @pl.when(rep_ref[0] == i)
+        def _():
+            part_ref[...] = kv_ref[:, i * HEAD_SIZE : (i + 1) * HEAD_SIZE]
+
+
+def fetch_kernel(experts, *refs):
+    count = (len(refs) - 4) // 2
+    sources, home_in, targets, (target_ref, home_ref, sems) = (
+        refs[:count],
+        refs[count],
+        refs[count + 1 : 2 * count + 1],
+        refs[2 * count + 1 :],
+    )
+    pairs = [(home_in, home_ref), *zip(sources, targets)]
     carry([pltpu.make_async_copy(a, b, sems.at[i]) for i, (a, b) in enumerate(pairs)])
-    ids = ids_ref[...]
+    ids = targets[-1][...]
     target = jnp.zeros(ids.shape, jnp.int32)
     for expert in range(experts):
         target = jnp.where(ids == expert, home_ref[0:1, expert : expert + 1], target)
     target_ref[...] = target
 
-    @pl.when(rep_ref[0] == 0)
-    def _():
-        part_ref[...] = key_ref[...]
-
-    @pl.when(rep_ref[0] == 1)
-    def _():
-        part_ref[...] = value_ref[...]
-
-
-def attend_kernel(n, cap, place_ref, rep_ref, gate_in, up_in, down_in, q_ref, stream_ref, gain_ref, router_ref, target_ref, key_ref, value_ref, *rest):
-    mine, theirs, rest = rest[: n - 1], rest[n - 1 : 2 * n - 2], rest[2 * n - 2 :]
+
+def attend_kernel(n, cap, place_ref, rep_ref, gate_in, up_in, down_in, q_ref, stream_ref, gain_ref, router_ref, target_ref, kv_ref, *rest):
+    (near_mine, near_theirs, far_mine, far_theirs), rest = rest[:4], rest[4:]
     (hidden_ref, stats_ref), row_refs, weight_refs, (k_all, v_all, gained, sems) = (
         rest[:2],
         rest[2 : n + 2],
@@ -115,28 +119,37 @@
     row = lax.broadcasted_iota(jnp.int32, (tokens, tokens), 0)
     col = lax.broadcasted_iota(jnp.int32, (tokens, tokens), 1)
     pieces = [jnp.where(row >= col, 0.0, HIDDEN_MASK)]
-    k_all[:tokens, :] = key_ref[...]
-    v_all[:tokens, :] = value_ref[...]
-    for i in range(n - 1):
-        rows = slice((i + 1) * tokens, (i + 2) * tokens)
-        seen = jnp.where(jnp.bitwise_xor(place, i + 1) < place, 0.0, HIDDEN_MASK)
-        pieces.append(jnp.full((tokens, tokens), seen, F32))
-
-        @pl.when(rep_ref[0] == 0)
-        def _():
-            k_all[rows, :] = mine[i][...]
-            v_all[rows, :] = theirs[i][...]
-
-        @pl.when(rep_ref[0] == 1)
-        def _():
-            k_all[rows, :] = theirs[i][...]
-            v_all[rows, :] = mine[i][...]
+    rep = rep_ref[0]
+    for block, (ref, offset) in enumerate(
+        ((kv_ref, 0), (None, 1), (far_mine, 2 + rep), (far_theirs, 3 - rep))
+    ):
+        rows = slice(block * tokens, (block + 1) * tokens)
+        if ref is not None:
+            k_all[rows, :] = ref[:, :HEAD_SIZE]
+            v_all[rows, :] = ref[:, HEAD_SIZE:]
+        if block:
+            seen = jnp.where(jnp.bitwise_xor(place, offset) < place, 0.0, HIDDEN_MASK)
+            pieces.append(jnp.full((tokens, tokens), seen, F32))
+
+    @pl.when(rep == 0)
+    def _():
+        k_all[tokens : 2 * tokens, :] = near_mine[...]
+        v_all[tokens : 2 * tokens, :] = near_theirs[...]
+
+    @pl.when(rep == 1)
+    def _():
+        k_all[tokens : 2 * tokens, :] = near_theirs[...]
+        v_all[tokens : 2 * tokens, :] = near_mine[...]
 
     bias = jnp.concatenate(pieces, axis=1)
+    stacked = jnp.concatenate(
+        [q_ref[:, h * HEAD_SIZE : (h + 1) * HEAD_SIZE] for h in range(heads)], axis=0
+    )
+    scored = dot_nt(stacked, k_all[...])
     squares = jnp.zeros((tokens, 1), F32)
     for head in range(heads):
         cols = slice(head * HEAD_SIZE, (head + 1) * HEAD_SIZE)
-        scores = dot_nt(q_ref[:, cols], k_all[...]) * (1.0 / math.sqrt(HEAD_SIZE)) + bias
+        scores = scored[head * tokens : (head + 1) * tokens, :] * (1.0 / math.sqrt(HEAD_SIZE)) + bias
         expo = jnp.exp(scores - jnp.max(scores, axis=-1, keepdims=True))
         total = jnp.sum(expo, axis=-1, keepdims=True)
         attended = dot(expo.astype(BF16), v_all[...]) / total
@@ -343,21 +356,29 @@
     def like(x):
         return jax.ShapeDtypeStruct(x.shape, x.dtype)
 
-    gain = norm_gain.reshape(width // LANES, LANES)
-    part, own_key, own_value, queries, stream, gain, router_rows, ids_rows, target = vmem_call(
-        functools.partial(prepare_kernel, experts),
-        [jax.ShapeDtypeStruct((tokens, HEAD_SIZE), BF16)] * 3
-        + [like(x) for x in (query_proj, stream, gain, router.T)]
-        + [jax.ShapeDtypeStruct((top, tokens), jnp.int32)] * 2,
+    own_kv, part = vmem_call(
+        prepare_kernel,
+        [jax.ShapeDtypeStruct((tokens, w * HEAD_SIZE), BF16) for w in (2, 1)],
         [kv_head, side],
         [],
-        remote=[key_proj, value_projected, query_proj, stream, gain, router.T, expert_ids.T]
-        + [expert_home.reshape(1, experts)],
-        scratch=[pltpu.VMEM((1, experts), jnp.int32), pltpu.SemaphoreType.DMA((8,))],
+        remote=[key_proj, value_projected],
+        scratch=[pltpu.SemaphoreType.DMA((2,))],
+    )
+    sources = [query_proj, stream, norm_gain.reshape(width // LANES, LANES), router.T, expert_ids.T]
+    queries, stream, gain, router_rows, ids_rows, target = vmem_call(
+        functools.partial(fetch_kernel, experts),
+        [like(x) for x in sources] + [jax.ShapeDtypeStruct((top, tokens), jnp.int32)],
+        [],
+        [],
+        remote=[*sources, expert_home.reshape(1, experts)],
+        after=[part],
+        scratch=[pltpu.VMEM((1, experts), jnp.int32), pltpu.SemaphoreType.DMA((6,))],
     )
     distance = sorted(range(1, n), key=lambda j: (j < n // 2, j))
-    mine = {j: exchange(part, j) for j in distance}
-    theirs = {j: swap(mine[j], "rep") for j in distance}
+    near_kv = exchange(part, 1)
+    far_kv = lax.ppermute(
+        own_kv, ("ctx", "rep"), [(2 * i + r, 2 * (i ^ (2 + r)) + r) for i in range(n) for r in range(2)]
+    )
     stat_rows = -(-(experts + 1) // 8) * 8
 
     weights = [w_gate[0], w_up[0], w_down[0]]
@@ -370,8 +391,8 @@
         + [jax.ShapeDtypeStruct((cap, width), BF16)] * n
         + [like(x) for x in weights],
         [where, side],
-        [queries, stream, gain, router_rows, target, own_key, own_value]
-        + [kept[j] for kept in (mine, theirs) for j in range(1, n)],
+        [queries, stream, gain, router_rows, target, own_kv, near_kv, swap(near_kv, "rep")]
+        + [far_kv, swap(far_kv, "rep")],
         remote=weights,
         scratch=[
             pltpu.VMEM((n * tokens, HEAD_SIZE), BF16),
@@ -467,7 +488,8 @@
             gates_step()
         elif int(name[1]) < n - (name[0] == "m"):
             steps[name[0]](chain[int(name[1])])
-    mix_step(chain[2:] if n > 2 else chain[1:], BF16, held=False)
+    early = [chain[int(name[1])] for name in plan if name[0] == "m" and int(name[1]) < n - 1]
+    mix_step([j for j in chain if j not in early], BF16, held=False)
     return made["partial"]
 
 
@@ -600,7 +622,7 @@
 def solution(mesh):
     size = dict(mesh.shape)
     pairs = size["section"] == 2 and size["rep"] == 2
-    short = size["ctx"] in (2, 4)
+    short = size["ctx"] == 4
     placed = (
         P(("group", "ctx"), ("section", "rep")),
         P(("group", "ctx"), ("section", "rep")),

time: 60.2 us -> 58.1 us (0.965)
  waiting for transfers between devices: 24.7 us -> 21.1 us
  starting transfers between devices: 22.9 us -> 24.4 us
    ppermute x9 -> x7, waiting for transfers between devices: 20.6 us -> 15.4 us  [exchange(): return lax.ppermute(x, 'ctx', [(i, i ^ j) for i in range(n)])]
    ppermute x0 -> x1, starting transfers between devices: none -> 4.1 us  [direct(): lax.ppermute(own_kv, ('ctx', 'rep'), [(2 * i + r, 2 * (i ^ 2 + r) + r) fo...]
    ppermute x9 -> x7, starting transfers between devices: 14.2 us -> 11.5 us  [exchange(): return lax.ppermute(x, 'ctx', [(i, i ^ j) for i in range(n)])]
    ppermute x0 -> x1, waiting for transfers between devices: none -> 2.19 us  [direct(): lax.ppermute(own_kv, ('ctx', 'rep'), [(2 * i + r, 2 * (i ^ 2 + r) + r) fo...]
    ppermute x19 -> x18, waiting for transfers between devices: 4.08 us -> 3.47 us  [swap(): return lax.ppermute(x, axis, [(0, 1), (1, 0)])]
    pallas_call x22 -> x23, Pallas kernels: 12.2 us -> 12.1 us  [vmem_call(): pl.pallas_call(kernel, out_shape=[placed(x) for x in out_shape] if multi...]
    ppermute x19 -> x18, starting transfers between devices: 8.73 us -> 8.83 us  [swap(): return lax.ppermute(x, axis, [(0, 1), (1, 0)])]
  transfers between devices with their start and end apart: 28 -> 26, of which waited for: 15 -> 13; matrix products, arithmetic and copies ran while one was open for 0% -> 0% of each run, Pallas kernels for 11% -> 13%
where the time goes in v3:
time: 58.1 us; the launch traced here: 57.9 us
  starting transfers between devices  24.4 us (42%)
  waiting for transfers between devices  21.1 us (36%)
  Pallas kernels  12.1 us (21%)
    ppermute x7, waiting for transfers between devices, exchange(): return lax.ppermute(x, 'ctx', [(i, i ^ j) for i in range(n)])  15.4 us
    pallas_call x23, Pallas kernels, vmem_call(): pl.pallas_call(kernel, out_shape=[placed(x) for x in out_shape] if multi...  12.1 us
    ppermute x7, starting transfers between devices, exchange(): return lax.ppermute(x, 'ctx', [(i, i ^ j) for i in range(n)])  11.5 us
    ppermute x18, starting transfers between devices, swap(): return lax.ppermute(x, axis, [(0, 1), (1, 0)])  8.83 us
    ppermute x1, starting transfers between devices, direct(): lax.ppermute(own_kv, ('ctx', 'rep'), [(2 * i + r, 2 * (i ^ 2 + r) + r) fo...  4.1 us
    ppermute x18, waiting for transfers between devices, swap(): return lax.ppermute(x, axis, [(0, 1), (1, 0)])  3.47 us
    ppermute x1, waiting for transfers between devices, direct(): lax.ppermute(own_kv, ('ctx', 'rep'), [(2 * i + r, 2 * (i ^ 2 + r) + r) fo...  2.19 us
  transfers between devices with their start and end apart: 26, of which 13 were waited for; matrix products, arithmetic and copies ran while one was open for 0% of the time, Pallas kernels for 13%

profile of v3, /device:TPU:0, one launch (start us, length us, event | category | flops | bytes accessed | tf_op | source)
XLA Modules:
  0.0 57.9 jit_solution(17407921866144845267)
XLA Ops:
  0.0 0.8 %shard_map.109 = (bf16[128,256]{1,0:T(8,128)(2,1)S(1)}, bf16[128,128]{1,0:T(8,128)(2,1)S(1)}) custom-call(s32[1]{0:T(128)} %bitcast.9.refs_0_, s32[1]{0:T(128)} %bitcast.1.refs_1_.refs_0_, bf16[128,256]{1,0:T(8,128)(2,1)} %refs_2_.1, bf16[128,256]{1,0:T(8,128)(2,1)} %refs_3_.1), custom_call_target="tpu_custom_call" | custom-call | flops 1 | bytes 1 | tf_op jit(solution)/shard_map/pallas_call | solution.py:44
  0.8 4.1 %collective-permute-start.2 = (bf16[128,256]{1,0:T(8,128)(2,1)S(1)}, bf16[128,256]{1,0:T(8,128)(2,1)S(1)}, u32[]{:S(2)}, u32[]{:S(2)}) collective-permute-start(bf16[128,256]{1,0:T(8,128)(2,1)S(1)} %get-tuple-element.55.refs_10_), channel_id=1, source_target_pairs={{0,8},{1,13},{4,12},{5,9},{8,0},{9,5},{12,4},{13,1},{2,10},{3,15},... | collective-permute-start | bytes 196616 | tf_op jit(solution)/shard_map/ppermute | solution.py:379
  4.9 1.6 %collective-permute-start = (bf16[128,128]{1,0:T(8,128)(2,1)S(1)}, bf16[128,128]{1,0:T(8,128)(2,1)S(1)}, u32[]{:S(2)}, u32[]{:S(2)}) collective-permute-start(bf16[128,128]{1,0:T(8,128)(2,1)S(1)} %get-tuple-element.49.refs_6_), channel_id=1, source_target_pairs={{0,4},{4,0},{8,12},{12,8},{1,5},{5,1},{9,13},{13,9},{2,6},{6,2},{1... | collective-permute-start | bytes 98312 | tf_op jit(solution)/shard_map/ppermute | solution.py:354
  6.5 2.2 %collective-permute-done.2.refs_13_ = bf16[128,256]{1,0:T(8,128)(2,1)S(1)} collective-permute-done((bf16[128,256]{1,0:T(8,128)(2,1)S(1)}, bf16[128,256]{1,0:T(8,128)(2,1)S(1)}, u32[]{:S(2)}, u32[]{:S(2)}) %collective-permute-start.2) | collective-permute-done | bytes 65568 | tf_op jit(solution)/shard_map/ppermute | solution.py:379
  9.2 1.2 %shard_map.110 = (bf16[128,1024]{1,0:T(8,128)(2,1)S(1)}, bf16[128,1024]{1,0:T(8,128)(2,1)S(1)}, bf16[8,128]{1,0:T(8,128)(2,1)S(1)}, bf16[4,1024]{1,0:T(4,128)(2,...) custom-call(bf16[128,1024]{1,0:T(8,128)(2,1)} %refs_0_.1, bf16[128,1024]{1,0:T(8,128)(2,1)} %refs_1_.1, ...), custom_call_target="tpu_custom_call" | custom-call | flops 1 | bytes 1 | tf_op jit(solution)/shard_map/pallas_call | solution.py:44
  10.4 2.4 %shard_map.111 = (f32[128,1024]{1,0:T(8,128)S(1)}, f32[8,128]{1,0:T(8,128)S(1)}, bf16[80,1024]{1,0:T(8,128)(2,1)S(1)}, bf16[80,1024]{1,0:T(8,128)(2,1)S(1)}, bf1...) custom-call(s32[1]{0:T(128)} %bitcast.refs_0_, ...), custom_call_target="tpu_custom_call" | custom-call | flops 1 | bytes 1 | tf_op jit(solution)/shard_map/pallas_call | solution.py:44
  12.8 2.2 %collective-permute-start.5 = (bf16[80,1024]{1,0:T(8,128)(2,1)S(1)}, bf16[80,1024]{1,0:T(8,128)(2,1)S(1)}, u32[]{:S(2)}, u32[]{:S(2)}) collective-permute-start(bf16[80,1024]{1,0:T(8,128)(2,1)S(1)} %get-tuple-element.61), channel_id=1, source_target_pairs={{0,8},{4,12},{8,0},{12,4},{1,9},{5,13},{9,1},{13,5},{2,10},{6,14},... | collective-permute-start | bytes 491528 | tf_op jit(solution)/shard_map/ppermute | solution.py:354
  15.0 0.6 %shard_map.112 = (f32[80,896]{1,0:T(8,128)S(1)}, bf16[80,384]{1,0:T(8,128)(2,1)S(1)}, bf16[80,512]{1,0:T(8,128)(2,1)S(1)}) custom-call(s32[1]{0:T(128)} %bitcast.1.refs_1_.refs_0_, bf16[1024,768]{1,0:T(8,128)(2,1)S(1)} %get-tuple-element.58.refs_1_, bf16[1024,768]{1,0:T(8,128)(2,1)S(1)} %get-tuple-element.59.refs_2_, ...), custom_call_target="tpu_custom_call" | custom-call | flops 1 | bytes 1 | tf_op jit(solution)/shard_map/pallas_call | solution.py:44
  16.2 2.0 %collective-permute-start.4 = (bf16[80,1024]{1,0:T(8,128)(2,1)S(1)}, bf16[80,1024]{1,0:T(8,128)(2,1)S(1)}, u32[]{:S(2)}, u32[]{:S(2)}) collective-permute-start(bf16[80,1024]{1,0:T(8,128)(2,1)S(1)} %get-tuple-element.60), channel_id=1, source_target_pairs={{0,4},{4,0},{8,12},{12,8},{1,5},{5,1},{9,13},{13,9},{2,6},{6,2},{1... | collective-permute-start | bytes 491528 | tf_op jit(solution)/shard_map/ppermute | solution.py:354
  18.3 1.6 %collective-permute-start.12 = (bf16[80,896]{1,0:T(8,128)(2,1)S(1)}, bf16[80,896]{1,0:T(8,128)(2,1)S(1)}, u32[]{:S(2)}, u32[]{:S(2)}) collective-permute-start(bf16[80,896]{1,0:T(8,128)(2,1)S(1)} %get-tuple-element.73), channel_id=1, source_target_pairs={{0,2},{2,0},{1,3},{3,1},{4,6},{6,4},{5,7},{7,5},{8,10},{10,8},{9,1... | collective-permute-start | bytes 430088 | tf_op jit(solution)/shard_map/ppermute | solution.py:323
  19.9 3.8 %collective-permute-done.5.refs_4_ = bf16[80,1024]{1,0:T(8,128)(2,1)S(1)} collective-permute-done((bf16[80,1024]{1,0:T(8,128)(2,1)S(1)}, bf16[80,1024]{1,0:T(8,128)(2,1)S(1)}, u32[]{:S(2)}, u32[]{:S(2)}) %collective-permute-start.5) | collective-permute-done | bytes 163872 | tf_op jit(solution)/shard_map/ppermute | solution.py:354
  24.9 2.8 %collective-permute-start.14 = (bf16[80,1024]{1,0:T(8,128)(2,1)S(1)}, bf16[80,1024]{1,0:T(8,128)(2,1)S(1)}, u32[]{:S(2)}, u32[]{:S(2)}) collective-permute-start(bf16[80,1024]{1,0:T(8,128)(2,1)S(1)} %get-tuple-element.78), channel_id=1, source_target_pairs={{0,12},{4,8},{8,4},{12,0},{1,13},{5,9},{9,5},{13,1},{2,14},{6,10},... | collective-permute-start | bytes 491528 | tf_op jit(solution)/shard_map/ppermute | solution.py:354
  28.7 1.6 %collective-permute-start.17 = (bf16[80,896]{1,0:T(8,128)(2,1)S(1)}, bf16[80,896]{1,0:T(8,128)(2,1)S(1)}, u32[]{:S(2)}, u32[]{:S(2)}) collective-permute-start(bf16[80,896]{1,0:T(8,128)(2,1)S(1)} %get-tuple-element.83), channel_id=1, source_target_pairs={{0,2},{2,0},{1,3},{3,1},{4,6},{6,4},{5,7},{7,5},{8,10},{10,8},{9,1... | collective-permute-start | bytes 430088 | tf_op jit(solution)/shard_map/ppermute | solution.py:323
  30.7 0.9 %collective-permute-done.8.refs_2_ = bf16[80,384]{1,0:T(8,128)(2,1)S(1)} collective-permute-done((bf16[80,384]{1,0:T(8,128)(2,1)S(1)}, bf16[80,384]{1,0:T(8,128)(2,1)S(1)}, u32[]{:S(2)}, u32[]{:S(2)}) %collective-permute-start.8) | collective-permute-done | bytes 61472 | tf_op jit(solution)/shard_map/ppermute | solution.py:323
  32.3 0.6 %collective-permute-done.14.refs_4_ = bf16[80,1024]{1,0:T(8,128)(2,1)S(1)} collective-permute-done((bf16[80,1024]{1,0:T(8,128)(2,1)S(1)}, bf16[80,1024]{1,0:T(8,128)(2,1)S(1)}, u32[]{:S(2)}, u32[]{:S(2)}) %collective-permute-start.14) | collective-permute-done | bytes 163872 | tf_op jit(solution)/shard_map/ppermute | solution.py:354
  36.3 1.9 %collective-permute-start.22 = (bf16[80,896]{1,0:T(8,128)(2,1)S(1)}, bf16[80,896]{1,0:T(8,128)(2,1)S(1)}, u32[]{:S(2)}, u32[]{:S(2)}) collective-permute-start(bf16[80,896]{1,0:T(8,128)(2,1)S(1)} %get-tuple-element.90), channel_id=1, source_target_pairs={{0,2},{2,0},{1,3},{3,1},{4,6},{6,4},{5,7},{7,5},{8,10},{10,8},{9,1... | collective-permute-start | bytes 430088 | tf_op jit(solution)/shard_map/ppermute | solution.py:323
  38.7 0.7 %shard_map.125 = (bf16[256,80]{1,0:T(8,128)(2,1)S(1)}, bf16[256,80]{1,0:T(8,128)(2,1)S(1)}, bf16[256,80]{1,0:T(8,128)(2,1)S(1)}, bf16[256,80]{1,0:T(8,128)(2,1)S(1)}) custom-call(s32[1]{0:T(128)} %bitcast.refs_0_, f32[8,128]{1,0:T(8,128)S(1)} %get-tuple-element.85.refs_1_, s32[2,128]{1,0:T(2,128)S(1)} %get-tuple-element.86.refs_2_, ...), custom_call_target="tpu_custom_call" | custom-call | flops 1 | bytes 1 | tf_op jit(solution)/shard_map/pallas_call | solution.py:44
  40.6 1.6 %collective-permute-done.22.refs_1_ = bf16[80,896]{1,0:T(8,128)(2,1)S(1)} collective-permute-done((bf16[80,896]{1,0:T(8,128)(2,1)S(1)}, bf16[80,896]{1,0:T(8,128)(2,1)S(1)}, u32[]{:S(2)}, u32[]{:S(2)}) %collective-permute-start.22) | collective-permute-done | bytes 143392 | tf_op jit(solution)/shard_map/ppermute | solution.py:323
  42.5 1.5 %collective-permute-start.23 = (bf16[80,1024]{1,0:T(8,128)(2,1)S(1)}, bf16[80,1024]{1,0:T(8,128)(2,1)S(1)}, u32[]{:S(2)}, u32[]{:S(2)}) collective-permute-start(bf16[80,1024]{1,0:T(8,128)(2,1)S(1)} %shard_map.126.refs_3_), channel_id=1, source_target_pairs={{0,4},{4,0},{8,12},{12,8},{1,5},{5,1},{9,13},{13,9},{2,6},{6,2},{1... | collective-permute-start | bytes 491528 | tf_op jit(solution)/shard_map/ppermute | solution.py:354
  44.0 4.6 %collective-permute-done.21.refs_2_ = bf16[80,1024]{1,0:T(8,128)(2,1)S(1)} collective-permute-done((bf16[80,1024]{1,0:T(8,128)(2,1)S(1)}, bf16[80,1024]{1,0:T(8,128)(2,1)S(1)}, u32[]{:S(2)}, u32[]{:S(2)}) %collective-permute-start.21) | collective-permute-done | bytes 163872 | tf_op jit(solution)/shard_map/ppermute | solution.py:354
  49.4 1.2 %collective-permute-start.25 = (bf16[80,1024]{1,0:T(8,128)(2,1)S(1)}, bf16[80,1024]{1,0:T(8,128)(2,1)S(1)}, u32[]{:S(2)}, u32[]{:S(2)}) collective-permute-start(bf16[80,1024]{1,0:T(8,128)(2,1)S(1)} %shard_map.130.refs_5_), channel_id=1, source_target_pairs={{0,12},{4,8},{8,4},{12,0},{1,13},{5,9},{9,5},{13,1},{2,14},{6,10},... | collective-permute-start | bytes 491528 | tf_op jit(solution)/shard_map/ppermute | solution.py:354
  50.6 1.3 %collective-permute-done.23.refs_3_ = bf16[80,1024]{1,0:T(8,128)(2,1)S(1)} collective-permute-done((bf16[80,1024]{1,0:T(8,128)(2,1)S(1)}, bf16[80,1024]{1,0:T(8,128)(2,1)S(1)}, u32[]{:S(2)}, u32[]{:S(2)}) %collective-permute-start.23) | collective-permute-done | bytes 163872 | tf_op jit(solution)/shard_map/ppermute | solution.py:354
  51.9 4.8 %collective-permute-done.25.refs_4_ = bf16[80,1024]{1,0:T(8,128)(2,1)S(1)} collective-permute-done((bf16[80,1024]{1,0:T(8,128)(2,1)S(1)}, bf16[80,1024]{1,0:T(8,128)(2,1)S(1)}, u32[]{:S(2)}, u32[]{:S(2)}) %collective-permute-start.25) | collective-permute-done | bytes 163872 | tf_op jit(solution)/shard_map/ppermute | solution.py:354
  56.8 1.1 %shard_map.131 = bf16[128,1024]{1,0:T(8,128)(2,1)} custom-call(f32[128,1024]{1,0:T(8,128)S(1)} %shard_map.129.refs_4_.refs_0_, bf16[256,80]{1,0:T(8,128)(2,1)S(1)} %get-tuple-element.91.refs_1_, bf16[256,80]{1,0:T(8,128)(2,1)S(1)} %get-tuple-element.92.refs_2_, bf16[80,1024]{1,0:T(8,128)(2,1)S(1)} %collective-permute-done.23.refs_3_, ...), custom_call_target="tpu_custom_call" | custom-call | flops 1 | bytes 1 | tf_op jit(solution)/shard_map/pallas_call | solution.py:44
  (51 shorter events, 10.5 us)
Async XLA Ops:
  0.8 7.9 %collective-permute-start.2 = (bf16[128,256]{1,0:T(8,128)(2,1)S(1)}, bf16[128,256]{1,0:T(8,128)(2,1)S(1)}, u32[]{:S(2)}, u32[]{:S(2)}) collective-permute-start(bf16[128,256]{1,0:T(8,128)(2,1)S(1)} %get-tuple-element.55.refs_10_), channel_id=1, source_target_pairs={{0,8},{1,13},{4,12},{5,9},{8,0},{9,5},{12,4},{13,1},{2,10},{3,15},... | collective-permute-start | bytes 196616 | tf_op jit(solution)/shard_map/ppermute | solution.py:379
  4.9 4.0 %collective-permute-start = (bf16[128,128]{1,0:T(8,128)(2,1)S(1)}, bf16[128,128]{1,0:T(8,128)(2,1)S(1)}, u32[]{:S(2)}, u32[]{:S(2)}) collective-permute-start(bf16[128,128]{1,0:T(8,128)(2,1)S(1)} %get-tuple-element.49.refs_6_), channel_id=1, source_target_pairs={{0,4},{4,0},{8,12},{12,8},{1,5},{5,1},{9,13},{13,9},{2,6},{6,2},{1... | collective-permute-start | bytes 98312 | tf_op jit(solution)/shard_map/ppermute | solution.py:354
  8.7 1.7 %collective-permute-start.3 = (bf16[128,256]{1,0:T(8,128)(2,1)S(1)}, bf16[128,256]{1,0:T(8,128)(2,1)S(1)}, u32[]{:S(2)}, u32[]{:S(2)}) collective-permute-start(bf16[128,256]{1,0:T(8,128)(2,1)S(1)} %collective-permute-done.2.refs_13_), channel_id=1, source_target_pairs={{0,1},{1,0},{2,3},{3,2},{4,5},{5,4},{6,7},{7,6},{8,9},{9,8},{10,11... | collective-permute-start | bytes 196616 | tf_op jit(solution)/shard_map/ppermute | solution.py:323
  8.9 1.5 %collective-permute-start.1 = (bf16[128,128]{1,0:T(8,128)(2,1)S(1)}, bf16[128,128]{1,0:T(8,128)(2,1)S(1)}, u32[]{:S(2)}, u32[]{:S(2)}) collective-permute-start(bf16[128,128]{1,0:T(8,128)(2,1)S(1)} %collective-permute-done.refs_11_), channel_id=1, source_target_pairs={{0,1},{1,0},{2,3},{3,2},{4,5},{5,4},{6,7},{7,6},{8,9},{9,8},{10,11... | collective-permute-start | bytes 98312 | tf_op jit(solution)/shard_map/ppermute | solution.py:323
  12.8 10.9 %collective-permute-start.5 = (bf16[80,1024]{1,0:T(8,128)(2,1)S(1)}, bf16[80,1024]{1,0:T(8,128)(2,1)S(1)}, u32[]{:S(2)}, u32[]{:S(2)}) collective-permute-start(bf16[80,1024]{1,0:T(8,128)(2,1)S(1)} %get-tuple-element.61), channel_id=1, source_target_pairs={{0,8},{4,12},{8,0},{12,4},{1,9},{5,13},{9,1},{13,5},{2,10},{6,14},... | collective-permute-start | bytes 491528 | tf_op jit(solution)/shard_map/ppermute | solution.py:354
  15.6 2.6 %collective-permute-start.7 = (bf16[80,512]{1,0:T(8,128)(2,1)S(1)}, bf16[80,512]{1,0:T(8,128)(2,1)S(1)}, u32[]{:S(2)}, u32[]{:S(2)}) collective-permute-start(bf16[80,512]{1,0:T(8,128)(2,1)S(1)} %get-tuple-element.65), channel_id=1, source_target_pairs={{0,1},{1,0},{2,3},{3,2},{4,5},{5,4},{6,7},{7,6},{8,9},{9,8},{10,11... | collective-permute-start | bytes 245768 | tf_op jit(solution)/shard_map/ppermute | solution.py:323
  15.7 2.5 %collective-permute-start.6 = (bf16[80,384]{1,0:T(8,128)(2,1)S(1)}, bf16[80,384]{1,0:T(8,128)(2,1)S(1)}, u32[]{:S(2)}, u32[]{:S(2)}) collective-permute-start(bf16[80,384]{1,0:T(8,128)(2,1)S(1)} %get-tuple-element.64), channel_id=1, source_target_pairs={{0,1},{1,0},{2,3},{3,2},{4,5},{5,4},{6,7},{7,6},{8,9},{9,8},{10,11... | collective-permute-start | bytes 184328 | tf_op jit(solution)/shard_map/ppermute | solution.py:323
  16.2 11.5 %collective-permute-start.4 = (bf16[80,1024]{1,0:T(8,128)(2,1)S(1)}, bf16[80,1024]{1,0:T(8,128)(2,1)S(1)}, u32[]{:S(2)}, u32[]{:S(2)}) collective-permute-start(bf16[80,1024]{1,0:T(8,128)(2,1)S(1)} %get-tuple-element.60), channel_id=1, source_target_pairs={{0,4},{4,0},{8,12},{12,8},{1,5},{5,1},{9,13},{13,9},{2,6},{6,2},{1... | collective-permute-start | bytes 491528 | tf_op jit(solution)/shard_map/ppermute | solution.py:354
  18.3 10.0 %collective-permute-start.12 = (bf16[80,896]{1,0:T(8,128)(2,1)S(1)}, bf16[80,896]{1,0:T(8,128)(2,1)S(1)}, u32[]{:S(2)}, u32[]{:S(2)}) collective-permute-start(bf16[80,896]{1,0:T(8,128)(2,1)S(1)} %get-tuple-element.73), channel_id=1, source_target_pairs={{0,2},{2,0},{1,3},{3,1},{4,6},{6,4},{5,7},{7,5},{8,10},{10,8},{9,1... | collective-permute-start | bytes 430088 | tf_op jit(solution)/shard_map/ppermute | solution.py:323
  24.3 4.2 %collective-permute-start.11 = (bf16[80,512]{1,0:T(8,128)(2,1)S(1)}, bf16[80,512]{1,0:T(8,128)(2,1)S(1)}, u32[]{:S(2)}, u32[]{:S(2)}) collective-permute-start(bf16[80,512]{1,0:T(8,128)(2,1)S(1)} %get-tuple-element.72), channel_id=1, source_target_pairs={{0,1},{1,0},{2,3},{3,2},{4,5},{5,4},{6,7},{7,6},{8,9},{9,8},{10,11... | collective-permute-start | bytes 245768 | tf_op jit(solution)/shard_map/ppermute | solution.py:323
  24.4 4.1 %collective-permute-start.10 = (bf16[80,384]{1,0:T(8,128)(2,1)S(1)}, bf16[80,384]{1,0:T(8,128)(2,1)S(1)}, u32[]{:S(2)}, u32[]{:S(2)}) collective-permute-start(bf16[80,384]{1,0:T(8,128)(2,1)S(1)} %get-tuple-element.71), channel_id=1, source_target_pairs={{0,1},{1,0},{2,3},{3,2},{4,5},{5,4},{6,7},{7,6},{8,9},{9,8},{10,11... | collective-permute-start | bytes 184328 | tf_op jit(solution)/shard_map/ppermute | solution.py:323
  24.9 8.1 %collective-permute-start.14 = (bf16[80,1024]{1,0:T(8,128)(2,1)S(1)}, bf16[80,1024]{1,0:T(8,128)(2,1)S(1)}, u32[]{:S(2)}, u32[]{:S(2)}) collective-permute-start(bf16[80,1024]{1,0:T(8,128)(2,1)S(1)} %get-tuple-element.78), channel_id=1, source_target_pairs={{0,12},{4,8},{8,4},{12,0},{1,13},{5,9},{9,5},{13,1},{2,14},{6,10},... | collective-permute-start | bytes 491528 | tf_op jit(solution)/shard_map/ppermute | solution.py:354
  28.7 5.5 %collective-permute-start.17 = (bf16[80,896]{1,0:T(8,128)(2,1)S(1)}, bf16[80,896]{1,0:T(8,128)(2,1)S(1)}, u32[]{:S(2)}, u32[]{:S(2)}) collective-permute-start(bf16[80,896]{1,0:T(8,128)(2,1)S(1)} %get-tuple-element.83), channel_id=1, source_target_pairs={{0,2},{2,0},{1,3},{3,1},{4,6},{6,4},{5,7},{7,5},{8,10},{10,8},{9,1... | collective-permute-start | bytes 430088 | tf_op jit(solution)/shard_map/ppermute | solution.py:323
  30.2 1.4 %collective-permute-start.9 = (bf16[96,512]{1,0:T(8,128)(2,1)S(1)}, bf16[96,512]{1,0:T(8,128)(2,1)S(1)}, u32[]{:S(2)}, u32[]{:S(2)}) collective-permute-start(bf16[96,512]{1,0:T(8,128)(2,1)S(1)} %get-tuple-element.70), channel_id=1, source_target_pairs={{0,1},{1,0},{2,3},{3,2},{4,5},{5,4},{6,7},{7,6},{8,9},{9,8},{10,11... | collective-permute-start | bytes 294920 | tf_op jit(solution)/shard_map/ppermute | solution.py:323
  30.2 1.4 %collective-permute-start.8 = (bf16[80,384]{1,0:T(8,128)(2,1)S(1)}, bf16[80,384]{1,0:T(8,128)(2,1)S(1)}, u32[]{:S(2)}, u32[]{:S(2)}) collective-permute-start(bf16[80,384]{1,0:T(8,128)(2,1)S(1)} %get-tuple-element.69), channel_id=1, source_target_pairs={{0,1},{1,0},{2,3},{3,2},{4,5},{5,4},{6,7},{7,6},{8,9},{9,8},{10,11... | collective-permute-start | bytes 184328 | tf_op jit(solution)/shard_map/ppermute | solution.py:323
  31.7 6.7 %collective-permute-start.13 = (bf16[96,896]{1,0:T(8,128)(2,1)S(1)}, bf16[96,896]{1,0:T(8,128)(2,1)S(1)}, u32[]{:S(2)}, u32[]{:S(2)}) collective-permute-start(bf16[96,896]{1,0:T(8,128)(2,1)S(1)} %get-tuple-element.77), channel_id=1, source_target_pairs={{0,2},{2,0},{1,3},{3,1},{4,6},{6,4},{5,7},{7,5},{8,10},{10,8},{9,1... | collective-permute-start | bytes 516104 | tf_op jit(solution)/shard_map/ppermute | solution.py:323
  33.6 2.5 %collective-permute-start.16 = (bf16[80,512]{1,0:T(8,128)(2,1)S(1)}, bf16[80,512]{1,0:T(8,128)(2,1)S(1)}, u32[]{:S(2)}, u32[]{:S(2)}) collective-permute-start(bf16[80,512]{1,0:T(8,128)(2,1)S(1)} %get-tuple-element.81), channel_id=1, source_target_pairs={{0,1},{1,0},{2,3},{3,2},{4,5},{5,4},{6,7},{7,6},{8,9},{9,8},{10,11... | collective-permute-start | bytes 245768 | tf_op jit(solution)/shard_map/ppermute | solution.py:323
  33.7 1.4 %collective-permute-start.19 = (bf16[80,384]{1,0:T(8,128)(2,1)S(1)}, bf16[80,384]{1,0:T(8,128)(2,1)S(1)}, u32[]{:S(2)}, u32[]{:S(2)}) collective-permute-start(bf16[80,384]{1,0:T(8,128)(2,1)S(1)} %shard_map.116.refs_3_.refs_2_), channel_id=1, source_target_pairs={{0,1},{1,0},{2,3},{3,2},{4,5},{5,4},{6,7},{7,6},{8,9},{9,8},{10,11... | collective-permute-start | bytes 184328 | tf_op jit(solution)/shard_map/ppermute | solution.py:323
  34.5 1.6 %collective-permute-start.15 = (bf16[80,384]{1,0:T(8,128)(2,1)S(1)}, bf16[80,384]{1,0:T(8,128)(2,1)S(1)}, u32[]{:S(2)}, u32[]{:S(2)}) collective-permute-start(bf16[80,384]{1,0:T(8,128)(2,1)S(1)} %get-tuple-element.80), channel_id=1, source_target_pairs={{0,1},{1,0},{2,3},{3,2},{4,5},{5,4},{6,7},{7,6},{8,9},{9,8},{10,11... | collective-permute-start | bytes 184328 | tf_op jit(solution)/shard_map/ppermute | solution.py:323
  36.3 6.0 %collective-permute-start.22 = (bf16[80,896]{1,0:T(8,128)(2,1)S(1)}, bf16[80,896]{1,0:T(8,128)(2,1)S(1)}, u32[]{:S(2)}, u32[]{:S(2)}) collective-permute-start(bf16[80,896]{1,0:T(8,128)(2,1)S(1)} %get-tuple-element.90), channel_id=1, source_target_pairs={{0,2},{2,0},{1,3},{3,1},{4,6},{6,4},{5,7},{7,5},{8,10},{10,8},{9,1... | collective-permute-start | bytes 430088 | tf_op jit(solution)/shard_map/ppermute | solution.py:323
  38.2 10.5 %collective-permute-start.21 = (bf16[80,1024]{1,0:T(8,128)(2,1)S(1)}, bf16[80,1024]{1,0:T(8,128)(2,1)S(1)}, u32[]{:S(2)}, u32[]{:S(2)}) collective-permute-start(bf16[80,1024]{1,0:T(8,128)(2,1)S(1)} %shard_map.122.refs_3_), channel_id=1, source_target_pairs={{0,8},{4,12},{8,0},{12,4},{1,9},{5,13},{9,1},{13,5},{2,10},{6,14},... | collective-permute-start | bytes 491528 | tf_op jit(solution)/shard_map/ppermute | solution.py:354
  42.4 6.5 %collective-permute-start.24 = (bf16[80,384]{1,0:T(8,128)(2,1)S(1)}, bf16[80,384]{1,0:T(8,128)(2,1)S(1)}, u32[]{:S(2)}, u32[]{:S(2)}) collective-permute-start(bf16[80,384]{1,0:T(8,128)(2,1)S(1)} %shard_map.128.refs_3_.refs_2_), channel_id=1, source_target_pairs={{0,1},{1,0},{2,3},{3,2},{4,5},{5,4},{6,7},{7,6},{8,9},{9,8},{10,11... | collective-permute-start | bytes 184328 | tf_op jit(solution)/shard_map/ppermute | solution.py:323
  42.5 9.4 %collective-permute-start.23 = (bf16[80,1024]{1,0:T(8,128)(2,1)S(1)}, bf16[80,1024]{1,0:T(8,128)(2,1)S(1)}, u32[]{:S(2)}, u32[]{:S(2)}) collective-permute-start(bf16[80,1024]{1,0:T(8,128)(2,1)S(1)} %shard_map.126.refs_3_), channel_id=1, source_target_pairs={{0,4},{4,0},{8,12},{12,8},{1,5},{5,1},{9,13},{13,9},{2,6},{6,2},{1... | collective-permute-start | bytes 491528 | tf_op jit(solution)/shard_map/ppermute | solution.py:354
  49.4 7.4 %collective-permute-start.25 = (bf16[80,1024]{1,0:T(8,128)(2,1)S(1)}, bf16[80,1024]{1,0:T(8,128)(2,1)S(1)}, u32[]{:S(2)}, u32[]{:S(2)}) collective-permute-start(bf16[80,1024]{1,0:T(8,128)(2,1)S(1)} %shard_map.130.refs_5_), channel_id=1, source_target_pairs={{0,12},{4,8},{8,4},{12,0},{1,13},{5,9},{9,5},{13,1},{2,14},{6,10},... | collective-permute-start | bytes 491528 | tf_op jit(solution)/shard_map/ppermute | solution.py:354
  (2 other events, 2.6 us)

commit v4 on v3

--- a/solution.py
+++ b/solution.py
@@ -101,15 +101,10 @@
     target_ref[...] = target
 
 
-def attend_kernel(n, cap, place_ref, rep_ref, gate_in, up_in, down_in, q_ref, stream_ref, gain_ref, router_ref, target_ref, kv_ref, *rest):
+def attend_kernel(n, first, place_ref, rep_ref, gate_in, up_in, q_ref, stream_ref, gain_ref, target_ref, kv_ref, *rest):
     (near_mine, near_theirs, far_mine, far_theirs), rest = rest[:4], rest[4:]
-    (hidden_ref, stats_ref), row_refs, weight_refs, (k_all, v_all, gained, sems) = (
-        rest[:2],
-        rest[2 : n + 2],
-        rest[n + 2 : n + 5],
-        rest[n + 5 :],
-    )
-    pairs = zip((gate_in, up_in, down_in), weight_refs)
+    hidden_ref, gained, squares_ref, first_ref, *weight_refs, k_all, v_all, sems = rest
+    pairs = zip((gate_in, up_in), weight_refs)
     copies = [pltpu.make_async_copy(a, b, sems.at[i]) for i, (a, b) in enumerate(pairs)]
     for copy in copies:
         copy.start()
@@ -157,22 +152,39 @@
         hidden_ref[:, cols] = hidden
         squares = squares + jnp.sum(hidden * hidden, axis=-1, keepdims=True)
         gained[:, cols] = (hidden * gain_ref[head : head + 1, :].astype(F32)).astype(BF16)
-    values = gained[...]
-    earlier = (row < col).astype(F32).astype(BF16)
-    slot = lax.broadcasted_iota(jnp.int32, (cap, tokens), 0)
-    for j in range(n):
+    squares_ref[...] = jnp.broadcast_to(squares, squares_ref.shape)
+    place_rows(place, target_ref, gained[...], [first], [first_ref])
+    for copy in copies:
+        copy.wait()
+
+
+def place_rows(place, target_ref, values, blocks, row_refs):
+    tokens = values.shape[0]
+    earlier = (
+        lax.broadcasted_iota(jnp.int32, (tokens, tokens), 0)
+        < lax.broadcasted_iota(jnp.int32, (tokens, tokens), 1)
+    ).astype(F32).astype(BF16)
+    slot = lax.broadcasted_iota(jnp.int32, (row_refs[0].shape[0], tokens), 0)
+    for j, row_ref in zip(blocks, row_refs):
         member = jnp.sum((target_ref[...] == jnp.bitwise_xor(place, j)).astype(F32), axis=0, keepdims=True)
         rank = dot(jnp.broadcast_to(member, (8, tokens)).astype(BF16), earlier)[0:1, :]
         rank = jnp.where(member > 0.5, rank, -1.0).astype(jnp.int32)
         placing = (slot == rank).astype(F32).astype(BF16)
-        row_refs[j][...] = dot(placing, values).astype(BF16)
-    squares_row = jnp.transpose(jnp.broadcast_to(squares, (tokens, LANES)))
+        row_ref[...] = dot(placing, values).astype(BF16)
+
+
+def rows_kernel(blocks, place_ref, down_in, gained_ref, squares_ref, router_ref, target_ref, *refs):
+    row_refs, (stats_ref, down_ref, sem) = refs[: len(blocks)], refs[len(blocks) :]
+    copy = pltpu.make_async_copy(down_in, down_ref, sem)
+    copy.start()
+    values = gained_ref[...]
+    place_rows(place_ref[0], target_ref, values, blocks, row_refs)
+    squares_row = jnp.transpose(squares_ref[...])
     height = stats_ref.shape[0]
     stats_ref[...] = jnp.concatenate(
         [dot_nt(router_ref[...], values), squares_row[: height - router_ref.shape[0], :]], axis=0
     )
-    for copy in copies:
-        copy.wait()
+    copy.wait()
 
 
 def split_pair(x):
@@ -381,27 +393,38 @@
     )
     stat_rows = -(-(experts + 1) // 8) * 8
 
-    weights = [w_gate[0], w_up[0], w_down[0]]
-    hidden, stats, *rows = vmem_call(
-        functools.partial(attend_kernel, n, cap),
+    chain = [0] + [distance[0], *distance[:0:-1]]
+    block = jax.ShapeDtypeStruct((cap, width), BF16)
+    weights = [w_gate[0], w_up[0]]
+    hidden, gained, squares, first_rows, gate, up = vmem_call(
+        functools.partial(attend_kernel, n, chain[1]),
         [
             jax.ShapeDtypeStruct((tokens, width), F32),
-            jax.ShapeDtypeStruct((stat_rows, tokens), F32),
+            jax.ShapeDtypeStruct((tokens, width), BF16),
+            jax.ShapeDtypeStruct((tokens, LANES), F32),
+            block,
         ]
-        + [jax.ShapeDtypeStruct((cap, width), BF16)] * n
         + [like(x) for x in weights],
         [where, side],
-        [queries, stream, gain, router_rows, target, own_kv, near_kv, swap(near_kv, "rep")]
+        [queries, stream, gain, target, own_kv, near_kv, swap(near_kv, "rep")]
         + [far_kv, swap(far_kv, "rep")],
         remote=weights,
         scratch=[
             pltpu.VMEM((n * tokens, HEAD_SIZE), BF16),
             pltpu.VMEM((n * tokens, HEAD_SIZE), BF16),
-            pltpu.VMEM((tokens, width), BF16),
-            pltpu.SemaphoreType.DMA((3,)),
+            pltpu.SemaphoreType.DMA((2,)),
         ],
     )
-    rows, (gate, up, down) = rows[:n], rows[n:]
+    others = [j for j in range(n) if j != chain[1]]
+    *rows, stats, down = vmem_call(
+        functools.partial(rows_kernel, others),
+        [block] * (n - 1) + [jax.ShapeDtypeStruct((stat_rows, tokens), F32), like(w_down[0])],
+        [where],
+        [gained, squares, router_rows, target],
+        remote=[w_down[0]],
+        scratch=[pltpu.SemaphoreType.DMA],
+    )
+    rows = {chain[1]: first_rows, **dict(zip(others, rows))}
     arrived = {j: exchange(rows[j], j) for j in distance}
     arrived[0] = rows[0]
 
@@ -478,10 +501,9 @@
         )
 
     steps = dict(u=up_step, a=add_step, i=inner_step, d=down_step, m=lambda j: mix_step([j]))
-    chain = [0] + [distance[0], *distance[:0:-1]]
     plan = (
-        *("u0", "a0", "u1", "u2", "i0", "a1", "a2", "u3", "i1", "d0", "d1"),
-        *("a3", "i2", "g", "d2", "m0", "i3", "m1", "d3"),
+        *("u0", "a0", "u1", "i0", "a1", "u2", "a2", "u3", "i1", "d1"),
+        *("d0", "a3", "i2", "g", "d2", "m0", "i3", "m1", "d3", "m2"),
     )
     for name in plan:
         if name == "g":

time: 58.1 us -> 57.4 us (0.988)
  waiting for transfers between devices: 21.1 us -> 19.1 us
  Pallas kernels: 12.1 us -> 13.3 us
    ppermute x7, waiting for transfers between devices: 15.4 us -> 13.3 us  [exchange(): return lax.ppermute(x, 'ctx', [(i, i ^ j) for i in range(n)])]
    pallas_call x23 -> x25, Pallas kernels: 12.1 us -> 13.3 us  [vmem_call(): pl.pallas_call(kernel, out_shape=[placed(x) for x in out_shape] if multi...]
  transfers between devices with their start and end apart: 26 -> 26, of which waited for: 13 -> 12; matrix products, arithmetic and copies ran while one was open for 0% -> 0% of each run, Pallas kernels for 13% -> 17%
where the time goes in v4:
time: 57.4 us; the launch traced here: 57.2 us
  starting transfers between devices  24.6 us (43%)
  waiting for transfers between devices  19.1 us (33%)
  Pallas kernels  13.3 us (23%)
    ppermute x7, waiting for transfers between devices, exchange(): return lax.ppermute(x, 'ctx', [(i, i ^ j) for i in range(n)])  13.3 us
    pallas_call x25, Pallas kernels, vmem_call(): pl.pallas_call(kernel, out_shape=[placed(x) for x in out_shape] if multi...  13.3 us
    ppermute x7, starting transfers between devices, exchange(): return lax.ppermute(x, 'ctx', [(i, i ^ j) for i in range(n)])  11.8 us
    ppermute x18, starting transfers between devices, swap(): return lax.ppermute(x, axis, [(0, 1), (1, 0)])  8.7 us
    ppermute x1, starting transfers between devices, direct(): lax.ppermute(own_kv, ('ctx', 'rep'), [(2 * i + r, 2 * (i ^ 2 + r) + r) fo...  4.1 us
    ppermute x18, waiting for transfers between devices, swap(): return lax.ppermute(x, axis, [(0, 1), (1, 0)])  3.61 us
    ppermute x1, waiting for transfers between devices, direct(): lax.ppermute(own_kv, ('ctx', 'rep'), [(2 * i + r, 2 * (i ^ 2 + r) + r) fo...  2.19 us
  transfers between devices with their start and end apart: 26, of which 12 were waited for; matrix products, arithmetic and copies ran while one was open for 0% of the time, Pallas kernels for 17%

profile of v4, /device:TPU:0, one launch (start us, length us, event | category | flops | bytes accessed | tf_op | source)
XLA Modules:
  0.0 57.2 jit_solution(12713951660727058272)
XLA Ops:
  0.0 0.8 %shard_map.109 = (bf16[128,256]{1,0:T(8,128)(2,1)S(1)}, bf16[128,128]{1,0:T(8,128)(2,1)S(1)}) custom-call(s32[1]{0:T(128)} %bitcast.8.refs_0_, s32[1]{0:T(128)} %bitcast.1.refs_1_.refs_0_, bf16[128,256]{1,0:T(8,128)(2,1)} %refs_2_.1, bf16[128,256]{1,0:T(8,128)(2,1)} %refs_3_.1), custom_call_target="tpu_custom_call" | custom-call | flops 1 | bytes 1 | tf_op jit(solution)/shard_map/pallas_call | solution.py:44
  0.8 4.1 %collective-permute-start.2 = (bf16[128,256]{1,0:T(8,128)(2,1)S(1)}, bf16[128,256]{1,0:T(8,128)(2,1)S(1)}, u32[]{:S(2)}, u32[]{:S(2)}) collective-permute-start(bf16[128,256]{1,0:T(8,128)(2,1)S(1)} %get-tuple-element.56.refs_8_), channel_id=1, source_target_pairs={{0,8},{1,13},{4,12},{5,9},{8,0},{9,5},{12,4},{13,1},{2,10},{3,15},... | collective-permute-start | bytes 196616 | tf_op jit(solution)/shard_map/ppermute | solution.py:391
  4.9 1.6 %collective-permute-start = (bf16[128,128]{1,0:T(8,128)(2,1)S(1)}, bf16[128,128]{1,0:T(8,128)(2,1)S(1)}, u32[]{:S(2)}, u32[]{:S(2)}) collective-permute-start(bf16[128,128]{1,0:T(8,128)(2,1)S(1)} %get-tuple-element.51.refs_6_), channel_id=1, source_target_pairs={{0,4},{4,0},{8,12},{12,8},{1,5},{5,1},{9,13},{13,9},{2,6},{6,2},{1... | collective-permute-start | bytes 98312 | tf_op jit(solution)/shard_map/ppermute | solution.py:366
  6.5 2.2 %collective-permute-done.2.refs_11_ = bf16[128,256]{1,0:T(8,128)(2,1)S(1)} collective-permute-done((bf16[128,256]{1,0:T(8,128)(2,1)S(1)}, bf16[128,256]{1,0:T(8,128)(2,1)S(1)}, u32[]{:S(2)}, u32[]{:S(2)}) %collective-permute-start.2) | collective-permute-done | bytes 65568 | tf_op jit(solution)/shard_map/ppermute | solution.py:391
  9.2 1.2 %shard_map.110 = (bf16[128,1024]{1,0:T(8,128)(2,1)S(1)}, bf16[128,1024]{1,0:T(8,128)(2,1)S(1)}, bf16[8,128]{1,0:T(8,128)(2,1)S(1)}, bf16[4,1024]{1,0:T(4,128)(2,...) custom-call(bf16[128,1024]{1,0:T(8,128)(2,1)} %refs_0_.1, bf16[128,1024]{1,0:T(8,128)(2,1)} %refs_1_.1, ...), custom_call_target="tpu_custom_call" | custom-call | flops 1 | bytes 1 | tf_op jit(solution)/shard_map/pallas_call | solution.py:44
  10.4 1.9 %shard_map.111 = (f32[128,1024]{1,0:T(8,128)S(1)}, bf16[128,1024]{1,0:T(8,128)(2,1)S(1)}, f32[128,128]{1,0:T(8,128)S(1)}, bf16[80,1024]{1,0:T(8,128)(2,1)S(1)}, ...) custom-call(s32[1]{0:T(128)} %bitcast.refs_0_, s32[1]{0:T(128)} %bitcast.1.refs_1_.refs_0_, ...), custom_call_target="tpu_custom_call" | custom-call | flops 1 | bytes 1 | tf_op jit(solution)/shard_map/pallas_call | solution.py:44
  12.3 2.2 %collective-permute-start.5 = (bf16[80,1024]{1,0:T(8,128)(2,1)S(1)}, bf16[80,1024]{1,0:T(8,128)(2,1)S(1)}, u32[]{:S(2)}, u32[]{:S(2)}) collective-permute-start(bf16[80,1024]{1,0:T(8,128)(2,1)S(1)} %get-tuple-element.65), channel_id=1, source_target_pairs={{0,8},{4,12},{8,0},{12,4},{1,9},{5,13},{9,1},{13,5},{2,10},{6,14},... | collective-permute-start | bytes 491528 | tf_op jit(solution)/shard_map/ppermute | solution.py:366
  14.5 1.4 %shard_map.112 = (bf16[80,1024]{1,0:T(8,128)(2,1)S(1)}, bf16[80,1024]{1,0:T(8,128)(2,1)S(1)}, bf16[80,1024]{1,0:T(8,128)(2,1)S(1)}, f32[8,128]{1,0:T(8,128)S(1)}, bf16[768,1024]{1,0:T(8,128)(2,1)S(1)}) custom-call(s32[1]{0:T(128)} %bitcast.refs_0_, bf16[768,1024]{1,0:T(8,128)(2,1)} %bitcast.12, bf16[128,1024]{1,0:T(8,128)(2,1)S(1)} %get-tuple-element.58.refs_2_, ...), custom_call_target="tpu_custom_call" | custom-call | flops 1 | bytes 1 | tf_op jit(solution)/shard_map/pallas_call | solution.py:44
  17.1 2.0 %collective-permute-start.4 = (bf16[80,1024]{1,0:T(8,128)(2,1)S(1)}, bf16[80,1024]{1,0:T(8,128)(2,1)S(1)}, u32[]{:S(2)}, u32[]{:S(2)}) collective-permute-start(bf16[80,1024]{1,0:T(8,128)(2,1)S(1)} %get-tuple-element.64), channel_id=1, source_target_pairs={{0,4},{4,0},{8,12},{12,8},{1,5},{5,1},{9,13},{13,9},{2,6},{6,2},{1... | collective-permute-start | bytes 491528 | tf_op jit(solution)/shard_map/ppermute | solution.py:366
  19.3 1.6 %collective-permute-start.10 = (bf16[80,896]{1,0:T(8,128)(2,1)S(1)}, bf16[80,896]{1,0:T(8,128)(2,1)S(1)}, u32[]{:S(2)}, u32[]{:S(2)}) collective-permute-start(bf16[80,896]{1,0:T(8,128)(2,1)S(1)} %get-tuple-element.74), channel_id=1, source_target_pairs={{0,2},{2,0},{1,3},{3,1},{4,6},{6,4},{5,7},{7,5},{8,10},{10,8},{9,1... | collective-permute-start | bytes 430088 | tf_op jit(solution)/shard_map/ppermute | solution.py:335
  20.8 2.4 %collective-permute-done.5.refs_4_ = bf16[80,1024]{1,0:T(8,128)(2,1)S(1)} collective-permute-done((bf16[80,1024]{1,0:T(8,128)(2,1)S(1)}, bf16[80,1024]{1,0:T(8,128)(2,1)S(1)}, u32[]{:S(2)}, u32[]{:S(2)}) %collective-permute-start.5) | collective-permute-done | bytes 163872 | tf_op jit(solution)/shard_map/ppermute | solution.py:366
  23.2 0.6 %shard_map.115 = (f32[80,896]{1,0:T(8,128)S(1)}, bf16[80,384]{1,0:T(8,128)(2,1)S(1)}, bf16[80,512]{1,0:T(8,128)(2,1)S(1)}) custom-call(s32[1]{0:T(128)} %bitcast.1.refs_1_.refs_0_, bf16[1024,768]{1,0:T(8,128)(2,1)S(1)} %get-tuple-element.62.refs_1_, bf16[1024,768]{1,0:T(8,128)(2,1)S(1)} %get-tuple-element.63.refs_2_, ...), custom_call_target="tpu_custom_call" | custom-call | flops 1 | bytes 1 | tf_op jit(solution)/shard_map/pallas_call | solution.py:44
  24.4 2.8 %collective-permute-start.14 = (bf16[80,1024]{1,0:T(8,128)(2,1)S(1)}, bf16[80,1024]{1,0:T(8,128)(2,1)S(1)}, u32[]{:S(2)}, u32[]{:S(2)}) collective-permute-start(bf16[80,1024]{1,0:T(8,128)(2,1)S(1)} %get-tuple-element.82), channel_id=1, source_target_pairs={{0,12},{4,8},{8,4},{12,0},{1,13},{5,9},{9,5},{13,1},{2,14},{6,10},... | collective-permute-start | bytes 491528 | tf_op jit(solution)/shard_map/ppermute | solution.py:366
  27.6 1.6 %collective-permute-start.18 = (bf16[80,896]{1,0:T(8,128)(2,1)S(1)}, bf16[80,896]{1,0:T(8,128)(2,1)S(1)}, u32[]{:S(2)}, u32[]{:S(2)}) collective-permute-start(bf16[80,896]{1,0:T(8,128)(2,1)S(1)} %get-tuple-element.87), channel_id=1, source_target_pairs={{0,2},{2,0},{1,3},{3,1},{4,6},{6,4},{5,7},{7,5},{8,10},{10,8},{9,1... | collective-permute-start | bytes 430088 | tf_op jit(solution)/shard_map/ppermute | solution.py:335
  30.3 0.9 %collective-permute-done.11.refs_2_ = bf16[80,384]{1,0:T(8,128)(2,1)S(1)} collective-permute-done((bf16[80,384]{1,0:T(8,128)(2,1)S(1)}, bf16[80,384]{1,0:T(8,128)(2,1)S(1)}, u32[]{:S(2)}, u32[]{:S(2)}) %collective-permute-start.11) | collective-permute-done | bytes 61472 | tf_op jit(solution)/shard_map/ppermute | solution.py:335
  35.9 1.7 %collective-permute-start.22 = (bf16[80,896]{1,0:T(8,128)(2,1)S(1)}, bf16[80,896]{1,0:T(8,128)(2,1)S(1)}, u32[]{:S(2)}, u32[]{:S(2)}) collective-permute-start(bf16[80,896]{1,0:T(8,128)(2,1)S(1)} %get-tuple-element.94), channel_id=1, source_target_pairs={{0,2},{2,0},{1,3},{3,1},{4,6},{6,4},{5,7},{7,5},{8,10},{10,8},{9,1... | collective-permute-start | bytes 430088 | tf_op jit(solution)/shard_map/ppermute | solution.py:335
  38.3 0.7 %shard_map.126 = (bf16[256,80]{1,0:T(8,128)(2,1)S(1)}, bf16[256,80]{1,0:T(8,128)(2,1)S(1)}, bf16[256,80]{1,0:T(8,128)(2,1)S(1)}, bf16[256,80]{1,0:T(8,128)(2,1)S(1)}) custom-call(s32[1]{0:T(128)} %bitcast.refs_0_, f32[8,128]{1,0:T(8,128)S(1)} %get-tuple-element.89.refs_1_, s32[2,128]{1,0:T(2,128)S(1)} %get-tuple-element.90.refs_2_, ...), custom_call_target="tpu_custom_call" | custom-call | flops 1 | bytes 1 | tf_op jit(solution)/shard_map/pallas_call | solution.py:44
  40.2 1.7 %collective-permute-done.22.refs_1_ = bf16[80,896]{1,0:T(8,128)(2,1)S(1)} collective-permute-done((bf16[80,896]{1,0:T(8,128)(2,1)S(1)}, bf16[80,896]{1,0:T(8,128)(2,1)S(1)}, u32[]{:S(2)}, u32[]{:S(2)}) %collective-permute-start.22) | collective-permute-done | bytes 143392 | tf_op jit(solution)/shard_map/ppermute | solution.py:335
  42.2 1.6 %collective-permute-start.23 = (bf16[80,1024]{1,0:T(8,128)(2,1)S(1)}, bf16[80,1024]{1,0:T(8,128)(2,1)S(1)}, u32[]{:S(2)}, u32[]{:S(2)}) collective-permute-start(bf16[80,1024]{1,0:T(8,128)(2,1)S(1)} %shard_map.127.refs_3_), channel_id=1, source_target_pairs={{0,4},{4,0},{8,12},{12,8},{1,5},{5,1},{9,13},{13,9},{2,6},{6,2},{1... | collective-permute-start | bytes 491528 | tf_op jit(solution)/shard_map/ppermute | solution.py:366
  43.8 4.4 %collective-permute-done.21.refs_2_ = bf16[80,1024]{1,0:T(8,128)(2,1)S(1)} collective-permute-done((bf16[80,1024]{1,0:T(8,128)(2,1)S(1)}, bf16[80,1024]{1,0:T(8,128)(2,1)S(1)}, u32[]{:S(2)}, u32[]{:S(2)}) %collective-permute-start.21) | collective-permute-done | bytes 163872 | tf_op jit(solution)/shard_map/ppermute | solution.py:366
  49.0 1.3 %collective-permute-start.25 = (bf16[80,1024]{1,0:T(8,128)(2,1)S(1)}, bf16[80,1024]{1,0:T(8,128)(2,1)S(1)}, u32[]{:S(2)}, u32[]{:S(2)}) collective-permute-start(bf16[80,1024]{1,0:T(8,128)(2,1)S(1)} %shard_map.131.refs_3_), channel_id=1, source_target_pairs={{0,12},{4,8},{8,4},{12,0},{1,13},{5,9},{9,5},{13,1},{2,14},{6,10},... | collective-permute-start | bytes 491528 | tf_op jit(solution)/shard_map/ppermute | solution.py:366
  50.3 1.2 %collective-permute-done.23.refs_2_ = bf16[80,1024]{1,0:T(8,128)(2,1)S(1)} collective-permute-done((bf16[80,1024]{1,0:T(8,128)(2,1)S(1)}, bf16[80,1024]{1,0:T(8,128)(2,1)S(1)}, u32[]{:S(2)}, u32[]{:S(2)}) %collective-permute-start.23) | collective-permute-done | bytes 163872 | tf_op jit(solution)/shard_map/ppermute | solution.py:366
  51.7 4.5 %collective-permute-done.25.refs_2_ = bf16[80,1024]{1,0:T(8,128)(2,1)S(1)} collective-permute-done((bf16[80,1024]{1,0:T(8,128)(2,1)S(1)}, bf16[80,1024]{1,0:T(8,128)(2,1)S(1)}, u32[]{:S(2)}, u32[]{:S(2)}) %collective-permute-start.25) | collective-permute-done | bytes 163872 | tf_op jit(solution)/shard_map/ppermute | solution.py:366
  56.2 1.0 %shard_map.133 = bf16[128,1024]{1,0:T(8,128)(2,1)} custom-call(f32[128,1024]{1,0:T(8,128)S(1)} %shard_map.132.refs_0_.refs_3_, bf16[256,80]{1,0:T(8,128)(2,1)S(1)} %get-tuple-element.96.refs_1_, bf16[80,1024]{1,0:T(8,128)(2,1)S(1)} %collective-permute-done.25.refs_2_, f32[128,1024]{1,0:T(8,128)S(1)} %shard_map.132.refs_0_.refs_3_), custom_call_target="tpu_custom_call" | custom-call | flops 1 | bytes 1 | tf_op jit(solution)/shard_map/pallas_call | solution.py:44
  (53 shorter events, 11.6 us)
Async XLA Ops:
  0.8 7.9 %collective-permute-start.2 = (bf16[128,256]{1,0:T(8,128)(2,1)S(1)}, bf16[128,256]{1,0:T(8,128)(2,1)S(1)}, u32[]{:S(2)}, u32[]{:S(2)}) collective-permute-start(bf16[128,256]{1,0:T(8,128)(2,1)S(1)} %get-tuple-element.56.refs_8_), channel_id=1, source_target_pairs={{0,8},{1,13},{4,12},{5,9},{8,0},{9,5},{12,4},{13,1},{2,10},{3,15},... | collective-permute-start | bytes 196616 | tf_op jit(solution)/shard_map/ppermute | solution.py:391
  4.9 4.0 %collective-permute-start = (bf16[128,128]{1,0:T(8,128)(2,1)S(1)}, bf16[128,128]{1,0:T(8,128)(2,1)S(1)}, u32[]{:S(2)}, u32[]{:S(2)}) collective-permute-start(bf16[128,128]{1,0:T(8,128)(2,1)S(1)} %get-tuple-element.51.refs_6_), channel_id=1, source_target_pairs={{0,4},{4,0},{8,12},{12,8},{1,5},{5,1},{9,13},{13,9},{2,6},{6,2},{1... | collective-permute-start | bytes 98312 | tf_op jit(solution)/shard_map/ppermute | solution.py:366
  8.7 1.7 %collective-permute-start.3 = (bf16[128,256]{1,0:T(8,128)(2,1)S(1)}, bf16[128,256]{1,0:T(8,128)(2,1)S(1)}, u32[]{:S(2)}, u32[]{:S(2)}) collective-permute-start(bf16[128,256]{1,0:T(8,128)(2,1)S(1)} %collective-permute-done.2.refs_11_), channel_id=1, source_target_pairs={{0,1},{1,0},{2,3},{3,2},{4,5},{5,4},{6,7},{7,6},{8,9},{9,8},{10,11... | collective-permute-start | bytes 196616 | tf_op jit(solution)/shard_map/ppermute | solution.py:335
  8.9 1.5 %collective-permute-start.1 = (bf16[128,128]{1,0:T(8,128)(2,1)S(1)}, bf16[128,128]{1,0:T(8,128)(2,1)S(1)}, u32[]{:S(2)}, u32[]{:S(2)}) collective-permute-start(bf16[128,128]{1,0:T(8,128)(2,1)S(1)} %collective-permute-done.refs_9_), channel_id=1, source_target_pairs={{0,1},{1,0},{2,3},{3,2},{4,5},{5,4},{6,7},{7,6},{8,9},{9,8},{10,11... | collective-permute-start | bytes 98312 | tf_op jit(solution)/shard_map/ppermute | solution.py:335
  12.3 10.9 %collective-permute-start.5 = (bf16[80,1024]{1,0:T(8,128)(2,1)S(1)}, bf16[80,1024]{1,0:T(8,128)(2,1)S(1)}, u32[]{:S(2)}, u32[]{:S(2)}) collective-permute-start(bf16[80,1024]{1,0:T(8,128)(2,1)S(1)} %get-tuple-element.65), channel_id=1, source_target_pairs={{0,8},{4,12},{8,0},{12,4},{1,9},{5,13},{9,1},{13,5},{2,10},{6,14},... | collective-permute-start | bytes 491528 | tf_op jit(solution)/shard_map/ppermute | solution.py:366
  16.5 2.6 %collective-permute-start.7 = (bf16[80,512]{1,0:T(8,128)(2,1)S(1)}, bf16[80,512]{1,0:T(8,128)(2,1)S(1)}, u32[]{:S(2)}, u32[]{:S(2)}) collective-permute-start(bf16[80,512]{1,0:T(8,128)(2,1)S(1)} %get-tuple-element.69), channel_id=1, source_target_pairs={{0,1},{1,0},{2,3},{3,2},{4,5},{5,4},{6,7},{7,6},{8,9},{9,8},{10,11... | collective-permute-start | bytes 245768 | tf_op jit(solution)/shard_map/ppermute | solution.py:335
  16.6 2.5 %collective-permute-start.6 = (bf16[80,384]{1,0:T(8,128)(2,1)S(1)}, bf16[80,384]{1,0:T(8,128)(2,1)S(1)}, u32[]{:S(2)}, u32[]{:S(2)}) collective-permute-start(bf16[80,384]{1,0:T(8,128)(2,1)S(1)} %get-tuple-element.68), channel_id=1, source_target_pairs={{0,1},{1,0},{2,3},{3,2},{4,5},{5,4},{6,7},{7,6},{8,9},{9,8},{10,11... | collective-permute-start | bytes 184328 | tf_op jit(solution)/shard_map/ppermute | solution.py:335
  17.1 12.0 %collective-permute-start.4 = (bf16[80,1024]{1,0:T(8,128)(2,1)S(1)}, bf16[80,1024]{1,0:T(8,128)(2,1)S(1)}, u32[]{:S(2)}, u32[]{:S(2)}) collective-permute-start(bf16[80,1024]{1,0:T(8,128)(2,1)S(1)} %get-tuple-element.64), channel_id=1, source_target_pairs={{0,4},{4,0},{8,12},{12,8},{1,5},{5,1},{9,13},{13,9},{2,6},{6,2},{1... | collective-permute-start | bytes 491528 | tf_op jit(solution)/shard_map/ppermute | solution.py:366
  19.3 7.9 %collective-permute-start.10 = (bf16[80,896]{1,0:T(8,128)(2,1)S(1)}, bf16[80,896]{1,0:T(8,128)(2,1)S(1)}, u32[]{:S(2)}, u32[]{:S(2)}) collective-permute-start(bf16[80,896]{1,0:T(8,128)(2,1)S(1)} %get-tuple-element.74), channel_id=1, source_target_pairs={{0,2},{2,0},{1,3},{3,1},{4,6},{6,4},{5,7},{7,5},{8,10},{10,8},{9,1... | collective-permute-start | bytes 430088 | tf_op jit(solution)/shard_map/ppermute | solution.py:335
  23.8 3.6 %collective-permute-start.9 = (bf16[80,512]{1,0:T(8,128)(2,1)S(1)}, bf16[80,512]{1,0:T(8,128)(2,1)S(1)}, u32[]{:S(2)}, u32[]{:S(2)}) collective-permute-start(bf16[80,512]{1,0:T(8,128)(2,1)S(1)} %get-tuple-element.73), channel_id=1, source_target_pairs={{0,1},{1,0},{2,3},{3,2},{4,5},{5,4},{6,7},{7,6},{8,9},{9,8},{10,11... | collective-permute-start | bytes 245768 | tf_op jit(solution)/shard_map/ppermute | solution.py:335
  23.9 3.5 %collective-permute-start.8 = (bf16[80,384]{1,0:T(8,128)(2,1)S(1)}, bf16[80,384]{1,0:T(8,128)(2,1)S(1)}, u32[]{:S(2)}, u32[]{:S(2)}) collective-permute-start(bf16[80,384]{1,0:T(8,128)(2,1)S(1)} %get-tuple-element.72), channel_id=1, source_target_pairs={{0,1},{1,0},{2,3},{3,2},{4,5},{5,4},{6,7},{7,6},{8,9},{9,8},{10,11... | collective-permute-start | bytes 184328 | tf_op jit(solution)/shard_map/ppermute | solution.py:335
  24.4 8.1 %collective-permute-start.14 = (bf16[80,1024]{1,0:T(8,128)(2,1)S(1)}, bf16[80,1024]{1,0:T(8,128)(2,1)S(1)}, u32[]{:S(2)}, u32[]{:S(2)}) collective-permute-start(bf16[80,1024]{1,0:T(8,128)(2,1)S(1)} %get-tuple-element.82), channel_id=1, source_target_pairs={{0,12},{4,8},{8,4},{12,0},{1,13},{5,9},{9,5},{13,1},{2,14},{6,10},... | collective-permute-start | bytes 491528 | tf_op jit(solution)/shard_map/ppermute | solution.py:366
  27.6 5.6 %collective-permute-start.18 = (bf16[80,896]{1,0:T(8,128)(2,1)S(1)}, bf16[80,896]{1,0:T(8,128)(2,1)S(1)}, u32[]{:S(2)}, u32[]{:S(2)}) collective-permute-start(bf16[80,896]{1,0:T(8,128)(2,1)S(1)} %get-tuple-element.87), channel_id=1, source_target_pairs={{0,2},{2,0},{1,3},{3,1},{4,6},{6,4},{5,7},{7,5},{8,10},{10,8},{9,1... | collective-permute-start | bytes 430088 | tf_op jit(solution)/shard_map/ppermute | solution.py:335
  29.7 1.5 %collective-permute-start.12 = (bf16[96,512]{1,0:T(8,128)(2,1)S(1)}, bf16[96,512]{1,0:T(8,128)(2,1)S(1)}, u32[]{:S(2)}, u32[]{:S(2)}) collective-permute-start(bf16[96,512]{1,0:T(8,128)(2,1)S(1)} %get-tuple-element.78), channel_id=1, source_target_pairs={{0,1},{1,0},{2,3},{3,2},{4,5},{5,4},{6,7},{7,6},{8,9},{9,8},{10,11... | collective-permute-start | bytes 294920 | tf_op jit(solution)/shard_map/ppermute | solution.py:335
  29.8 1.4 %collective-permute-start.11 = (bf16[80,384]{1,0:T(8,128)(2,1)S(1)}, bf16[80,384]{1,0:T(8,128)(2,1)S(1)}, u32[]{:S(2)}, u32[]{:S(2)}) collective-permute-start(bf16[80,384]{1,0:T(8,128)(2,1)S(1)} %get-tuple-element.77), channel_id=1, source_target_pairs={{0,1},{1,0},{2,3},{3,2},{4,5},{5,4},{6,7},{7,6},{8,9},{9,8},{10,11... | collective-permute-start | bytes 184328 | tf_op jit(solution)/shard_map/ppermute | solution.py:335
  31.3 6.7 %collective-permute-start.13 = (bf16[96,896]{1,0:T(8,128)(2,1)S(1)}, bf16[96,896]{1,0:T(8,128)(2,1)S(1)}, u32[]{:S(2)}, u32[]{:S(2)}) collective-permute-start(bf16[96,896]{1,0:T(8,128)(2,1)S(1)} %get-tuple-element.81), channel_id=1, source_target_pairs={{0,2},{2,0},{1,3},{3,1},{4,6},{6,4},{5,7},{7,5},{8,10},{10,8},{9,1... | collective-permute-start | bytes 516104 | tf_op jit(solution)/shard_map/ppermute | solution.py:335
  33.1 2.6 %collective-permute-start.16 = (bf16[80,512]{1,0:T(8,128)(2,1)S(1)}, bf16[80,512]{1,0:T(8,128)(2,1)S(1)}, u32[]{:S(2)}, u32[]{:S(2)}) collective-permute-start(bf16[80,512]{1,0:T(8,128)(2,1)S(1)} %get-tuple-element.85), channel_id=1, source_target_pairs={{0,1},{1,0},{2,3},{3,2},{4,5},{5,4},{6,7},{7,6},{8,9},{9,8},{10,11... | collective-permute-start | bytes 245768 | tf_op jit(solution)/shard_map/ppermute | solution.py:335
  33.4 1.5 %collective-permute-start.19 = (bf16[80,384]{1,0:T(8,128)(2,1)S(1)}, bf16[80,384]{1,0:T(8,128)(2,1)S(1)}, u32[]{:S(2)}, u32[]{:S(2)}) collective-permute-start(bf16[80,384]{1,0:T(8,128)(2,1)S(1)} %shard_map.121.refs_2_.refs_4_), channel_id=1, source_target_pairs={{0,1},{1,0},{2,3},{3,2},{4,5},{5,4},{6,7},{7,6},{8,9},{9,8},{10,11... | collective-permute-start | bytes 184328 | tf_op jit(solution)/shard_map/ppermute | solution.py:335
  34.0 1.7 %collective-permute-start.15 = (bf16[80,384]{1,0:T(8,128)(2,1)S(1)}, bf16[80,384]{1,0:T(8,128)(2,1)S(1)}, u32[]{:S(2)}, u32[]{:S(2)}) collective-permute-start(bf16[80,384]{1,0:T(8,128)(2,1)S(1)} %get-tuple-element.84), channel_id=1, source_target_pairs={{0,1},{1,0},{2,3},{3,2},{4,5},{5,4},{6,7},{7,6},{8,9},{9,8},{10,11... | collective-permute-start | bytes 184328 | tf_op jit(solution)/shard_map/ppermute | solution.py:335
  35.9 6.1 %collective-permute-start.22 = (bf16[80,896]{1,0:T(8,128)(2,1)S(1)}, bf16[80,896]{1,0:T(8,128)(2,1)S(1)}, u32[]{:S(2)}, u32[]{:S(2)}) collective-permute-start(bf16[80,896]{1,0:T(8,128)(2,1)S(1)} %get-tuple-element.94), channel_id=1, source_target_pairs={{0,2},{2,0},{1,3},{3,1},{4,6},{6,4},{5,7},{7,5},{8,10},{10,8},{9,1... | collective-permute-start | bytes 430088 | tf_op jit(solution)/shard_map/ppermute | solution.py:335
  37.6 10.7 %collective-permute-start.21 = (bf16[80,1024]{1,0:T(8,128)(2,1)S(1)}, bf16[80,1024]{1,0:T(8,128)(2,1)S(1)}, u32[]{:S(2)}, u32[]{:S(2)}) collective-permute-start(bf16[80,1024]{1,0:T(8,128)(2,1)S(1)} %shard_map.122.refs_4_), channel_id=1, source_target_pairs={{0,8},{4,12},{8,0},{12,4},{1,9},{5,13},{9,1},{13,5},{2,10},{6,14},... | collective-permute-start | bytes 491528 | tf_op jit(solution)/shard_map/ppermute | solution.py:366
  42.2 6.4 %collective-permute-start.24 = (bf16[80,384]{1,0:T(8,128)(2,1)S(1)}, bf16[80,384]{1,0:T(8,128)(2,1)S(1)}, u32[]{:S(2)}, u32[]{:S(2)}) collective-permute-start(bf16[80,384]{1,0:T(8,128)(2,1)S(1)} %shard_map.129.refs_3_.refs_2_), channel_id=1, source_target_pairs={{0,1},{1,0},{2,3},{3,2},{4,5},{5,4},{6,7},{7,6},{8,9},{9,8},{10,11... | collective-permute-start | bytes 184328 | tf_op jit(solution)/shard_map/ppermute | solution.py:335
  42.2 9.2 %collective-permute-start.23 = (bf16[80,1024]{1,0:T(8,128)(2,1)S(1)}, bf16[80,1024]{1,0:T(8,128)(2,1)S(1)}, u32[]{:S(2)}, u32[]{:S(2)}) collective-permute-start(bf16[80,1024]{1,0:T(8,128)(2,1)S(1)} %shard_map.127.refs_3_), channel_id=1, source_target_pairs={{0,4},{4,0},{8,12},{12,8},{1,5},{5,1},{9,13},{13,9},{2,6},{6,2},{1... | collective-permute-start | bytes 491528 | tf_op jit(solution)/shard_map/ppermute | solution.py:366
  49.0 7.2 %collective-permute-start.25 = (bf16[80,1024]{1,0:T(8,128)(2,1)S(1)}, bf16[80,1024]{1,0:T(8,128)(2,1)S(1)}, u32[]{:S(2)}, u32[]{:S(2)}) collective-permute-start(bf16[80,1024]{1,0:T(8,128)(2,1)S(1)} %shard_map.131.refs_3_), channel_id=1, source_target_pairs={{0,12},{4,8},{8,4},{12,0},{1,13},{5,9},{9,5},{13,1},{2,14},{6,10},... | collective-permute-start | bytes 491528 | tf_op jit(solution)/shard_map/ppermute | solution.py:366
  (2 other events, 2.6 us)

commit v5 on v4

--- a/solution.py
+++ b/solution.py
@@ -273,14 +273,16 @@
         total_ref[...] = stats_ref[...] + get_stats(got_ref, count, stats_ref)
 
 
-def down_kernel(rep_ref, down_ref, mine_ref, other_ref, out_ref):
+def down_kernel(rep_ref, down_ref, mine_ref, other_ref, out_ref, inner):
     half = mine_ref.shape[1]
-    mine = pl.multiple_of(rep_ref[0] * half, LANES)
-    other = pl.multiple_of((1 - rep_ref[0]) * half, LANES)
-    out_ref[...] = (
-        dot(mine_ref[...], down_ref[pl.ds(mine, half), :])
-        + dot(other_ref[...], down_ref[pl.ds(other, half), :])
-    ).astype(BF16)
+    for i in range(2):
+
+        @pl.when(rep_ref[0] == i)
+        def _():
+            inner[:, i * half : (i + 1) * half] = mine_ref[...]
+            inner[:, (1 - i) * half : (2 - i) * half] = other_ref[...]
+
+    out_ref[...] = dot(inner[...], down_ref[...]).astype(BF16)
 
 
 def gates_kernel(cap, features, place_ref, stats_ref, ids_ref, target_ref, *weight_refs):
@@ -432,8 +434,10 @@
     state = {}
     made = {"last": hidden, "stats": stats, "partial": hidden}
 
-    def run(body, out_shape, scalars, arrays, held=True):
-        outs = vmem_call(body, out_shape, scalars, arrays, after=[made["last"]], held=held)
+    def run(body, out_shape, scalars, arrays, scratch=(), held=True):
+        outs = vmem_call(
+            body, out_shape, scalars, arrays, after=[made["last"]], scratch=scratch, held=held
+        )
         made["last"] = outs[0] if isinstance(outs, (tuple, list)) else outs
         return outs
 
@@ -480,7 +484,13 @@
         state[j] = (inner, swap(inner, "rep"))
 
     def down_step(j):
-        answer = run(down_kernel, jax.ShapeDtypeStruct((cap, width), BF16), [side], [down, *state[j]])
+        answer = run(
+            down_kernel,
+            jax.ShapeDtypeStruct((cap, width), BF16),
+            [side],
+            [down, *state[j]],
+            scratch=[pltpu.VMEM((cap, hid), BF16)],
+        )
         state[j] = exchange(answer, j) if j else answer
 
     def gates_step():
@@ -502,8 +512,8 @@
 
     steps = dict(u=up_step, a=add_step, i=inner_step, d=down_step, m=lambda j: mix_step([j]))
     plan = (
-        *("u0", "a0", "u1", "i0", "a1", "u2", "a2", "u3", "i1", "d1"),
-        *("d0", "a3", "i2", "g", "d2", "m0", "i3", "m1", "d3", "m2"),
+        *("u0", "a0", "u1", "i0", "a1", "u2", "a2", "u3", "i1", "d0"),
+        *("d1", "a3", "i2", "d2", "g", "m0", "i3", "m1", "d3", "m2"),
     )
     for name in plan:
         if name == "g":

time: 57.4 us -> 57.1 us (level)
  waiting for transfers between devices: 19.1 us -> 18.3 us
  transfers between devices with their start and end apart: 26 -> 26, of which waited for: 12 -> 13; matrix products, arithmetic and copies ran while one was open for 0% -> 0% of each run, Pallas kernels for 17% -> 17%
where the time goes in v5:
time: 57.1 us; the launch traced here: 56.9 us
  starting transfers between devices  25.1 us (44%)
  waiting for transfers between devices  18.3 us (32%)
  Pallas kernels  13.2 us (23%)
    pallas_call x25, Pallas kernels, vmem_call(): pl.pallas_call(kernel, out_shape=[placed(x) for x in out_shape] if multi...  13.2 us
    ppermute x7, waiting for transfers between devices, exchange(): return lax.ppermute(x, 'ctx', [(i, i ^ j) for i in range(n)])  12.8 us
    ppermute x7, starting transfers between devices, exchange(): return lax.ppermute(x, 'ctx', [(i, i ^ j) for i in range(n)])  12.3 us
    ppermute x18, starting transfers between devices, swap(): return lax.ppermute(x, axis, [(0, 1), (1, 0)])  8.7 us
    ppermute x1, starting transfers between devices, direct(): lax.ppermute(own_kv, ('ctx', 'rep'), [(2 * i + r, 2 * (i ^ 2 + r) + r) fo...  4.1 us
    ppermute x18, waiting for transfers between devices, swap(): return lax.ppermute(x, axis, [(0, 1), (1, 0)])  3.36 us
    ppermute x1, waiting for transfers between devices, direct(): lax.ppermute(own_kv, ('ctx', 'rep'), [(2 * i + r, 2 * (i ^ 2 + r) + r) fo...  2.19 us
  transfers between devices with their start and end apart: 26, of which 13 were waited for; matrix products, arithmetic and copies ran while one was open for 0% of the time, Pallas kernels for 17%

profile of v5, /device:TPU:0, one launch (start us, length us, event | category | flops | bytes accessed | tf_op | source)
XLA Modules:
  0.0 56.9 jit_solution(1791912988614163784)
XLA Ops:
  0.0 0.8 %shard_map.109 = (bf16[128,256]{1,0:T(8,128)(2,1)S(1)}, bf16[128,128]{1,0:T(8,128)(2,1)S(1)}) custom-call(s32[1]{0:T(128)} %bitcast.8.refs_0_, s32[1]{0:T(128)} %bitcast.1.refs_1_.refs_0_, bf16[128,256]{1,0:T(8,128)(2,1)} %refs_2_.1, bf16[128,256]{1,0:T(8,128)(2,1)} %refs_3_.1), custom_call_target="tpu_custom_call" | custom-call | flops 1 | bytes 1 | tf_op jit(solution)/shard_map/pallas_call | solution.py:44
  0.8 4.1 %collective-permute-start.2 = (bf16[128,256]{1,0:T(8,128)(2,1)S(1)}, bf16[128,256]{1,0:T(8,128)(2,1)S(1)}, u32[]{:S(2)}, u32[]{:S(2)}) collective-permute-start(bf16[128,256]{1,0:T(8,128)(2,1)S(1)} %get-tuple-element.56.refs_8_), channel_id=1, source_target_pairs={{0,8},{1,13},{4,12},{5,9},{8,0},{9,5},{12,4},{13,1},{2,10},{3,15},... | collective-permute-start | bytes 196616 | tf_op jit(solution)/shard_map/ppermute | solution.py:393
  4.9 1.6 %collective-permute-start = (bf16[128,128]{1,0:T(8,128)(2,1)S(1)}, bf16[128,128]{1,0:T(8,128)(2,1)S(1)}, u32[]{:S(2)}, u32[]{:S(2)}) collective-permute-start(bf16[128,128]{1,0:T(8,128)(2,1)S(1)} %get-tuple-element.51.refs_6_), channel_id=1, source_target_pairs={{0,4},{4,0},{8,12},{12,8},{1,5},{5,1},{9,13},{13,9},{2,6},{6,2},{1... | collective-permute-start | bytes 98312 | tf_op jit(solution)/shard_map/ppermute | solution.py:368
  6.5 2.2 %collective-permute-done.2.refs_11_ = bf16[128,256]{1,0:T(8,128)(2,1)S(1)} collective-permute-done((bf16[128,256]{1,0:T(8,128)(2,1)S(1)}, bf16[128,256]{1,0:T(8,128)(2,1)S(1)}, u32[]{:S(2)}, u32[]{:S(2)}) %collective-permute-start.2) | collective-permute-done | bytes 65568 | tf_op jit(solution)/shard_map/ppermute | solution.py:393
  9.2 1.2 %shard_map.110 = (bf16[128,1024]{1,0:T(8,128)(2,1)S(1)}, bf16[128,1024]{1,0:T(8,128)(2,1)S(1)}, bf16[8,128]{1,0:T(8,128)(2,1)S(1)}, bf16[4,1024]{1,0:T(4,128)(2,...) custom-call(bf16[128,1024]{1,0:T(8,128)(2,1)} %refs_0_.1, bf16[128,1024]{1,0:T(8,128)(2,1)} %refs_1_.1, ...), custom_call_target="tpu_custom_call" | custom-call | flops 1 | bytes 1 | tf_op jit(solution)/shard_map/pallas_call | solution.py:44
  10.4 1.9 %shard_map.111 = (f32[128,1024]{1,0:T(8,128)S(1)}, bf16[128,1024]{1,0:T(8,128)(2,1)S(1)}, f32[128,128]{1,0:T(8,128)S(1)}, bf16[80,1024]{1,0:T(8,128)(2,1)S(1)}, ...) custom-call(s32[1]{0:T(128)} %bitcast.refs_0_, s32[1]{0:T(128)} %bitcast.1.refs_1_.refs_0_, ...), custom_call_target="tpu_custom_call" | custom-call | flops 1 | bytes 1 | tf_op jit(solution)/shard_map/pallas_call | solution.py:44
  12.3 2.2 %collective-permute-start.5 = (bf16[80,1024]{1,0:T(8,128)(2,1)S(1)}, bf16[80,1024]{1,0:T(8,128)(2,1)S(1)}, u32[]{:S(2)}, u32[]{:S(2)}) collective-permute-start(bf16[80,1024]{1,0:T(8,128)(2,1)S(1)} %get-tuple-element.65), channel_id=1, source_target_pairs={{0,8},{4,12},{8,0},{12,4},{1,9},{5,13},{9,1},{13,5},{2,10},{6,14},... | collective-permute-start | bytes 491528 | tf_op jit(solution)/shard_map/ppermute | solution.py:368
  14.5 1.4 %shard_map.112 = (bf16[80,1024]{1,0:T(8,128)(2,1)S(1)}, bf16[80,1024]{1,0:T(8,128)(2,1)S(1)}, bf16[80,1024]{1,0:T(8,128)(2,1)S(1)}, f32[8,128]{1,0:T(8,128)S(1)}, bf16[768,1024]{1,0:T(8,128)(2,1)S(1)}) custom-call(s32[1]{0:T(128)} %bitcast.refs_0_, bf16[768,1024]{1,0:T(8,128)(2,1)} %bitcast.12, bf16[128,1024]{1,0:T(8,128)(2,1)S(1)} %get-tuple-element.58.refs_2_, ...), custom_call_target="tpu_custom_call" | custom-call | flops 1 | bytes 1 | tf_op jit(solution)/shard_map/pallas_call | solution.py:44
  17.1 2.0 %collective-permute-start.4 = (bf16[80,1024]{1,0:T(8,128)(2,1)S(1)}, bf16[80,1024]{1,0:T(8,128)(2,1)S(1)}, u32[]{:S(2)}, u32[]{:S(2)}) collective-permute-start(bf16[80,1024]{1,0:T(8,128)(2,1)S(1)} %get-tuple-element.64), channel_id=1, source_target_pairs={{0,4},{4,0},{8,12},{12,8},{1,5},{5,1},{9,13},{13,9},{2,6},{6,2},{1... | collective-permute-start | bytes 491528 | tf_op jit(solution)/shard_map/ppermute | solution.py:368
  19.3 1.6 %collective-permute-start.10 = (bf16[80,896]{1,0:T(8,128)(2,1)S(1)}, bf16[80,896]{1,0:T(8,128)(2,1)S(1)}, u32[]{:S(2)}, u32[]{:S(2)}) collective-permute-start(bf16[80,896]{1,0:T(8,128)(2,1)S(1)} %get-tuple-element.74), channel_id=1, source_target_pairs={{0,2},{2,0},{1,3},{3,1},{4,6},{6,4},{5,7},{7,5},{8,10},{10,8},{9,1... | collective-permute-start | bytes 430088 | tf_op jit(solution)/shard_map/ppermute | solution.py:337
  20.8 2.4 %collective-permute-done.5.refs_4_ = bf16[80,1024]{1,0:T(8,128)(2,1)S(1)} collective-permute-done((bf16[80,1024]{1,0:T(8,128)(2,1)S(1)}, bf16[80,1024]{1,0:T(8,128)(2,1)S(1)}, u32[]{:S(2)}, u32[]{:S(2)}) %collective-permute-start.5) | collective-permute-done | bytes 163872 | tf_op jit(solution)/shard_map/ppermute | solution.py:368
  24.4 2.8 %collective-permute-start.14 = (bf16[80,1024]{1,0:T(8,128)(2,1)S(1)}, bf16[80,1024]{1,0:T(8,128)(2,1)S(1)}, u32[]{:S(2)}, u32[]{:S(2)}) collective-permute-start(bf16[80,1024]{1,0:T(8,128)(2,1)S(1)} %get-tuple-element.82), channel_id=1, source_target_pairs={{0,12},{4,8},{8,4},{12,0},{1,13},{5,9},{9,5},{13,1},{2,14},{6,10},... | collective-permute-start | bytes 491528 | tf_op jit(solution)/shard_map/ppermute | solution.py:368
  27.6 1.6 %collective-permute-start.17 = (bf16[80,896]{1,0:T(8,128)(2,1)S(1)}, bf16[80,896]{1,0:T(8,128)(2,1)S(1)}, u32[]{:S(2)}, u32[]{:S(2)}) collective-permute-start(bf16[80,896]{1,0:T(8,128)(2,1)S(1)} %get-tuple-element.87), channel_id=1, source_target_pairs={{0,2},{2,0},{1,3},{3,1},{4,6},{6,4},{5,7},{7,5},{8,10},{10,8},{9,1... | collective-permute-start | bytes 430088 | tf_op jit(solution)/shard_map/ppermute | solution.py:337
  30.3 0.9 %collective-permute-done.11.refs_2_ = bf16[80,384]{1,0:T(8,128)(2,1)S(1)} collective-permute-done((bf16[80,384]{1,0:T(8,128)(2,1)S(1)}, bf16[80,384]{1,0:T(8,128)(2,1)S(1)}, u32[]{:S(2)}, u32[]{:S(2)}) %collective-permute-start.11) | collective-permute-done | bytes 61472 | tf_op jit(solution)/shard_map/ppermute | solution.py:337
  35.8 1.7 %collective-permute-start.22 = (bf16[80,896]{1,0:T(8,128)(2,1)S(1)}, bf16[80,896]{1,0:T(8,128)(2,1)S(1)}, u32[]{:S(2)}, u32[]{:S(2)}) collective-permute-start(bf16[80,896]{1,0:T(8,128)(2,1)S(1)} %get-tuple-element.94), channel_id=1, source_target_pairs={{0,2},{2,0},{1,3},{3,1},{4,6},{6,4},{5,7},{7,5},{8,10},{10,8},{9,1... | collective-permute-start | bytes 430088 | tf_op jit(solution)/shard_map/ppermute | solution.py:337
  38.3 1.2 %collective-permute-done.20.refs_3_ = bf16[80,384]{1,0:T(8,128)(2,1)S(1)} collective-permute-done((bf16[80,384]{1,0:T(8,128)(2,1)S(1)}, bf16[80,384]{1,0:T(8,128)(2,1)S(1)}, u32[]{:S(2)}, u32[]{:S(2)}) %collective-permute-start.20) | collective-permute-done | bytes 61472 | tf_op jit(solution)/shard_map/ppermute | solution.py:337
  40.0 0.7 %shard_map.127 = (bf16[256,80]{1,0:T(8,128)(2,1)S(1)}, bf16[256,80]{1,0:T(8,128)(2,1)S(1)}, bf16[256,80]{1,0:T(8,128)(2,1)S(1)}, bf16[256,80]{1,0:T(8,128)(2,1)S(1)}) custom-call(s32[1]{0:T(128)} %bitcast.refs_0_, f32[8,128]{1,0:T(8,128)S(1)} %get-tuple-element.89.refs_1_, s32[2,128]{1,0:T(2,128)S(1)} %get-tuple-element.90.refs_2_, ...), custom_call_target="tpu_custom_call" | custom-call | flops 1 | bytes 1 | tf_op jit(solution)/shard_map/pallas_call | solution.py:44
  41.0 0.7 %collective-permute-done.22.refs_1_ = bf16[80,896]{1,0:T(8,128)(2,1)S(1)} collective-permute-done((bf16[80,896]{1,0:T(8,128)(2,1)S(1)}, bf16[80,896]{1,0:T(8,128)(2,1)S(1)}, u32[]{:S(2)}, u32[]{:S(2)}) %collective-permute-start.22) | collective-permute-done | bytes 143392 | tf_op jit(solution)/shard_map/ppermute | solution.py:337
  42.0 2.0 %collective-permute-start.23 = (bf16[80,1024]{1,0:T(8,128)(2,1)S(1)}, bf16[80,1024]{1,0:T(8,128)(2,1)S(1)}, u32[]{:S(2)}, u32[]{:S(2)}) collective-permute-start(bf16[80,1024]{1,0:T(8,128)(2,1)S(1)} %shard_map.126.refs_4_), channel_id=1, source_target_pairs={{0,4},{4,0},{8,12},{12,8},{1,5},{5,1},{9,13},{13,9},{2,6},{6,2},{1... | collective-permute-start | bytes 491528 | tf_op jit(solution)/shard_map/ppermute | solution.py:368
  44.0 4.0 %collective-permute-done.21.refs_2_ = bf16[80,1024]{1,0:T(8,128)(2,1)S(1)} collective-permute-done((bf16[80,1024]{1,0:T(8,128)(2,1)S(1)}, bf16[80,1024]{1,0:T(8,128)(2,1)S(1)}, u32[]{:S(2)}, u32[]{:S(2)}) %collective-permute-start.21) | collective-permute-done | bytes 163872 | tf_op jit(solution)/shard_map/ppermute | solution.py:368
  48.7 1.3 %collective-permute-start.25 = (bf16[80,1024]{1,0:T(8,128)(2,1)S(1)}, bf16[80,1024]{1,0:T(8,128)(2,1)S(1)}, u32[]{:S(2)}, u32[]{:S(2)}) collective-permute-start(bf16[80,1024]{1,0:T(8,128)(2,1)S(1)} %shard_map.131.refs_3_), channel_id=1, source_target_pairs={{0,12},{4,8},{8,4},{12,0},{1,13},{5,9},{9,5},{13,1},{2,14},{6,10},... | collective-permute-start | bytes 491528 | tf_op jit(solution)/shard_map/ppermute | solution.py:368
  50.0 1.3 %collective-permute-done.23.refs_2_ = bf16[80,1024]{1,0:T(8,128)(2,1)S(1)} collective-permute-done((bf16[80,1024]{1,0:T(8,128)(2,1)S(1)}, bf16[80,1024]{1,0:T(8,128)(2,1)S(1)}, u32[]{:S(2)}, u32[]{:S(2)}) %collective-permute-start.23) | collective-permute-done | bytes 163872 | tf_op jit(solution)/shard_map/ppermute | solution.py:368
  51.6 4.3 %collective-permute-done.25.refs_2_ = bf16[80,1024]{1,0:T(8,128)(2,1)S(1)} collective-permute-done((bf16[80,1024]{1,0:T(8,128)(2,1)S(1)}, bf16[80,1024]{1,0:T(8,128)(2,1)S(1)}, u32[]{:S(2)}, u32[]{:S(2)}) %collective-permute-start.25) | collective-permute-done | bytes 163872 | tf_op jit(solution)/shard_map/ppermute | solution.py:368
  55.9 1.0 %shard_map.133 = bf16[128,1024]{1,0:T(8,128)(2,1)} custom-call(f32[128,1024]{1,0:T(8,128)S(1)} %shard_map.132.refs_0_.refs_3_, bf16[256,80]{1,0:T(8,128)(2,1)S(1)} %get-tuple-element.96.refs_1_, bf16[80,1024]{1,0:T(8,128)(2,1)S(1)} %collective-permute-done.25.refs_2_, f32[128,1024]{1,0:T(8,128)S(1)} %shard_map.132.refs_0_.refs_3_), custom_call_target="tpu_custom_call" | custom-call | flops 1 | bytes 1 | tf_op jit(solution)/shard_map/pallas_call | solution.py:44
  (53 shorter events, 11.8 us)
Async XLA Ops:
  0.8 7.9 %collective-permute-start.2 = (bf16[128,256]{1,0:T(8,128)(2,1)S(1)}, bf16[128,256]{1,0:T(8,128)(2,1)S(1)}, u32[]{:S(2)}, u32[]{:S(2)}) collective-permute-start(bf16[128,256]{1,0:T(8,128)(2,1)S(1)} %get-tuple-element.56.refs_8_), channel_id=1, source_target_pairs={{0,8},{1,13},{4,12},{5,9},{8,0},{9,5},{12,4},{13,1},{2,10},{3,15},... | collective-permute-start | bytes 196616 | tf_op jit(solution)/shard_map/ppermute | solution.py:393
  4.9 4.0 %collective-permute-start = (bf16[128,128]{1,0:T(8,128)(2,1)S(1)}, bf16[128,128]{1,0:T(8,128)(2,1)S(1)}, u32[]{:S(2)}, u32[]{:S(2)}) collective-permute-start(bf16[128,128]{1,0:T(8,128)(2,1)S(1)} %get-tuple-element.51.refs_6_), channel_id=1, source_target_pairs={{0,4},{4,0},{8,12},{12,8},{1,5},{5,1},{9,13},{13,9},{2,6},{6,2},{1... | collective-permute-start | bytes 98312 | tf_op jit(solution)/shard_map/ppermute | solution.py:368
  8.7 1.7 %collective-permute-start.3 = (bf16[128,256]{1,0:T(8,128)(2,1)S(1)}, bf16[128,256]{1,0:T(8,128)(2,1)S(1)}, u32[]{:S(2)}, u32[]{:S(2)}) collective-permute-start(bf16[128,256]{1,0:T(8,128)(2,1)S(1)} %collective-permute-done.2.refs_11_), channel_id=1, source_target_pairs={{0,1},{1,0},{2,3},{3,2},{4,5},{5,4},{6,7},{7,6},{8,9},{9,8},{10,11... | collective-permute-start | bytes 196616 | tf_op jit(solution)/shard_map/ppermute | solution.py:337
  8.9 1.5 %collective-permute-start.1 = (bf16[128,128]{1,0:T(8,128)(2,1)S(1)}, bf16[128,128]{1,0:T(8,128)(2,1)S(1)}, u32[]{:S(2)}, u32[]{:S(2)}) collective-permute-start(bf16[128,128]{1,0:T(8,128)(2,1)S(1)} %collective-permute-done.refs_9_), channel_id=1, source_target_pairs={{0,1},{1,0},{2,3},{3,2},{4,5},{5,4},{6,7},{7,6},{8,9},{9,8},{10,11... | collective-permute-start | bytes 98312 | tf_op jit(solution)/shard_map/ppermute | solution.py:337
  12.3 10.9 %collective-permute-start.5 = (bf16[80,1024]{1,0:T(8,128)(2,1)S(1)}, bf16[80,1024]{1,0:T(8,128)(2,1)S(1)}, u32[]{:S(2)}, u32[]{:S(2)}) collective-permute-start(bf16[80,1024]{1,0:T(8,128)(2,1)S(1)} %get-tuple-element.65), channel_id=1, source_target_pairs={{0,8},{4,12},{8,0},{12,4},{1,9},{5,13},{9,1},{13,5},{2,10},{6,14},... | collective-permute-start | bytes 491528 | tf_op jit(solution)/shard_map/ppermute | solution.py:368
  16.5 2.6 %collective-permute-start.7 = (bf16[80,512]{1,0:T(8,128)(2,1)S(1)}, bf16[80,512]{1,0:T(8,128)(2,1)S(1)}, u32[]{:S(2)}, u32[]{:S(2)}) collective-permute-start(bf16[80,512]{1,0:T(8,128)(2,1)S(1)} %get-tuple-element.69), channel_id=1, source_target_pairs={{0,1},{1,0},{2,3},{3,2},{4,5},{5,4},{6,7},{7,6},{8,9},{9,8},{10,11... | collective-permute-start | bytes 245768 | tf_op jit(solution)/shard_map/ppermute | solution.py:337
  16.6 2.5 %collective-permute-start.6 = (bf16[80,384]{1,0:T(8,128)(2,1)S(1)}, bf16[80,384]{1,0:T(8,128)(2,1)S(1)}, u32[]{:S(2)}, u32[]{:S(2)}) collective-permute-start(bf16[80,384]{1,0:T(8,128)(2,1)S(1)} %get-tuple-element.68), channel_id=1, source_target_pairs={{0,1},{1,0},{2,3},{3,2},{4,5},{5,4},{6,7},{7,6},{8,9},{9,8},{10,11... | collective-permute-start | bytes 184328 | tf_op jit(solution)/shard_map/ppermute | solution.py:337
  17.1 12.0 %collective-permute-start.4 = (bf16[80,1024]{1,0:T(8,128)(2,1)S(1)}, bf16[80,1024]{1,0:T(8,128)(2,1)S(1)}, u32[]{:S(2)}, u32[]{:S(2)}) collective-permute-start(bf16[80,1024]{1,0:T(8,128)(2,1)S(1)} %get-tuple-element.64), channel_id=1, source_target_pairs={{0,4},{4,0},{8,12},{12,8},{1,5},{5,1},{9,13},{13,9},{2,6},{6,2},{1... | collective-permute-start | bytes 491528 | tf_op jit(solution)/shard_map/ppermute | solution.py:368
  19.3 7.9 %collective-permute-start.10 = (bf16[80,896]{1,0:T(8,128)(2,1)S(1)}, bf16[80,896]{1,0:T(8,128)(2,1)S(1)}, u32[]{:S(2)}, u32[]{:S(2)}) collective-permute-start(bf16[80,896]{1,0:T(8,128)(2,1)S(1)} %get-tuple-element.74), channel_id=1, source_target_pairs={{0,2},{2,0},{1,3},{3,1},{4,6},{6,4},{5,7},{7,5},{8,10},{10,8},{9,1... | collective-permute-start | bytes 430088 | tf_op jit(solution)/shard_map/ppermute | solution.py:337
  23.8 3.6 %collective-permute-start.9 = (bf16[80,512]{1,0:T(8,128)(2,1)S(1)}, bf16[80,512]{1,0:T(8,128)(2,1)S(1)}, u32[]{:S(2)}, u32[]{:S(2)}) collective-permute-start(bf16[80,512]{1,0:T(8,128)(2,1)S(1)} %get-tuple-element.73), channel_id=1, source_target_pairs={{0,1},{1,0},{2,3},{3,2},{4,5},{5,4},{6,7},{7,6},{8,9},{9,8},{10,11... | collective-permute-start | bytes 245768 | tf_op jit(solution)/shard_map/ppermute | solution.py:337
  23.9 3.5 %collective-permute-start.8 = (bf16[80,384]{1,0:T(8,128)(2,1)S(1)}, bf16[80,384]{1,0:T(8,128)(2,1)S(1)}, u32[]{:S(2)}, u32[]{:S(2)}) collective-permute-start(bf16[80,384]{1,0:T(8,128)(2,1)S(1)} %get-tuple-element.72), channel_id=1, source_target_pairs={{0,1},{1,0},{2,3},{3,2},{4,5},{5,4},{6,7},{7,6},{8,9},{9,8},{10,11... | collective-permute-start | bytes 184328 | tf_op jit(solution)/shard_map/ppermute | solution.py:337
  24.4 8.1 %collective-permute-start.14 = (bf16[80,1024]{1,0:T(8,128)(2,1)S(1)}, bf16[80,1024]{1,0:T(8,128)(2,1)S(1)}, u32[]{:S(2)}, u32[]{:S(2)}) collective-permute-start(bf16[80,1024]{1,0:T(8,128)(2,1)S(1)} %get-tuple-element.82), channel_id=1, source_target_pairs={{0,12},{4,8},{8,4},{12,0},{1,13},{5,9},{9,5},{13,1},{2,14},{6,10},... | collective-permute-start | bytes 491528 | tf_op jit(solution)/shard_map/ppermute | solution.py:368
  27.6 6.1 %collective-permute-start.17 = (bf16[80,896]{1,0:T(8,128)(2,1)S(1)}, bf16[80,896]{1,0:T(8,128)(2,1)S(1)}, u32[]{:S(2)}, u32[]{:S(2)}) collective-permute-start(bf16[80,896]{1,0:T(8,128)(2,1)S(1)} %get-tuple-element.87), channel_id=1, source_target_pairs={{0,2},{2,0},{1,3},{3,1},{4,6},{6,4},{5,7},{7,5},{8,10},{10,8},{9,1... | collective-permute-start | bytes 430088 | tf_op jit(solution)/shard_map/ppermute | solution.py:337
  29.7 1.5 %collective-permute-start.12 = (bf16[96,512]{1,0:T(8,128)(2,1)S(1)}, bf16[96,512]{1,0:T(8,128)(2,1)S(1)}, u32[]{:S(2)}, u32[]{:S(2)}) collective-permute-start(bf16[96,512]{1,0:T(8,128)(2,1)S(1)} %get-tuple-element.78), channel_id=1, source_target_pairs={{0,1},{1,0},{2,3},{3,2},{4,5},{5,4},{6,7},{7,6},{8,9},{9,8},{10,11... | collective-permute-start | bytes 294920 | tf_op jit(solution)/shard_map/ppermute | solution.py:337
  29.8 1.4 %collective-permute-start.11 = (bf16[80,384]{1,0:T(8,128)(2,1)S(1)}, bf16[80,384]{1,0:T(8,128)(2,1)S(1)}, u32[]{:S(2)}, u32[]{:S(2)}) collective-permute-start(bf16[80,384]{1,0:T(8,128)(2,1)S(1)} %get-tuple-element.77), channel_id=1, source_target_pairs={{0,1},{1,0},{2,3},{3,2},{4,5},{5,4},{6,7},{7,6},{8,9},{9,8},{10,11... | collective-permute-start | bytes 184328 | tf_op jit(solution)/shard_map/ppermute | solution.py:337
  31.3 6.7 %collective-permute-start.13 = (bf16[96,896]{1,0:T(8,128)(2,1)S(1)}, bf16[96,896]{1,0:T(8,128)(2,1)S(1)}, u32[]{:S(2)}, u32[]{:S(2)}) collective-permute-start(bf16[96,896]{1,0:T(8,128)(2,1)S(1)} %get-tuple-element.81), channel_id=1, source_target_pairs={{0,2},{2,0},{1,3},{3,1},{4,6},{6,4},{5,7},{7,5},{8,10},{10,8},{9,1... | collective-permute-start | bytes 516104 | tf_op jit(solution)/shard_map/ppermute | solution.py:337
  33.1 2.5 %collective-permute-start.16 = (bf16[80,512]{1,0:T(8,128)(2,1)S(1)}, bf16[80,512]{1,0:T(8,128)(2,1)S(1)}, u32[]{:S(2)}, u32[]{:S(2)}) collective-permute-start(bf16[80,512]{1,0:T(8,128)(2,1)S(1)} %get-tuple-element.85), channel_id=1, source_target_pairs={{0,1},{1,0},{2,3},{3,2},{4,5},{5,4},{6,7},{7,6},{8,9},{9,8},{10,11... | collective-permute-start | bytes 245768 | tf_op jit(solution)/shard_map/ppermute | solution.py:337
  33.2 1.4 %collective-permute-start.19 = (bf16[80,384]{1,0:T(8,128)(2,1)S(1)}, bf16[80,384]{1,0:T(8,128)(2,1)S(1)}, u32[]{:S(2)}, u32[]{:S(2)}) collective-permute-start(bf16[80,384]{1,0:T(8,128)(2,1)S(1)} %shard_map.116.refs_3_.refs_2_), channel_id=1, source_target_pairs={{0,1},{1,0},{2,3},{3,2},{4,5},{5,4},{6,7},{7,6},{8,9},{9,8},{10,11... | collective-permute-start | bytes 184328 | tf_op jit(solution)/shard_map/ppermute | solution.py:337
  34.1 1.6 %collective-permute-start.15 = (bf16[80,384]{1,0:T(8,128)(2,1)S(1)}, bf16[80,384]{1,0:T(8,128)(2,1)S(1)}, u32[]{:S(2)}, u32[]{:S(2)}) collective-permute-start(bf16[80,384]{1,0:T(8,128)(2,1)S(1)} %get-tuple-element.84), channel_id=1, source_target_pairs={{0,1},{1,0},{2,3},{3,2},{4,5},{5,4},{6,7},{7,6},{8,9},{9,8},{10,11... | collective-permute-start | bytes 184328 | tf_op jit(solution)/shard_map/ppermute | solution.py:337
  35.8 5.9 %collective-permute-start.22 = (bf16[80,896]{1,0:T(8,128)(2,1)S(1)}, bf16[80,896]{1,0:T(8,128)(2,1)S(1)}, u32[]{:S(2)}, u32[]{:S(2)}) collective-permute-start(bf16[80,896]{1,0:T(8,128)(2,1)S(1)} %get-tuple-element.94), channel_id=1, source_target_pairs={{0,2},{2,0},{1,3},{3,1},{4,6},{6,4},{5,7},{7,5},{8,10},{10,8},{9,1... | collective-permute-start | bytes 430088 | tf_op jit(solution)/shard_map/ppermute | solution.py:337
  37.5 10.5 %collective-permute-start.21 = (bf16[80,1024]{1,0:T(8,128)(2,1)S(1)}, bf16[80,1024]{1,0:T(8,128)(2,1)S(1)}, u32[]{:S(2)}, u32[]{:S(2)}) collective-permute-start(bf16[80,1024]{1,0:T(8,128)(2,1)S(1)} %shard_map.123.refs_3_), channel_id=1, source_target_pairs={{0,8},{4,12},{8,0},{12,4},{1,9},{5,13},{9,1},{13,5},{2,10},{6,14},... | collective-permute-start | bytes 491528 | tf_op jit(solution)/shard_map/ppermute | solution.py:368
  41.9 6.4 %collective-permute-start.24 = (bf16[80,384]{1,0:T(8,128)(2,1)S(1)}, bf16[80,384]{1,0:T(8,128)(2,1)S(1)}, u32[]{:S(2)}, u32[]{:S(2)}) collective-permute-start(bf16[80,384]{1,0:T(8,128)(2,1)S(1)} %shard_map.129.refs_3_.refs_2_), channel_id=1, source_target_pairs={{0,1},{1,0},{2,3},{3,2},{4,5},{5,4},{6,7},{7,6},{8,9},{9,8},{10,11... | collective-permute-start | bytes 184328 | tf_op jit(solution)/shard_map/ppermute | solution.py:337
  42.0 9.3 %collective-permute-start.23 = (bf16[80,1024]{1,0:T(8,128)(2,1)S(1)}, bf16[80,1024]{1,0:T(8,128)(2,1)S(1)}, u32[]{:S(2)}, u32[]{:S(2)}) collective-permute-start(bf16[80,1024]{1,0:T(8,128)(2,1)S(1)} %shard_map.126.refs_4_), channel_id=1, source_target_pairs={{0,4},{4,0},{8,12},{12,8},{1,5},{5,1},{9,13},{13,9},{2,6},{6,2},{1... | collective-permute-start | bytes 491528 | tf_op jit(solution)/shard_map/ppermute | solution.py:368
  48.7 7.2 %collective-permute-start.25 = (bf16[80,1024]{1,0:T(8,128)(2,1)S(1)}, bf16[80,1024]{1,0:T(8,128)(2,1)S(1)}, u32[]{:S(2)}, u32[]{:S(2)}) collective-permute-start(bf16[80,1024]{1,0:T(8,128)(2,1)S(1)} %shard_map.131.refs_3_), channel_id=1, source_target_pairs={{0,12},{4,8},{8,4},{12,0},{1,13},{5,9},{9,5},{13,1},{2,14},{6,10},... | collective-permute-start | bytes 491528 | tf_op jit(solution)/shard_map/ppermute | solution.py:368
  (2 other events, 2.6 us)

commit v6 on v5

--- a/solution.py
+++ b/solution.py
@@ -48,7 +48,7 @@
         + [pl.BlockSpec(memory_space=pltpu.HBM)] * len(remote)
         + [whole] * len(arrays)
         + [anywhere] * len(after),
-        out_specs=[whole] * n_out if multi else whole,
+        out_specs=[whole] * n_out if multi else (whole if held else anywhere),
         scratch_shapes=list(scratch),
         compiler_params=pltpu.CompilerParams(vmem_limit_bytes=VMEM_LIMIT),
         cost_estimate=pl.CostEstimate(flops=1, bytes_accessed=1, transcendentals=0),
@@ -331,6 +331,29 @@
         mixed = dot(weights_ref[...], answer_ref[...])
         total = total + (mixed[:tokens] + mixed[tokens:])
     out_ref[...] = total.astype(out_ref.dtype)
+
+
+def last_kernel(count, partial_ref, *rest):
+    weights, answers, (out_ref, staged, sems) = rest[:count], rest[count : 2 * count], rest[2 * count :]
+    tokens, width = partial_ref.shape
+    pieces = sems.shape[0]
+    span = width // pieces
+    copies = []
+    for i in range(pieces):
+        cols = slice(i * span, (i + 1) * span)
+        total = partial_ref[:, cols]
+        for weights_ref, answer_ref in zip(weights, answers):
+            mixed = dot(weights_ref[...], answer_ref[:, cols])
+            total = total + (mixed[:tokens] + mixed[tokens:])
+        staged[:, cols] = total.astype(BF16)
+        copies.append(
+            pltpu.make_async_copy(
+                staged.at[:, pl.ds(i * span, span)], out_ref.at[:, pl.ds(i * span, span)], sems.at[i]
+            )
+        )
+        copies[-1].start()
+    for copy in copies:
+        copy.wait()
 
 
 def swap(x, axis):
@@ -501,13 +524,15 @@
             [made["stats"], ids_rows, target],
         )
 
-    def mix_step(blocks, dtype=F32, held=True):
+    def mix_step(blocks, last=False):
+        pieces = 2 if width % (2 * LANES) == 0 else 1
         made["partial"] = run(
-            functools.partial(mix_kernel, len(blocks)),
-            jax.ShapeDtypeStruct((tokens, width), dtype),
+            functools.partial(last_kernel if last else mix_kernel, len(blocks)),
+            jax.ShapeDtypeStruct((tokens, width), BF16 if last else F32),
             [],
             [made["partial"]] + [made["weights"][j] for j in blocks] + [state[j] for j in blocks],
-            held=held,
+            scratch=[pltpu.VMEM((tokens, width), BF16), pltpu.SemaphoreType.DMA((pieces,))] if last else (),
+            held=not last,
         )
 
     steps = dict(u=up_step, a=add_step, i=inner_step, d=down_step, m=lambda j: mix_step([j]))
@@ -521,7 +546,7 @@
         elif int(name[1]) < n - (name[0] == "m"):
             steps[name[0]](chain[int(name[1])])
     early = [chain[int(name[1])] for name in plan if name[0] == "m" and int(name[1]) < n - 1]
-    mix_step([j for j in chain if j not in early], BF16, held=False)
+    mix_step([j for j in chain if j not in early], last=True)
     return made["partial"]
 
 

time: 57.1 us -> 57.1 us (level)
  no operation moved by 1% of the time
where the time goes in v6:
time: 57.1 us; the launch traced here: 56.9 us
  starting transfers between devices  25.1 us (44%)
  waiting for transfers between devices  18.3 us (32%)
  Pallas kernels  13.2 us (23%)
    pallas_call x25, Pallas kernels, vmem_call(): pl.pallas_call(kernel, out_shape=[placed(x) for x in out_shape] if multi...  13.2 us
    ppermute x7, waiting for transfers between devices, exchange(): return lax.ppermute(x, 'ctx', [(i, i ^ j) for i in range(n)])  12.8 us
    ppermute x7, starting transfers between devices, exchange(): return lax.ppermute(x, 'ctx', [(i, i ^ j) for i in range(n)])  12.3 us
    ppermute x18, starting transfers between devices, swap(): return lax.ppermute(x, axis, [(0, 1), (1, 0)])  8.7 us
    ppermute x1, starting transfers between devices, direct(): lax.ppermute(own_kv, ('ctx', 'rep'), [(2 * i + r, 2 * (i ^ 2 + r) + r) fo...  4.1 us
    ppermute x18, waiting for transfers between devices, swap(): return lax.ppermute(x, axis, [(0, 1), (1, 0)])  3.36 us
    ppermute x1, waiting for transfers between devices, direct(): lax.ppermute(own_kv, ('ctx', 'rep'), [(2 * i + r, 2 * (i ^ 2 + r) + r) fo...  2.19 us
  transfers between devices with their start and end apart: 26, of which 13 were waited for; matrix products, arithmetic and copies ran while one was open for 0% of the time, Pallas kernels for 17%

profile of v6, /device:TPU:0, one launch (start us, length us, event | category | flops | bytes accessed | tf_op | source)
XLA Modules:
  0.0 56.9 jit_solution(15766887236264975840)
XLA Ops:
  0.0 0.8 %shard_map.109 = (bf16[128,256]{1,0:T(8,128)(2,1)S(1)}, bf16[128,128]{1,0:T(8,128)(2,1)S(1)}) custom-call(s32[1]{0:T(128)} %bitcast.8.refs_0_, s32[1]{0:T(128)} %bitcast.1.refs_1_.refs_0_, bf16[128,256]{1,0:T(8,128)(2,1)} %refs_2_.1, bf16[128,256]{1,0:T(8,128)(2,1)} %refs_3_.1), custom_call_target="tpu_custom_call" | custom-call | flops 1 | bytes 1 | tf_op jit(solution)/shard_map/pallas_call | solution.py:44
  0.8 4.1 %collective-permute-start.2 = (bf16[128,256]{1,0:T(8,128)(2,1)S(1)}, bf16[128,256]{1,0:T(8,128)(2,1)S(1)}, u32[]{:S(2)}, u32[]{:S(2)}) collective-permute-start(bf16[128,256]{1,0:T(8,128)(2,1)S(1)} %get-tuple-element.56.refs_8_), channel_id=1, source_target_pairs={{0,8},{1,13},{4,12},{5,9},{8,0},{9,5},{12,4},{13,1},{2,10},{3,15},... | collective-permute-start | bytes 196616 | tf_op jit(solution)/shard_map/ppermute | solution.py:416
  4.9 1.6 %collective-permute-start = (bf16[128,128]{1,0:T(8,128)(2,1)S(1)}, bf16[128,128]{1,0:T(8,128)(2,1)S(1)}, u32[]{:S(2)}, u32[]{:S(2)}) collective-permute-start(bf16[128,128]{1,0:T(8,128)(2,1)S(1)} %get-tuple-element.51.refs_6_), channel_id=1, source_target_pairs={{0,4},{4,0},{8,12},{12,8},{1,5},{5,1},{9,13},{13,9},{2,6},{6,2},{1... | collective-permute-start | bytes 98312 | tf_op jit(solution)/shard_map/ppermute | solution.py:391
  6.5 2.2 %collective-permute-done.2.refs_11_ = bf16[128,256]{1,0:T(8,128)(2,1)S(1)} collective-permute-done((bf16[128,256]{1,0:T(8,128)(2,1)S(1)}, bf16[128,256]{1,0:T(8,128)(2,1)S(1)}, u32[]{:S(2)}, u32[]{:S(2)}) %collective-permute-start.2) | collective-permute-done | bytes 65568 | tf_op jit(solution)/shard_map/ppermute | solution.py:416
  9.2 1.2 %shard_map.110 = (bf16[128,1024]{1,0:T(8,128)(2,1)S(1)}, bf16[128,1024]{1,0:T(8,128)(2,1)S(1)}, bf16[8,128]{1,0:T(8,128)(2,1)S(1)}, bf16[4,1024]{1,0:T(4,128)(2,...) custom-call(bf16[128,1024]{1,0:T(8,128)(2,1)} %refs_0_.1, bf16[128,1024]{1,0:T(8,128)(2,1)} %refs_1_.1, ...), custom_call_target="tpu_custom_call" | custom-call | flops 1 | bytes 1 | tf_op jit(solution)/shard_map/pallas_call | solution.py:44
  10.4 1.9 %shard_map.111 = (f32[128,1024]{1,0:T(8,128)S(1)}, bf16[128,1024]{1,0:T(8,128)(2,1)S(1)}, f32[128,128]{1,0:T(8,128)S(1)}, bf16[80,1024]{1,0:T(8,128)(2,1)S(1)}, ...) custom-call(s32[1]{0:T(128)} %bitcast.refs_0_, s32[1]{0:T(128)} %bitcast.1.refs_1_.refs_0_, ...), custom_call_target="tpu_custom_call" | custom-call | flops 1 | bytes 1 | tf_op jit(solution)/shard_map/pallas_call | solution.py:44
  12.3 2.2 %collective-permute-start.5 = (bf16[80,1024]{1,0:T(8,128)(2,1)S(1)}, bf16[80,1024]{1,0:T(8,128)(2,1)S(1)}, u32[]{:S(2)}, u32[]{:S(2)}) collective-permute-start(bf16[80,1024]{1,0:T(8,128)(2,1)S(1)} %get-tuple-element.65), channel_id=1, source_target_pairs={{0,8},{4,12},{8,0},{12,4},{1,9},{5,13},{9,1},{13,5},{2,10},{6,14},... | collective-permute-start | bytes 491528 | tf_op jit(solution)/shard_map/ppermute | solution.py:391
  14.5 1.4 %shard_map.112 = (bf16[80,1024]{1,0:T(8,128)(2,1)S(1)}, bf16[80,1024]{1,0:T(8,128)(2,1)S(1)}, bf16[80,1024]{1,0:T(8,128)(2,1)S(1)}, f32[8,128]{1,0:T(8,128)S(1)}, bf16[768,1024]{1,0:T(8,128)(2,1)S(1)}) custom-call(s32[1]{0:T(128)} %bitcast.refs_0_, bf16[768,1024]{1,0:T(8,128)(2,1)} %bitcast.12, bf16[128,1024]{1,0:T(8,128)(2,1)S(1)} %get-tuple-element.58.refs_2_, ...), custom_call_target="tpu_custom_call" | custom-call | flops 1 | bytes 1 | tf_op jit(solution)/shard_map/pallas_call | solution.py:44
  17.1 2.0 %collective-permute-start.4 = (bf16[80,1024]{1,0:T(8,128)(2,1)S(1)}, bf16[80,1024]{1,0:T(8,128)(2,1)S(1)}, u32[]{:S(2)}, u32[]{:S(2)}) collective-permute-start(bf16[80,1024]{1,0:T(8,128)(2,1)S(1)} %get-tuple-element.64), channel_id=1, source_target_pairs={{0,4},{4,0},{8,12},{12,8},{1,5},{5,1},{9,13},{13,9},{2,6},{6,2},{1... | collective-permute-start | bytes 491528 | tf_op jit(solution)/shard_map/ppermute | solution.py:391
  19.3 1.6 %collective-permute-start.10 = (bf16[80,896]{1,0:T(8,128)(2,1)S(1)}, bf16[80,896]{1,0:T(8,128)(2,1)S(1)}, u32[]{:S(2)}, u32[]{:S(2)}) collective-permute-start(bf16[80,896]{1,0:T(8,128)(2,1)S(1)} %get-tuple-element.74), channel_id=1, source_target_pairs={{0,2},{2,0},{1,3},{3,1},{4,6},{6,4},{5,7},{7,5},{8,10},{10,8},{9,1... | collective-permute-start | bytes 430088 | tf_op jit(solution)/shard_map/ppermute | solution.py:360
  20.8 2.4 %collective-permute-done.5.refs_4_ = bf16[80,1024]{1,0:T(8,128)(2,1)S(1)} collective-permute-done((bf16[80,1024]{1,0:T(8,128)(2,1)S(1)}, bf16[80,1024]{1,0:T(8,128)(2,1)S(1)}, u32[]{:S(2)}, u32[]{:S(2)}) %collective-permute-start.5) | collective-permute-done | bytes 163872 | tf_op jit(solution)/shard_map/ppermute | solution.py:391
  24.4 2.8 %collective-permute-start.14 = (bf16[80,1024]{1,0:T(8,128)(2,1)S(1)}, bf16[80,1024]{1,0:T(8,128)(2,1)S(1)}, u32[]{:S(2)}, u32[]{:S(2)}) collective-permute-start(bf16[80,1024]{1,0:T(8,128)(2,1)S(1)} %get-tuple-element.82), channel_id=1, source_target_pairs={{0,12},{4,8},{8,4},{12,0},{1,13},{5,9},{9,5},{13,1},{2,14},{6,10},... | collective-permute-start | bytes 491528 | tf_op jit(solution)/shard_map/ppermute | solution.py:391
  27.6 1.6 %collective-permute-start.17 = (bf16[80,896]{1,0:T(8,128)(2,1)S(1)}, bf16[80,896]{1,0:T(8,128)(2,1)S(1)}, u32[]{:S(2)}, u32[]{:S(2)}) collective-permute-start(bf16[80,896]{1,0:T(8,128)(2,1)S(1)} %get-tuple-element.87), channel_id=1, source_target_pairs={{0,2},{2,0},{1,3},{3,1},{4,6},{6,4},{5,7},{7,5},{8,10},{10,8},{9,1... | collective-permute-start | bytes 430088 | tf_op jit(solution)/shard_map/ppermute | solution.py:360
  30.3 0.9 %collective-permute-done.11.refs_2_ = bf16[80,384]{1,0:T(8,128)(2,1)S(1)} collective-permute-done((bf16[80,384]{1,0:T(8,128)(2,1)S(1)}, bf16[80,384]{1,0:T(8,128)(2,1)S(1)}, u32[]{:S(2)}, u32[]{:S(2)}) %collective-permute-start.11) | collective-permute-done | bytes 61472 | tf_op jit(solution)/shard_map/ppermute | solution.py:360
  35.8 1.7 %collective-permute-start.22 = (bf16[80,896]{1,0:T(8,128)(2,1)S(1)}, bf16[80,896]{1,0:T(8,128)(2,1)S(1)}, u32[]{:S(2)}, u32[]{:S(2)}) collective-permute-start(bf16[80,896]{1,0:T(8,128)(2,1)S(1)} %get-tuple-element.94), channel_id=1, source_target_pairs={{0,2},{2,0},{1,3},{3,1},{4,6},{6,4},{5,7},{7,5},{8,10},{10,8},{9,1... | collective-permute-start | bytes 430088 | tf_op jit(solution)/shard_map/ppermute | solution.py:360
  38.3 1.2 %collective-permute-done.20.refs_3_ = bf16[80,384]{1,0:T(8,128)(2,1)S(1)} collective-permute-done((bf16[80,384]{1,0:T(8,128)(2,1)S(1)}, bf16[80,384]{1,0:T(8,128)(2,1)S(1)}, u32[]{:S(2)}, u32[]{:S(2)}) %collective-permute-start.20) | collective-permute-done | bytes 61472 | tf_op jit(solution)/shard_map/ppermute | solution.py:360
  40.0 0.7 %shard_map.127 = (bf16[256,80]{1,0:T(8,128)(2,1)S(1)}, bf16[256,80]{1,0:T(8,128)(2,1)S(1)}, bf16[256,80]{1,0:T(8,128)(2,1)S(1)}, bf16[256,80]{1,0:T(8,128)(2,1)S(1)}) custom-call(s32[1]{0:T(128)} %bitcast.refs_0_, f32[8,128]{1,0:T(8,128)S(1)} %get-tuple-element.89.refs_1_, s32[2,128]{1,0:T(2,128)S(1)} %get-tuple-element.90.refs_2_, ...), custom_call_target="tpu_custom_call" | custom-call | flops 1 | bytes 1 | tf_op jit(solution)/shard_map/pallas_call | solution.py:44
  41.0 0.7 %collective-permute-done.22.refs_1_ = bf16[80,896]{1,0:T(8,128)(2,1)S(1)} collective-permute-done((bf16[80,896]{1,0:T(8,128)(2,1)S(1)}, bf16[80,896]{1,0:T(8,128)(2,1)S(1)}, u32[]{:S(2)}, u32[]{:S(2)}) %collective-permute-start.22) | collective-permute-done | bytes 143392 | tf_op jit(solution)/shard_map/ppermute | solution.py:360
  42.0 2.0 %collective-permute-start.23 = (bf16[80,1024]{1,0:T(8,128)(2,1)S(1)}, bf16[80,1024]{1,0:T(8,128)(2,1)S(1)}, u32[]{:S(2)}, u32[]{:S(2)}) collective-permute-start(bf16[80,1024]{1,0:T(8,128)(2,1)S(1)} %shard_map.126.refs_4_), channel_id=1, source_target_pairs={{0,4},{4,0},{8,12},{12,8},{1,5},{5,1},{9,13},{13,9},{2,6},{6,2},{1... | collective-permute-start | bytes 491528 | tf_op jit(solution)/shard_map/ppermute | solution.py:391
  44.0 4.0 %collective-permute-done.21.refs_2_ = bf16[80,1024]{1,0:T(8,128)(2,1)S(1)} collective-permute-done((bf16[80,1024]{1,0:T(8,128)(2,1)S(1)}, bf16[80,1024]{1,0:T(8,128)(2,1)S(1)}, u32[]{:S(2)}, u32[]{:S(2)}) %collective-permute-start.21) | collective-permute-done | bytes 163872 | tf_op jit(solution)/shard_map/ppermute | solution.py:391
  48.7 1.3 %collective-permute-start.25 = (bf16[80,1024]{1,0:T(8,128)(2,1)S(1)}, bf16[80,1024]{1,0:T(8,128)(2,1)S(1)}, u32[]{:S(2)}, u32[]{:S(2)}) collective-permute-start(bf16[80,1024]{1,0:T(8,128)(2,1)S(1)} %shard_map.131.refs_3_), channel_id=1, source_target_pairs={{0,12},{4,8},{8,4},{12,0},{1,13},{5,9},{9,5},{13,1},{2,14},{6,10},... | collective-permute-start | bytes 491528 | tf_op jit(solution)/shard_map/ppermute | solution.py:391
  50.0 1.3 %collective-permute-done.23.refs_2_ = bf16[80,1024]{1,0:T(8,128)(2,1)S(1)} collective-permute-done((bf16[80,1024]{1,0:T(8,128)(2,1)S(1)}, bf16[80,1024]{1,0:T(8,128)(2,1)S(1)}, u32[]{:S(2)}, u32[]{:S(2)}) %collective-permute-start.23) | collective-permute-done | bytes 163872 | tf_op jit(solution)/shard_map/ppermute | solution.py:391
  51.6 4.3 %collective-permute-done.25.refs_2_ = bf16[80,1024]{1,0:T(8,128)(2,1)S(1)} collective-permute-done((bf16[80,1024]{1,0:T(8,128)(2,1)S(1)}, bf16[80,1024]{1,0:T(8,128)(2,1)S(1)}, u32[]{:S(2)}, u32[]{:S(2)}) %collective-permute-start.25) | collective-permute-done | bytes 163872 | tf_op jit(solution)/shard_map/ppermute | solution.py:391
  55.9 1.0 %shard_map.133 = bf16[128,1024]{1,0:T(8,128)(2,1)} custom-call(f32[128,1024]{1,0:T(8,128)S(1)} %shard_map.132.refs_0_.refs_3_, bf16[256,80]{1,0:T(8,128)(2,1)S(1)} %get-tuple-element.96.refs_1_, bf16[80,1024]{1,0:T(8,128)(2,1)S(1)} %collective-permute-done.25.refs_2_, f32[128,1024]{1,0:T(8,128)S(1)} %shard_map.132.refs_0_.refs_3_), custom_call_target="tpu_custom_call" | custom-call | flops 1 | bytes 1 | tf_op jit(solution)/shard_map/pallas_call | solution.py:44
  (53 shorter events, 11.8 us)
Async XLA Ops:
  0.8 7.9 %collective-permute-start.2 = (bf16[128,256]{1,0:T(8,128)(2,1)S(1)}, bf16[128,256]{1,0:T(8,128)(2,1)S(1)}, u32[]{:S(2)}, u32[]{:S(2)}) collective-permute-start(bf16[128,256]{1,0:T(8,128)(2,1)S(1)} %get-tuple-element.56.refs_8_), channel_id=1, source_target_pairs={{0,8},{1,13},{4,12},{5,9},{8,0},{9,5},{12,4},{13,1},{2,10},{3,15},... | collective-permute-start | bytes 196616 | tf_op jit(solution)/shard_map/ppermute | solution.py:416
  4.9 4.0 %collective-permute-start = (bf16[128,128]{1,0:T(8,128)(2,1)S(1)}, bf16[128,128]{1,0:T(8,128)(2,1)S(1)}, u32[]{:S(2)}, u32[]{:S(2)}) collective-permute-start(bf16[128,128]{1,0:T(8,128)(2,1)S(1)} %get-tuple-element.51.refs_6_), channel_id=1, source_target_pairs={{0,4},{4,0},{8,12},{12,8},{1,5},{5,1},{9,13},{13,9},{2,6},{6,2},{1... | collective-permute-start | bytes 98312 | tf_op jit(solution)/shard_map/ppermute | solution.py:391
  8.7 1.7 %collective-permute-start.3 = (bf16[128,256]{1,0:T(8,128)(2,1)S(1)}, bf16[128,256]{1,0:T(8,128)(2,1)S(1)}, u32[]{:S(2)}, u32[]{:S(2)}) collective-permute-start(bf16[128,256]{1,0:T(8,128)(2,1)S(1)} %collective-permute-done.2.refs_11_), channel_id=1, source_target_pairs={{0,1},{1,0},{2,3},{3,2},{4,5},{5,4},{6,7},{7,6},{8,9},{9,8},{10,11... | collective-permute-start | bytes 196616 | tf_op jit(solution)/shard_map/ppermute | solution.py:360
  8.9 1.5 %collective-permute-start.1 = (bf16[128,128]{1,0:T(8,128)(2,1)S(1)}, bf16[128,128]{1,0:T(8,128)(2,1)S(1)}, u32[]{:S(2)}, u32[]{:S(2)}) collective-permute-start(bf16[128,128]{1,0:T(8,128)(2,1)S(1)} %collective-permute-done.refs_9_), channel_id=1, source_target_pairs={{0,1},{1,0},{2,3},{3,2},{4,5},{5,4},{6,7},{7,6},{8,9},{9,8},{10,11... | collective-permute-start | bytes 98312 | tf_op jit(solution)/shard_map/ppermute | solution.py:360
  12.3 10.9 %collective-permute-start.5 = (bf16[80,1024]{1,0:T(8,128)(2,1)S(1)}, bf16[80,1024]{1,0:T(8,128)(2,1)S(1)}, u32[]{:S(2)}, u32[]{:S(2)}) collective-permute-start(bf16[80,1024]{1,0:T(8,128)(2,1)S(1)} %get-tuple-element.65), channel_id=1, source_target_pairs={{0,8},{4,12},{8,0},{12,4},{1,9},{5,13},{9,1},{13,5},{2,10},{6,14},... | collective-permute-start | bytes 491528 | tf_op jit(solution)/shard_map/ppermute | solution.py:391
  16.5 2.6 %collective-permute-start.7 = (bf16[80,512]{1,0:T(8,128)(2,1)S(1)}, bf16[80,512]{1,0:T(8,128)(2,1)S(1)}, u32[]{:S(2)}, u32[]{:S(2)}) collective-permute-start(bf16[80,512]{1,0:T(8,128)(2,1)S(1)} %get-tuple-element.69), channel_id=1, source_target_pairs={{0,1},{1,0},{2,3},{3,2},{4,5},{5,4},{6,7},{7,6},{8,9},{9,8},{10,11... | collective-permute-start | bytes 245768 | tf_op jit(solution)/shard_map/ppermute | solution.py:360
  16.6 2.5 %collective-permute-start.6 = (bf16[80,384]{1,0:T(8,128)(2,1)S(1)}, bf16[80,384]{1,0:T(8,128)(2,1)S(1)}, u32[]{:S(2)}, u32[]{:S(2)}) collective-permute-start(bf16[80,384]{1,0:T(8,128)(2,1)S(1)} %get-tuple-element.68), channel_id=1, source_target_pairs={{0,1},{1,0},{2,3},{3,2},{4,5},{5,4},{6,7},{7,6},{8,9},{9,8},{10,11... | collective-permute-start | bytes 184328 | tf_op jit(solution)/shard_map/ppermute | solution.py:360
  17.1 12.0 %collective-permute-start.4 = (bf16[80,1024]{1,0:T(8,128)(2,1)S(1)}, bf16[80,1024]{1,0:T(8,128)(2,1)S(1)}, u32[]{:S(2)}, u32[]{:S(2)}) collective-permute-start(bf16[80,1024]{1,0:T(8,128)(2,1)S(1)} %get-tuple-element.64), channel_id=1, source_target_pairs={{0,4},{4,0},{8,12},{12,8},{1,5},{5,1},{9,13},{13,9},{2,6},{6,2},{1... | collective-permute-start | bytes 491528 | tf_op jit(solution)/shard_map/ppermute | solution.py:391
  19.3 7.9 %collective-permute-start.10 = (bf16[80,896]{1,0:T(8,128)(2,1)S(1)}, bf16[80,896]{1,0:T(8,128)(2,1)S(1)}, u32[]{:S(2)}, u32[]{:S(2)}) collective-permute-start(bf16[80,896]{1,0:T(8,128)(2,1)S(1)} %get-tuple-element.74), channel_id=1, source_target_pairs={{0,2},{2,0},{1,3},{3,1},{4,6},{6,4},{5,7},{7,5},{8,10},{10,8},{9,1... | collective-permute-start | bytes 430088 | tf_op jit(solution)/shard_map/ppermute | solution.py:360
  23.8 3.6 %collective-permute-start.9 = (bf16[80,512]{1,0:T(8,128)(2,1)S(1)}, bf16[80,512]{1,0:T(8,128)(2,1)S(1)}, u32[]{:S(2)}, u32[]{:S(2)}) collective-permute-start(bf16[80,512]{1,0:T(8,128)(2,1)S(1)} %get-tuple-element.73), channel_id=1, source_target_pairs={{0,1},{1,0},{2,3},{3,2},{4,5},{5,4},{6,7},{7,6},{8,9},{9,8},{10,11... | collective-permute-start | bytes 245768 | tf_op jit(solution)/shard_map/ppermute | solution.py:360
  23.9 3.5 %collective-permute-start.8 = (bf16[80,384]{1,0:T(8,128)(2,1)S(1)}, bf16[80,384]{1,0:T(8,128)(2,1)S(1)}, u32[]{:S(2)}, u32[]{:S(2)}) collective-permute-start(bf16[80,384]{1,0:T(8,128)(2,1)S(1)} %get-tuple-element.72), channel_id=1, source_target_pairs={{0,1},{1,0},{2,3},{3,2},{4,5},{5,4},{6,7},{7,6},{8,9},{9,8},{10,11... | collective-permute-start | bytes 184328 | tf_op jit(solution)/shard_map/ppermute | solution.py:360
  24.4 8.1 %collective-permute-start.14 = (bf16[80,1024]{1,0:T(8,128)(2,1)S(1)}, bf16[80,1024]{1,0:T(8,128)(2,1)S(1)}, u32[]{:S(2)}, u32[]{:S(2)}) collective-permute-start(bf16[80,1024]{1,0:T(8,128)(2,1)S(1)} %get-tuple-element.82), channel_id=1, source_target_pairs={{0,12},{4,8},{8,4},{12,0},{1,13},{5,9},{9,5},{13,1},{2,14},{6,10},... | collective-permute-start | bytes 491528 | tf_op jit(solution)/shard_map/ppermute | solution.py:391
  27.6 6.1 %collective-permute-start.17 = (bf16[80,896]{1,0:T(8,128)(2,1)S(1)}, bf16[80,896]{1,0:T(8,128)(2,1)S(1)}, u32[]{:S(2)}, u32[]{:S(2)}) collective-permute-start(bf16[80,896]{1,0:T(8,128)(2,1)S(1)} %get-tuple-element.87), channel_id=1, source_target_pairs={{0,2},{2,0},{1,3},{3,1},{4,6},{6,4},{5,7},{7,5},{8,10},{10,8},{9,1... | collective-permute-start | bytes 430088 | tf_op jit(solution)/shard_map/ppermute | solution.py:360
  29.7 1.5 %collective-permute-start.12 = (bf16[96,512]{1,0:T(8,128)(2,1)S(1)}, bf16[96,512]{1,0:T(8,128)(2,1)S(1)}, u32[]{:S(2)}, u32[]{:S(2)}) collective-permute-start(bf16[96,512]{1,0:T(8,128)(2,1)S(1)} %get-tuple-element.78), channel_id=1, source_target_pairs={{0,1},{1,0},{2,3},{3,2},{4,5},{5,4},{6,7},{7,6},{8,9},{9,8},{10,11... | collective-permute-start | bytes 294920 | tf_op jit(solution)/shard_map/ppermute | solution.py:360
  29.8 1.4 %collective-permute-start.11 = (bf16[80,384]{1,0:T(8,128)(2,1)S(1)}, bf16[80,384]{1,0:T(8,128)(2,1)S(1)}, u32[]{:S(2)}, u32[]{:S(2)}) collective-permute-start(bf16[80,384]{1,0:T(8,128)(2,1)S(1)} %get-tuple-element.77), channel_id=1, source_target_pairs={{0,1},{1,0},{2,3},{3,2},{4,5},{5,4},{6,7},{7,6},{8,9},{9,8},{10,11... | collective-permute-start | bytes 184328 | tf_op jit(solution)/shard_map/ppermute | solution.py:360
  31.3 6.7 %collective-permute-start.13 = (bf16[96,896]{1,0:T(8,128)(2,1)S(1)}, bf16[96,896]{1,0:T(8,128)(2,1)S(1)}, u32[]{:S(2)}, u32[]{:S(2)}) collective-permute-start(bf16[96,896]{1,0:T(8,128)(2,1)S(1)} %get-tuple-element.81), channel_id=1, source_target_pairs={{0,2},{2,0},{1,3},{3,1},{4,6},{6,4},{5,7},{7,5},{8,10},{10,8},{9,1... | collective-permute-start | bytes 516104 | tf_op jit(solution)/shard_map/ppermute | solution.py:360
  33.1 2.5 %collective-permute-start.16 = (bf16[80,512]{1,0:T(8,128)(2,1)S(1)}, bf16[80,512]{1,0:T(8,128)(2,1)S(1)}, u32[]{:S(2)}, u32[]{:S(2)}) collective-permute-start(bf16[80,512]{1,0:T(8,128)(2,1)S(1)} %get-tuple-element.85), channel_id=1, source_target_pairs={{0,1},{1,0},{2,3},{3,2},{4,5},{5,4},{6,7},{7,6},{8,9},{9,8},{10,11... | collective-permute-start | bytes 245768 | tf_op jit(solution)/shard_map/ppermute | solution.py:360
  33.2 1.4 %collective-permute-start.19 = (bf16[80,384]{1,0:T(8,128)(2,1)S(1)}, bf16[80,384]{1,0:T(8,128)(2,1)S(1)}, u32[]{:S(2)}, u32[]{:S(2)}) collective-permute-start(bf16[80,384]{1,0:T(8,128)(2,1)S(1)} %shard_map.116.refs_3_.refs_2_), channel_id=1, source_target_pairs={{0,1},{1,0},{2,3},{3,2},{4,5},{5,4},{6,7},{7,6},{8,9},{9,8},{10,11... | collective-permute-start | bytes 184328 | tf_op jit(solution)/shard_map/ppermute | solution.py:360
  34.1 1.6 %collective-permute-start.15 = (bf16[80,384]{1,0:T(8,128)(2,1)S(1)}, bf16[80,384]{1,0:T(8,128)(2,1)S(1)}, u32[]{:S(2)}, u32[]{:S(2)}) collective-permute-start(bf16[80,384]{1,0:T(8,128)(2,1)S(1)} %get-tuple-element.84), channel_id=1, source_target_pairs={{0,1},{1,0},{2,3},{3,2},{4,5},{5,4},{6,7},{7,6},{8,9},{9,8},{10,11... | collective-permute-start | bytes 184328 | tf_op jit(solution)/shard_map/ppermute | solution.py:360
  35.8 5.9 %collective-permute-start.22 = (bf16[80,896]{1,0:T(8,128)(2,1)S(1)}, bf16[80,896]{1,0:T(8,128)(2,1)S(1)}, u32[]{:S(2)}, u32[]{:S(2)}) collective-permute-start(bf16[80,896]{1,0:T(8,128)(2,1)S(1)} %get-tuple-element.94), channel_id=1, source_target_pairs={{0,2},{2,0},{1,3},{3,1},{4,6},{6,4},{5,7},{7,5},{8,10},{10,8},{9,1... | collective-permute-start | bytes 430088 | tf_op jit(solution)/shard_map/ppermute | solution.py:360
  37.5 10.5 %collective-permute-start.21 = (bf16[80,1024]{1,0:T(8,128)(2,1)S(1)}, bf16[80,1024]{1,0:T(8,128)(2,1)S(1)}, u32[]{:S(2)}, u32[]{:S(2)}) collective-permute-start(bf16[80,1024]{1,0:T(8,128)(2,1)S(1)} %shard_map.123.refs_3_), channel_id=1, source_target_pairs={{0,8},{4,12},{8,0},{12,4},{1,9},{5,13},{9,1},{13,5},{2,10},{6,14},... | collective-permute-start | bytes 491528 | tf_op jit(solution)/shard_map/ppermute | solution.py:391
  41.9 6.4 %collective-permute-start.24 = (bf16[80,384]{1,0:T(8,128)(2,1)S(1)}, bf16[80,384]{1,0:T(8,128)(2,1)S(1)}, u32[]{:S(2)}, u32[]{:S(2)}) collective-permute-start(bf16[80,384]{1,0:T(8,128)(2,1)S(1)} %shard_map.129.refs_3_.refs_2_), channel_id=1, source_target_pairs={{0,1},{1,0},{2,3},{3,2},{4,5},{5,4},{6,7},{7,6},{8,9},{9,8},{10,11... | collective-permute-start | bytes 184328 | tf_op jit(solution)/shard_map/ppermute | solution.py:360
  42.0 9.3 %collective-permute-start.23 = (bf16[80,1024]{1,0:T(8,128)(2,1)S(1)}, bf16[80,1024]{1,0:T(8,128)(2,1)S(1)}, u32[]{:S(2)}, u32[]{:S(2)}) collective-permute-start(bf16[80,1024]{1,0:T(8,128)(2,1)S(1)} %shard_map.126.refs_4_), channel_id=1, source_target_pairs={{0,4},{4,0},{8,12},{12,8},{1,5},{5,1},{9,13},{13,9},{2,6},{6,2},{1... | collective-permute-start | bytes 491528 | tf_op jit(solution)/shard_map/ppermute | solution.py:391
  48.7 7.2 %collective-permute-start.25 = (bf16[80,1024]{1,0:T(8,128)(2,1)S(1)}, bf16[80,1024]{1,0:T(8,128)(2,1)S(1)}, u32[]{:S(2)}, u32[]{:S(2)}) collective-permute-start(bf16[80,1024]{1,0:T(8,128)(2,1)S(1)} %shard_map.131.refs_3_), channel_id=1, source_target_pairs={{0,12},{4,8},{8,4},{12,0},{1,13},{5,9},{9,5},{13,1},{2,14},{6,10},... | collective-permute-start | bytes 491528 | tf_op jit(solution)/shard_map/ppermute | solution.py:391
  (2 other events, 2.6 us)

commit v7 on v5

--- a/solution.py
+++ b/solution.py
@@ -513,7 +513,7 @@
     steps = dict(u=up_step, a=add_step, i=inner_step, d=down_step, m=lambda j: mix_step([j]))
     plan = (
         *("u0", "a0", "u1", "i0", "a1", "u2", "a2", "u3", "i1", "d0"),
-        *("d1", "a3", "i2", "d2", "g", "m0", "i3", "m1", "d3", "m2"),
+        *("d1", "a3", "i2", "d2", "g", "i3", "m0", "m1", "d3", "m2"),
     )
     for name in plan:
         if name == "g":

time: 57.1 us -> 57.1 us (level)
  no operation moved by 1% of the time
where the time goes in v7:
time: 57.1 us; the launch traced here: 56.9 us
  starting transfers between devices  24.8 us (43%)
  waiting for transfers between devices  18.6 us (33%)
  Pallas kernels  13.2 us (23%)
    pallas_call x25, Pallas kernels, vmem_call(): pl.pallas_call(kernel, out_shape=[placed(x) for x in out_shape] if multi...  13.2 us
    ppermute x7, waiting for transfers between devices, exchange(): return lax.ppermute(x, 'ctx', [(i, i ^ j) for i in range(n)])  12.8 us
    ppermute x7, starting transfers between devices, exchange(): return lax.ppermute(x, 'ctx', [(i, i ^ j) for i in range(n)])  12 us
    ppermute x18, starting transfers between devices, swap(): return lax.ppermute(x, axis, [(0, 1), (1, 0)])  8.7 us
    ppermute x1, starting transfers between devices, direct(): lax.ppermute(own_kv, ('ctx', 'rep'), [(2 * i + r, 2 * (i ^ 2 + r) + r) fo...  4.1 us
    ppermute x18, waiting for transfers between devices, swap(): return lax.ppermute(x, axis, [(0, 1), (1, 0)])  3.63 us
    ppermute x1, waiting for transfers between devices, direct(): lax.ppermute(own_kv, ('ctx', 'rep'), [(2 * i + r, 2 * (i ^ 2 + r) + r) fo...  2.19 us
  transfers between devices with their start and end apart: 26, of which 13 were waited for; matrix products, arithmetic and copies ran while one was open for 0% of the time, Pallas kernels for 17%

profile of v7, /device:TPU:0, one launch (start us, length us, event | category | flops | bytes accessed | tf_op | source)
XLA Modules:
  0.0 56.9 jit_solution(16300293687976273210)
XLA Ops:
  0.0 0.8 %shard_map.109 = (bf16[128,256]{1,0:T(8,128)(2,1)S(1)}, bf16[128,128]{1,0:T(8,128)(2,1)S(1)}) custom-call(s32[1]{0:T(128)} %bitcast.8.refs_0_, s32[1]{0:T(128)} %bitcast.1.refs_1_.refs_0_, bf16[128,256]{1,0:T(8,128)(2,1)} %refs_2_.1, bf16[128,256]{1,0:T(8,128)(2,1)} %refs_3_.1), custom_call_target="tpu_custom_call" | custom-call | flops 1 | bytes 1 | tf_op jit(solution)/shard_map/pallas_call | solution.py:44
  0.8 4.1 %collective-permute-start.2 = (bf16[128,256]{1,0:T(8,128)(2,1)S(1)}, bf16[128,256]{1,0:T(8,128)(2,1)S(1)}, u32[]{:S(2)}, u32[]{:S(2)}) collective-permute-start(bf16[128,256]{1,0:T(8,128)(2,1)S(1)} %get-tuple-element.56.refs_8_), channel_id=1, source_target_pairs={{0,8},{1,13},{4,12},{5,9},{8,0},{9,5},{12,4},{13,1},{2,10},{3,15},... | collective-permute-start | bytes 196616 | tf_op jit(solution)/shard_map/ppermute | solution.py:393
  4.9 1.6 %collective-permute-start = (bf16[128,128]{1,0:T(8,128)(2,1)S(1)}, bf16[128,128]{1,0:T(8,128)(2,1)S(1)}, u32[]{:S(2)}, u32[]{:S(2)}) collective-permute-start(bf16[128,128]{1,0:T(8,128)(2,1)S(1)} %get-tuple-element.51.refs_6_), channel_id=1, source_target_pairs={{0,4},{4,0},{8,12},{12,8},{1,5},{5,1},{9,13},{13,9},{2,6},{6,2},{1... | collective-permute-start | bytes 98312 | tf_op jit(solution)/shard_map/ppermute | solution.py:368
  6.5 2.2 %collective-permute-done.2.refs_11_ = bf16[128,256]{1,0:T(8,128)(2,1)S(1)} collective-permute-done((bf16[128,256]{1,0:T(8,128)(2,1)S(1)}, bf16[128,256]{1,0:T(8,128)(2,1)S(1)}, u32[]{:S(2)}, u32[]{:S(2)}) %collective-permute-start.2) | collective-permute-done | bytes 65568 | tf_op jit(solution)/shard_map/ppermute | solution.py:393
  9.2 1.2 %shard_map.110 = (bf16[128,1024]{1,0:T(8,128)(2,1)S(1)}, bf16[128,1024]{1,0:T(8,128)(2,1)S(1)}, bf16[8,128]{1,0:T(8,128)(2,1)S(1)}, bf16[4,1024]{1,0:T(4,128)(2,...) custom-call(bf16[128,1024]{1,0:T(8,128)(2,1)} %refs_0_.1, bf16[128,1024]{1,0:T(8,128)(2,1)} %refs_1_.1, ...), custom_call_target="tpu_custom_call" | custom-call | flops 1 | bytes 1 | tf_op jit(solution)/shard_map/pallas_call | solution.py:44
  10.4 1.9 %shard_map.111 = (f32[128,1024]{1,0:T(8,128)S(1)}, bf16[128,1024]{1,0:T(8,128)(2,1)S(1)}, f32[128,128]{1,0:T(8,128)S(1)}, bf16[80,1024]{1,0:T(8,128)(2,1)S(1)}, ...) custom-call(s32[1]{0:T(128)} %bitcast.refs_0_, s32[1]{0:T(128)} %bitcast.1.refs_1_.refs_0_, ...), custom_call_target="tpu_custom_call" | custom-call | flops 1 | bytes 1 | tf_op jit(solution)/shard_map/pallas_call | solution.py:44
  12.3 2.2 %collective-permute-start.5 = (bf16[80,1024]{1,0:T(8,128)(2,1)S(1)}, bf16[80,1024]{1,0:T(8,128)(2,1)S(1)}, u32[]{:S(2)}, u32[]{:S(2)}) collective-permute-start(bf16[80,1024]{1,0:T(8,128)(2,1)S(1)} %get-tuple-element.65), channel_id=1, source_target_pairs={{0,8},{4,12},{8,0},{12,4},{1,9},{5,13},{9,1},{13,5},{2,10},{6,14},... | collective-permute-start | bytes 491528 | tf_op jit(solution)/shard_map/ppermute | solution.py:368
  14.5 1.4 %shard_map.112 = (bf16[80,1024]{1,0:T(8,128)(2,1)S(1)}, bf16[80,1024]{1,0:T(8,128)(2,1)S(1)}, bf16[80,1024]{1,0:T(8,128)(2,1)S(1)}, f32[8,128]{1,0:T(8,128)S(1)}, bf16[768,1024]{1,0:T(8,128)(2,1)S(1)}) custom-call(s32[1]{0:T(128)} %bitcast.refs_0_, bf16[768,1024]{1,0:T(8,128)(2,1)} %bitcast.12, bf16[128,1024]{1,0:T(8,128)(2,1)S(1)} %get-tuple-element.58.refs_2_, ...), custom_call_target="tpu_custom_call" | custom-call | flops 1 | bytes 1 | tf_op jit(solution)/shard_map/pallas_call | solution.py:44
  17.1 2.0 %collective-permute-start.4 = (bf16[80,1024]{1,0:T(8,128)(2,1)S(1)}, bf16[80,1024]{1,0:T(8,128)(2,1)S(1)}, u32[]{:S(2)}, u32[]{:S(2)}) collective-permute-start(bf16[80,1024]{1,0:T(8,128)(2,1)S(1)} %get-tuple-element.64), channel_id=1, source_target_pairs={{0,4},{4,0},{8,12},{12,8},{1,5},{5,1},{9,13},{13,9},{2,6},{6,2},{1... | collective-permute-start | bytes 491528 | tf_op jit(solution)/shard_map/ppermute | solution.py:368
  19.3 1.6 %collective-permute-start.10 = (bf16[80,896]{1,0:T(8,128)(2,1)S(1)}, bf16[80,896]{1,0:T(8,128)(2,1)S(1)}, u32[]{:S(2)}, u32[]{:S(2)}) collective-permute-start(bf16[80,896]{1,0:T(8,128)(2,1)S(1)} %get-tuple-element.74), channel_id=1, source_target_pairs={{0,2},{2,0},{1,3},{3,1},{4,6},{6,4},{5,7},{7,5},{8,10},{10,8},{9,1... | collective-permute-start | bytes 430088 | tf_op jit(solution)/shard_map/ppermute | solution.py:337
  20.8 2.4 %collective-permute-done.5.refs_4_ = bf16[80,1024]{1,0:T(8,128)(2,1)S(1)} collective-permute-done((bf16[80,1024]{1,0:T(8,128)(2,1)S(1)}, bf16[80,1024]{1,0:T(8,128)(2,1)S(1)}, u32[]{:S(2)}, u32[]{:S(2)}) %collective-permute-start.5) | collective-permute-done | bytes 163872 | tf_op jit(solution)/shard_map/ppermute | solution.py:368
  24.4 2.8 %collective-permute-start.14 = (bf16[80,1024]{1,0:T(8,128)(2,1)S(1)}, bf16[80,1024]{1,0:T(8,128)(2,1)S(1)}, u32[]{:S(2)}, u32[]{:S(2)}) collective-permute-start(bf16[80,1024]{1,0:T(8,128)(2,1)S(1)} %get-tuple-element.82), channel_id=1, source_target_pairs={{0,12},{4,8},{8,4},{12,0},{1,13},{5,9},{9,5},{13,1},{2,14},{6,10},... | collective-permute-start | bytes 491528 | tf_op jit(solution)/shard_map/ppermute | solution.py:368
  27.6 1.6 %collective-permute-start.17 = (bf16[80,896]{1,0:T(8,128)(2,1)S(1)}, bf16[80,896]{1,0:T(8,128)(2,1)S(1)}, u32[]{:S(2)}, u32[]{:S(2)}) collective-permute-start(bf16[80,896]{1,0:T(8,128)(2,1)S(1)} %get-tuple-element.87), channel_id=1, source_target_pairs={{0,2},{2,0},{1,3},{3,1},{4,6},{6,4},{5,7},{7,5},{8,10},{10,8},{9,1... | collective-permute-start | bytes 430088 | tf_op jit(solution)/shard_map/ppermute | solution.py:337
  30.3 0.9 %collective-permute-done.11.refs_2_ = bf16[80,384]{1,0:T(8,128)(2,1)S(1)} collective-permute-done((bf16[80,384]{1,0:T(8,128)(2,1)S(1)}, bf16[80,384]{1,0:T(8,128)(2,1)S(1)}, u32[]{:S(2)}, u32[]{:S(2)}) %collective-permute-start.11) | collective-permute-done | bytes 61472 | tf_op jit(solution)/shard_map/ppermute | solution.py:337
  35.8 1.7 %collective-permute-start.21 = (bf16[80,896]{1,0:T(8,128)(2,1)S(1)}, bf16[80,896]{1,0:T(8,128)(2,1)S(1)}, u32[]{:S(2)}, u32[]{:S(2)}) collective-permute-start(bf16[80,896]{1,0:T(8,128)(2,1)S(1)} %get-tuple-element.93), channel_id=1, source_target_pairs={{0,2},{2,0},{1,3},{3,1},{4,6},{6,4},{5,7},{7,5},{8,10},{10,8},{9,1... | collective-permute-start | bytes 430088 | tf_op jit(solution)/shard_map/ppermute | solution.py:337
  38.3 1.2 %collective-permute-done.20.refs_3_ = bf16[80,384]{1,0:T(8,128)(2,1)S(1)} collective-permute-done((bf16[80,384]{1,0:T(8,128)(2,1)S(1)}, bf16[80,384]{1,0:T(8,128)(2,1)S(1)}, u32[]{:S(2)}, u32[]{:S(2)}) %collective-permute-start.20) | collective-permute-done | bytes 61472 | tf_op jit(solution)/shard_map/ppermute | solution.py:337
  40.0 0.7 %shard_map.127 = (bf16[256,80]{1,0:T(8,128)(2,1)S(1)}, bf16[256,80]{1,0:T(8,128)(2,1)S(1)}, bf16[256,80]{1,0:T(8,128)(2,1)S(1)}, bf16[256,80]{1,0:T(8,128)(2,1)S(1)}) custom-call(s32[1]{0:T(128)} %bitcast.refs_0_, f32[8,128]{1,0:T(8,128)S(1)} %get-tuple-element.89.refs_1_, s32[2,128]{1,0:T(2,128)S(1)} %get-tuple-element.90.refs_2_, ...), custom_call_target="tpu_custom_call" | custom-call | flops 1 | bytes 1 | tf_op jit(solution)/shard_map/pallas_call | solution.py:44
  40.7 1.0 %collective-permute-done.21.refs_1_ = bf16[80,896]{1,0:T(8,128)(2,1)S(1)} collective-permute-done((bf16[80,896]{1,0:T(8,128)(2,1)S(1)}, bf16[80,896]{1,0:T(8,128)(2,1)S(1)}, u32[]{:S(2)}, u32[]{:S(2)}) %collective-permute-start.21) | collective-permute-done | bytes 143392 | tf_op jit(solution)/shard_map/ppermute | solution.py:337
  42.0 1.8 %collective-permute-start.23 = (bf16[80,1024]{1,0:T(8,128)(2,1)S(1)}, bf16[80,1024]{1,0:T(8,128)(2,1)S(1)}, u32[]{:S(2)}, u32[]{:S(2)}) collective-permute-start(bf16[80,1024]{1,0:T(8,128)(2,1)S(1)} %shard_map.126.refs_4_), channel_id=1, source_target_pairs={{0,4},{4,0},{8,12},{12,8},{1,5},{5,1},{9,13},{13,9},{2,6},{6,2},{1... | collective-permute-start | bytes 491528 | tf_op jit(solution)/shard_map/ppermute | solution.py:368
  44.0 4.0 %collective-permute-done.22.refs_2_ = bf16[80,1024]{1,0:T(8,128)(2,1)S(1)} collective-permute-done((bf16[80,1024]{1,0:T(8,128)(2,1)S(1)}, bf16[80,1024]{1,0:T(8,128)(2,1)S(1)}, u32[]{:S(2)}, u32[]{:S(2)}) %collective-permute-start.22) | collective-permute-done | bytes 163872 | tf_op jit(solution)/shard_map/ppermute | solution.py:368
  48.7 1.3 %collective-permute-start.25 = (bf16[80,1024]{1,0:T(8,128)(2,1)S(1)}, bf16[80,1024]{1,0:T(8,128)(2,1)S(1)}, u32[]{:S(2)}, u32[]{:S(2)}) collective-permute-start(bf16[80,1024]{1,0:T(8,128)(2,1)S(1)} %shard_map.131.refs_3_), channel_id=1, source_target_pairs={{0,12},{4,8},{8,4},{12,0},{1,13},{5,9},{9,5},{13,1},{2,14},{6,10},... | collective-permute-start | bytes 491528 | tf_op jit(solution)/shard_map/ppermute | solution.py:368
  50.0 1.2 %collective-permute-done.23.refs_2_ = bf16[80,1024]{1,0:T(8,128)(2,1)S(1)} collective-permute-done((bf16[80,1024]{1,0:T(8,128)(2,1)S(1)}, bf16[80,1024]{1,0:T(8,128)(2,1)S(1)}, u32[]{:S(2)}, u32[]{:S(2)}) %collective-permute-start.23) | collective-permute-done | bytes 163872 | tf_op jit(solution)/shard_map/ppermute | solution.py:368
  51.4 4.5 %collective-permute-done.25.refs_2_ = bf16[80,1024]{1,0:T(8,128)(2,1)S(1)} collective-permute-done((bf16[80,1024]{1,0:T(8,128)(2,1)S(1)}, bf16[80,1024]{1,0:T(8,128)(2,1)S(1)}, u32[]{:S(2)}, u32[]{:S(2)}) %collective-permute-start.25) | collective-permute-done | bytes 163872 | tf_op jit(solution)/shard_map/ppermute | solution.py:368
  55.9 1.0 %shard_map.133 = bf16[128,1024]{1,0:T(8,128)(2,1)} custom-call(f32[128,1024]{1,0:T(8,128)S(1)} %shard_map.132.refs_0_.refs_3_, bf16[256,80]{1,0:T(8,128)(2,1)S(1)} %get-tuple-element.96.refs_1_, bf16[80,1024]{1,0:T(8,128)(2,1)S(1)} %collective-permute-done.25.refs_2_, f32[128,1024]{1,0:T(8,128)S(1)} %shard_map.132.refs_0_.refs_3_), custom_call_target="tpu_custom_call" | custom-call | flops 1 | bytes 1 | tf_op jit(solution)/shard_map/pallas_call | solution.py:44
  (53 shorter events, 11.8 us)
Async XLA Ops:
  0.8 7.9 %collective-permute-start.2 = (bf16[128,256]{1,0:T(8,128)(2,1)S(1)}, bf16[128,256]{1,0:T(8,128)(2,1)S(1)}, u32[]{:S(2)}, u32[]{:S(2)}) collective-permute-start(bf16[128,256]{1,0:T(8,128)(2,1)S(1)} %get-tuple-element.56.refs_8_), channel_id=1, source_target_pairs={{0,8},{1,13},{4,12},{5,9},{8,0},{9,5},{12,4},{13,1},{2,10},{3,15},... | collective-permute-start | bytes 196616 | tf_op jit(solution)/shard_map/ppermute | solution.py:393
  4.9 4.0 %collective-permute-start = (bf16[128,128]{1,0:T(8,128)(2,1)S(1)}, bf16[128,128]{1,0:T(8,128)(2,1)S(1)}, u32[]{:S(2)}, u32[]{:S(2)}) collective-permute-start(bf16[128,128]{1,0:T(8,128)(2,1)S(1)} %get-tuple-element.51.refs_6_), channel_id=1, source_target_pairs={{0,4},{4,0},{8,12},{12,8},{1,5},{5,1},{9,13},{13,9},{2,6},{6,2},{1... | collective-permute-start | bytes 98312 | tf_op jit(solution)/shard_map/ppermute | solution.py:368
  8.7 1.7 %collective-permute-start.3 = (bf16[128,256]{1,0:T(8,128)(2,1)S(1)}, bf16[128,256]{1,0:T(8,128)(2,1)S(1)}, u32[]{:S(2)}, u32[]{:S(2)}) collective-permute-start(bf16[128,256]{1,0:T(8,128)(2,1)S(1)} %collective-permute-done.2.refs_11_), channel_id=1, source_target_pairs={{0,1},{1,0},{2,3},{3,2},{4,5},{5,4},{6,7},{7,6},{8,9},{9,8},{10,11... | collective-permute-start | bytes 196616 | tf_op jit(solution)/shard_map/ppermute | solution.py:337
  8.9 1.5 %collective-permute-start.1 = (bf16[128,128]{1,0:T(8,128)(2,1)S(1)}, bf16[128,128]{1,0:T(8,128)(2,1)S(1)}, u32[]{:S(2)}, u32[]{:S(2)}) collective-permute-start(bf16[128,128]{1,0:T(8,128)(2,1)S(1)} %collective-permute-done.refs_9_), channel_id=1, source_target_pairs={{0,1},{1,0},{2,3},{3,2},{4,5},{5,4},{6,7},{7,6},{8,9},{9,8},{10,11... | collective-permute-start | bytes 98312 | tf_op jit(solution)/shard_map/ppermute | solution.py:337
  12.3 10.9 %collective-permute-start.5 = (bf16[80,1024]{1,0:T(8,128)(2,1)S(1)}, bf16[80,1024]{1,0:T(8,128)(2,1)S(1)}, u32[]{:S(2)}, u32[]{:S(2)}) collective-permute-start(bf16[80,1024]{1,0:T(8,128)(2,1)S(1)} %get-tuple-element.65), channel_id=1, source_target_pairs={{0,8},{4,12},{8,0},{12,4},{1,9},{5,13},{9,1},{13,5},{2,10},{6,14},... | collective-permute-start | bytes 491528 | tf_op jit(solution)/shard_map/ppermute | solution.py:368
  16.5 2.6 %collective-permute-start.7 = (bf16[80,512]{1,0:T(8,128)(2,1)S(1)}, bf16[80,512]{1,0:T(8,128)(2,1)S(1)}, u32[]{:S(2)}, u32[]{:S(2)}) collective-permute-start(bf16[80,512]{1,0:T(8,128)(2,1)S(1)} %get-tuple-element.69), channel_id=1, source_target_pairs={{0,1},{1,0},{2,3},{3,2},{4,5},{5,4},{6,7},{7,6},{8,9},{9,8},{10,11... | collective-permute-start | bytes 245768 | tf_op jit(solution)/shard_map/ppermute | solution.py:337
  16.6 2.5 %collective-permute-start.6 = (bf16[80,384]{1,0:T(8,128)(2,1)S(1)}, bf16[80,384]{1,0:T(8,128)(2,1)S(1)}, u32[]{:S(2)}, u32[]{:S(2)}) collective-permute-start(bf16[80,384]{1,0:T(8,128)(2,1)S(1)} %get-tuple-element.68), channel_id=1, source_target_pairs={{0,1},{1,0},{2,3},{3,2},{4,5},{5,4},{6,7},{7,6},{8,9},{9,8},{10,11... | collective-permute-start | bytes 184328 | tf_op jit(solution)/shard_map/ppermute | solution.py:337
  17.1 12.0 %collective-permute-start.4 = (bf16[80,1024]{1,0:T(8,128)(2,1)S(1)}, bf16[80,1024]{1,0:T(8,128)(2,1)S(1)}, u32[]{:S(2)}, u32[]{:S(2)}) collective-permute-start(bf16[80,1024]{1,0:T(8,128)(2,1)S(1)} %get-tuple-element.64), channel_id=1, source_target_pairs={{0,4},{4,0},{8,12},{12,8},{1,5},{5,1},{9,13},{13,9},{2,6},{6,2},{1... | collective-permute-start | bytes 491528 | tf_op jit(solution)/shard_map/ppermute | solution.py:368
  19.3 7.9 %collective-permute-start.10 = (bf16[80,896]{1,0:T(8,128)(2,1)S(1)}, bf16[80,896]{1,0:T(8,128)(2,1)S(1)}, u32[]{:S(2)}, u32[]{:S(2)}) collective-permute-start(bf16[80,896]{1,0:T(8,128)(2,1)S(1)} %get-tuple-element.74), channel_id=1, source_target_pairs={{0,2},{2,0},{1,3},{3,1},{4,6},{6,4},{5,7},{7,5},{8,10},{10,8},{9,1... | collective-permute-start | bytes 430088 | tf_op jit(solution)/shard_map/ppermute | solution.py:337
  23.8 3.6 %collective-permute-start.9 = (bf16[80,512]{1,0:T(8,128)(2,1)S(1)}, bf16[80,512]{1,0:T(8,128)(2,1)S(1)}, u32[]{:S(2)}, u32[]{:S(2)}) collective-permute-start(bf16[80,512]{1,0:T(8,128)(2,1)S(1)} %get-tuple-element.73), channel_id=1, source_target_pairs={{0,1},{1,0},{2,3},{3,2},{4,5},{5,4},{6,7},{7,6},{8,9},{9,8},{10,11... | collective-permute-start | bytes 245768 | tf_op jit(solution)/shard_map/ppermute | solution.py:337
  23.9 3.5 %collective-permute-start.8 = (bf16[80,384]{1,0:T(8,128)(2,1)S(1)}, bf16[80,384]{1,0:T(8,128)(2,1)S(1)}, u32[]{:S(2)}, u32[]{:S(2)}) collective-permute-start(bf16[80,384]{1,0:T(8,128)(2,1)S(1)} %get-tuple-element.72), channel_id=1, source_target_pairs={{0,1},{1,0},{2,3},{3,2},{4,5},{5,4},{6,7},{7,6},{8,9},{9,8},{10,11... | collective-permute-start | bytes 184328 | tf_op jit(solution)/shard_map/ppermute | solution.py:337
  24.4 8.1 %collective-permute-start.14 = (bf16[80,1024]{1,0:T(8,128)(2,1)S(1)}, bf16[80,1024]{1,0:T(8,128)(2,1)S(1)}, u32[]{:S(2)}, u32[]{:S(2)}) collective-permute-start(bf16[80,1024]{1,0:T(8,128)(2,1)S(1)} %get-tuple-element.82), channel_id=1, source_target_pairs={{0,12},{4,8},{8,4},{12,0},{1,13},{5,9},{9,5},{13,1},{2,14},{6,10},... | collective-permute-start | bytes 491528 | tf_op jit(solution)/shard_map/ppermute | solution.py:368
  27.6 6.1 %collective-permute-start.17 = (bf16[80,896]{1,0:T(8,128)(2,1)S(1)}, bf16[80,896]{1,0:T(8,128)(2,1)S(1)}, u32[]{:S(2)}, u32[]{:S(2)}) collective-permute-start(bf16[80,896]{1,0:T(8,128)(2,1)S(1)} %get-tuple-element.87), channel_id=1, source_target_pairs={{0,2},{2,0},{1,3},{3,1},{4,6},{6,4},{5,7},{7,5},{8,10},{10,8},{9,1... | collective-permute-start | bytes 430088 | tf_op jit(solution)/shard_map/ppermute | solution.py:337
  29.7 1.5 %collective-permute-start.12 = (bf16[96,512]{1,0:T(8,128)(2,1)S(1)}, bf16[96,512]{1,0:T(8,128)(2,1)S(1)}, u32[]{:S(2)}, u32[]{:S(2)}) collective-permute-start(bf16[96,512]{1,0:T(8,128)(2,1)S(1)} %get-tuple-element.78), channel_id=1, source_target_pairs={{0,1},{1,0},{2,3},{3,2},{4,5},{5,4},{6,7},{7,6},{8,9},{9,8},{10,11... | collective-permute-start | bytes 294920 | tf_op jit(solution)/shard_map/ppermute | solution.py:337
  29.8 1.4 %collective-permute-start.11 = (bf16[80,384]{1,0:T(8,128)(2,1)S(1)}, bf16[80,384]{1,0:T(8,128)(2,1)S(1)}, u32[]{:S(2)}, u32[]{:S(2)}) collective-permute-start(bf16[80,384]{1,0:T(8,128)(2,1)S(1)} %get-tuple-element.77), channel_id=1, source_target_pairs={{0,1},{1,0},{2,3},{3,2},{4,5},{5,4},{6,7},{7,6},{8,9},{9,8},{10,11... | collective-permute-start | bytes 184328 | tf_op jit(solution)/shard_map/ppermute | solution.py:337
  31.3 6.7 %collective-permute-start.13 = (bf16[96,896]{1,0:T(8,128)(2,1)S(1)}, bf16[96,896]{1,0:T(8,128)(2,1)S(1)}, u32[]{:S(2)}, u32[]{:S(2)}) collective-permute-start(bf16[96,896]{1,0:T(8,128)(2,1)S(1)} %get-tuple-element.81), channel_id=1, source_target_pairs={{0,2},{2,0},{1,3},{3,1},{4,6},{6,4},{5,7},{7,5},{8,10},{10,8},{9,1... | collective-permute-start | bytes 516104 | tf_op jit(solution)/shard_map/ppermute | solution.py:337
  33.1 2.5 %collective-permute-start.16 = (bf16[80,512]{1,0:T(8,128)(2,1)S(1)}, bf16[80,512]{1,0:T(8,128)(2,1)S(1)}, u32[]{:S(2)}, u32[]{:S(2)}) collective-permute-start(bf16[80,512]{1,0:T(8,128)(2,1)S(1)} %get-tuple-element.85), channel_id=1, source_target_pairs={{0,1},{1,0},{2,3},{3,2},{4,5},{5,4},{6,7},{7,6},{8,9},{9,8},{10,11... | collective-permute-start | bytes 245768 | tf_op jit(solution)/shard_map/ppermute | solution.py:337
  33.2 1.4 %collective-permute-start.19 = (bf16[80,384]{1,0:T(8,128)(2,1)S(1)}, bf16[80,384]{1,0:T(8,128)(2,1)S(1)}, u32[]{:S(2)}, u32[]{:S(2)}) collective-permute-start(bf16[80,384]{1,0:T(8,128)(2,1)S(1)} %shard_map.116.refs_3_.refs_2_), channel_id=1, source_target_pairs={{0,1},{1,0},{2,3},{3,2},{4,5},{5,4},{6,7},{7,6},{8,9},{9,8},{10,11... | collective-permute-start | bytes 184328 | tf_op jit(solution)/shard_map/ppermute | solution.py:337
  34.1 1.6 %collective-permute-start.15 = (bf16[80,384]{1,0:T(8,128)(2,1)S(1)}, bf16[80,384]{1,0:T(8,128)(2,1)S(1)}, u32[]{:S(2)}, u32[]{:S(2)}) collective-permute-start(bf16[80,384]{1,0:T(8,128)(2,1)S(1)} %get-tuple-element.84), channel_id=1, source_target_pairs={{0,1},{1,0},{2,3},{3,2},{4,5},{5,4},{6,7},{7,6},{8,9},{9,8},{10,11... | collective-permute-start | bytes 184328 | tf_op jit(solution)/shard_map/ppermute | solution.py:337
  35.8 5.9 %collective-permute-start.21 = (bf16[80,896]{1,0:T(8,128)(2,1)S(1)}, bf16[80,896]{1,0:T(8,128)(2,1)S(1)}, u32[]{:S(2)}, u32[]{:S(2)}) collective-permute-start(bf16[80,896]{1,0:T(8,128)(2,1)S(1)} %get-tuple-element.93), channel_id=1, source_target_pairs={{0,2},{2,0},{1,3},{3,1},{4,6},{6,4},{5,7},{7,5},{8,10},{10,8},{9,1... | collective-permute-start | bytes 430088 | tf_op jit(solution)/shard_map/ppermute | solution.py:337
  37.5 10.5 %collective-permute-start.22 = (bf16[80,1024]{1,0:T(8,128)(2,1)S(1)}, bf16[80,1024]{1,0:T(8,128)(2,1)S(1)}, u32[]{:S(2)}, u32[]{:S(2)}) collective-permute-start(bf16[80,1024]{1,0:T(8,128)(2,1)S(1)} %shard_map.123.refs_3_), channel_id=1, source_target_pairs={{0,8},{4,12},{8,0},{12,4},{1,9},{5,13},{9,1},{13,5},{2,10},{6,14},... | collective-permute-start | bytes 491528 | tf_op jit(solution)/shard_map/ppermute | solution.py:368
  41.9 6.4 %collective-permute-start.24 = (bf16[80,384]{1,0:T(8,128)(2,1)S(1)}, bf16[80,384]{1,0:T(8,128)(2,1)S(1)}, u32[]{:S(2)}, u32[]{:S(2)}) collective-permute-start(bf16[80,384]{1,0:T(8,128)(2,1)S(1)} %shard_map.128.refs_3_.refs_2_), channel_id=1, source_target_pairs={{0,1},{1,0},{2,3},{3,2},{4,5},{5,4},{6,7},{7,6},{8,9},{9,8},{10,11... | collective-permute-start | bytes 184328 | tf_op jit(solution)/shard_map/ppermute | solution.py:337
  42.0 9.2 %collective-permute-start.23 = (bf16[80,1024]{1,0:T(8,128)(2,1)S(1)}, bf16[80,1024]{1,0:T(8,128)(2,1)S(1)}, u32[]{:S(2)}, u32[]{:S(2)}) collective-permute-start(bf16[80,1024]{1,0:T(8,128)(2,1)S(1)} %shard_map.126.refs_4_), channel_id=1, source_target_pairs={{0,4},{4,0},{8,12},{12,8},{1,5},{5,1},{9,13},{13,9},{2,6},{6,2},{1... | collective-permute-start | bytes 491528 | tf_op jit(solution)/shard_map/ppermute | solution.py:368
  48.7 7.2 %collective-permute-start.25 = (bf16[80,1024]{1,0:T(8,128)(2,1)S(1)}, bf16[80,1024]{1,0:T(8,128)(2,1)S(1)}, u32[]{:S(2)}, u32[]{:S(2)}) collective-permute-start(bf16[80,1024]{1,0:T(8,128)(2,1)S(1)} %shard_map.131.refs_3_), channel_id=1, source_target_pairs={{0,12},{4,8},{8,4},{12,0},{1,13},{5,9},{9,5},{13,1},{2,14},{6,10},... | collective-permute-start | bytes 491528 | tf_op jit(solution)/shard_map/ppermute | solution.py:368
  (2 other events, 2.6 us)
